TPU v7x, 32 devices: a whole 2x2x4 slice. The times are simulated.
32 devices in a mesh: lev: 4 (over y, core), tile: 8 (over z, x).
Axes of the slice: x: 2, y: 2, z: 4, core: 2. Of those that a mesh axis runs over, the one named last changes fastest.
Arguments:
- levels: bfloat16 [16, 24, 96, 512], P('lev', None, 'tile'), may hold values from -6 to 6
- level_mask: int32 [16], P('lev'), may hold values from 0 to 1, as said below
- w_key: bfloat16 [512, 512], replicated, may hold values from -0.25 to 0.25
- w_value: bfloat16 [512, 512], replicated, may hold values from -0.25 to 0.25
- latent_query: bfloat16 [4, 512], replicated, may hold values from -52 to 52
- w_agg_out: bfloat16 [512, 512], replicated, may hold values from -0.25 to 0.25
- gain_attn: float32 [512], replicated, may hold values from 0.1 to 1.9
- w_qkv: bfloat16 [512, 1536], replicated, may hold values from -3 to 3
- w_proj: bfloat16 [512, 512], replicated, may hold values from -0.25 to 0.25
- gain_mlp: float32 [512], replicated, may hold values from 0.1 to 1.9
- w_up: bfloat16 [512, 2048], replicated, may hold values from -0.25 to 0.25
- w_down: bfloat16 [2048, 512], replicated, may hold values from -0.125 to 0.125
- cotangent: bfloat16 [4, 24, 96, 512], P(None, None, 'tile'), may hold values from -6 to 6
Outputs:
- encoded: bfloat16 [4, 24, 96, 512], P(None, None, 'tile')
- grad_up: float32 [512, 2048], P('lev', 'tile')
- grad_down_t: float32 [512, 2048], P('lev', 'tile')
Inputs may be any that keep to these rules, and one draw needn't show every extreme that they name: `level_mask`: exactly 13 of the entries are 1, the others 0.
All inputs are finite; a program needn't handle non-finite values.
Results may differ from a plain program's by a relative error of at most 0.03.
The roundings to bfloat16 on the way count: a program that leaves them out, or rounds other values in their place, can miss the bound.
Values may be sent and summed in bfloat16 or wider, within the bound.
No kernel may reach another device: no remote copies, remote signals or barrier semaphores. Data moves between devices by JAX's collectives and lax.ppermute only.
A program may use at most 128 MiB of HBM per device.

v0:
```python
import functools

import jax
import jax.numpy as jnp
from jax import lax
from jax.experimental import pallas as pl
from jax.experimental.pallas import tpu as pltpu
from jax.sharding import PartitionSpec as P

HEADS = 8
LATENT = 4
WL = 2
WA = 6
WO = 12
HALF = WO // 2
PIECE = WA * HALF
MARK = 2.0**40
F32 = jnp.float32
BF16 = jnp.bfloat16
MIB = 1 << 20


def dot(a, b, contract=((1,), (0,))):
    return lax.dot_general(a, b, (contract, ((), ())), preferred_element_type=F32)


def call(body, outs, scratch=(), smem_first=0, vmem=40, flops=0, moved=0, n_in=1, smem_last=0):
    ins = [pl.BlockSpec(memory_space=pltpu.SMEM)] * smem_first
    ins += [pl.BlockSpec(memory_space=pltpu.VMEM)] * (n_in - smem_first)
    return pl.pallas_call(
        body,
        out_shape=[jax.ShapeDtypeStruct(shape, dtype) for shape, dtype in outs],
        in_specs=ins,
        out_specs=[pl.BlockSpec(memory_space=pltpu.VMEM)] * len(outs),
        scratch_shapes=list(scratch),
        compiler_params=pltpu.CompilerParams(vmem_limit_bytes=vmem * MIB),
        cost_estimate=pl.CostEstimate(flops=flops, bytes_accessed=moved, transcendentals=0),
    )


def layer_norm(rows, gain):
    mean = jnp.mean(rows, -1, keepdims=True)
    centred = rows - mean
    spread = jnp.mean(centred * centred, -1, keepdims=True)
    return (centred * lax.rsqrt(spread + 1e-05) * gain).astype(BF16)


def gelu_parts(x):
    square = x * x
    t = jnp.tanh(x * (0.7978845608028654 + 0.7978845608028654 * 0.044715 * square))
    return square, t


def pack_levels_body(lev_count, mask_ref, lev_ref, *refs):
    outs, (east, west) = refs[: 2 * lev_count], refs[2 * lev_count :]
    count, lat = lev_ref.shape[0], lev_ref.shape[1]
    me = lax.axis_index("lev")
    for d in range(lev_count):
        other = me ^ d
        for j in range(count):
            live = mask_ref[j] > 0
            for a in range(WA):
                row = lax.rem(other * WA + WA // 2 + a, lat)
                cells = jnp.where(live, lev_ref[j, row].astype(F32), MARK)
                at = pl.ds(j * PIECE + a * HALF, HALF)
                east[at] = cells[HALF:]
                west[at] = cells[:HALF]
        outs[d][...] = east[...].astype(BF16)
        outs[lev_count + d][...] = west[...].astype(BF16)


def pack_cot_body(cot_ref, east_ref, west_ref, east, west):
    lat = cot_ref.shape[1]
    me = lax.axis_index("lev")
    for slot in range(2):
        other = me ^ (2 * slot)
        for l in range(LATENT):
            for a in range(WA):
                row = lax.rem(other * WA + WA // 2 + a, lat)
                cells = cot_ref[(l + WL // 2) % LATENT, row].astype(F32)
                at = pl.ds((slot * LATENT + l) * PIECE + a * HALF, HALF)
                east[at] = cells[HALF:]
                west[at] = cells[:HALF]
    east_ref[...] = east[...].astype(BF16)
    west_ref[...] = west[...].astype(BF16)


def aggregate(chunks, keep, query, w_key, w_value, w_agg_out, pool):
    width = w_key.shape[0]
    head_size = width // HEADS
    pairs = 2 * PIECE
    owner = lax.broadcasted_iota(jnp.int32, (HEADS, width), 1) // head_size
    table = (owner == lax.broadcasted_iota(jnp.int32, (HEADS, width), 0)).astype(F32)
    block_query = jnp.concatenate([table * query[l : l + 1].astype(F32) for l in range(LATENT)], 0)
    block_query = block_query.astype(BF16)
    lanes = LATENT * HEADS
    for h in range(2):
        rows = jnp.concatenate([ref[...] for ref in chunks[h]], 0)
        blocks = rows.shape[0] // pairs
        keys = dot(rows, w_key[...]).astype(BF16)
        values = dot(rows, w_value[...]).astype(BF16).astype(F32)
        scores = dot(keys, block_query, ((1,), (1,))) * head_size ** (-0.5)
        live = rows[:, :lanes].astype(F32) < MARK / 2
        scores = jnp.where(live, scores, -1e30)
        parts = [scores[b * pairs : (b + 1) * pairs] for b in range(blocks)]
        top = functools.reduce(jnp.maximum, parts)
        top = jnp.maximum(top, pltpu.roll(top, PIECE, 0))
        weights = [
            jnp.exp(part - top) * live[b * pairs : (b + 1) * pairs].astype(F32)
            for b, part in enumerate(parts)
        ]
        total = functools.reduce(jnp.add, weights)
        total = total + pltpu.roll(total, PIECE, 0)
        inverse = 1.0 / total
        weights = jnp.concatenate([w * inverse for w in weights], 0)
        high = weights.astype(BF16)
        low = (weights - high.astype(F32)).astype(BF16)
        step = 256
        per = step // head_size
        for l in range(LATENT):
            sums = []
            for n in range(width // step):
                at = l * HEADS + n * per
                head = lax.broadcasted_iota(jnp.int32, (lanes, step), 1) // head_size + at
                pick = (head == lax.broadcasted_iota(jnp.int32, (lanes, step), 0)).astype(BF16)
                spread = dot(high, pick) + dot(low, pick)
                prod = spread * values[:, n * step : (n + 1) * step]
                total_n = functools.reduce(
                    jnp.add, [prod[b * pairs : (b + 1) * pairs] for b in range(blocks)]
                )
                sums.append(total_n + pltpu.roll(total_n, PIECE, 0))
            slot = h * LATENT + (l - WL // 2) % LATENT
            pool[pl.ds(slot * PIECE, PIECE)] = jnp.concatenate(sums, 1)[:PIECE]
    pooled = pool[...].astype(BF16)
    return dot(pooled, w_agg_out[...]).astype(BF16)


def window_attention(lev_count, latent, gain, w_qkv):
    width = latent.shape[1]
    head_size = width // HEADS
    half = LATENT * PIECE
    slab = WL * PIECE
    size = 2 * slab
    normed = layer_norm(latent.astype(F32), gain[...])
    qkv = dot(normed, w_qkv[...])
    last = lax.axis_index("lev") == lev_count - 1
    shape = (2 * size, size)
    q_at = lax.rem(lax.broadcasted_iota(jnp.int32, shape, 0), slab)
    k_at = lax.rem(lax.broadcasted_iota(jnp.int32, shape, 1), slab)
    q_lat = lax.rem(q_at, PIECE) >= PIECE // 2
    k_lat = lax.rem(k_at, PIECE) >= PIECE // 2
    lat_differs = jnp.where(last, (q_lat != k_lat).astype(F32), 0.0)
    lev_differs = ((q_at >= PIECE) != (k_at >= PIECE)).astype(F32)
    lane = lax.broadcasted_iota(jnp.int32, (size, 2 * head_size), 1) < head_size
    mixed = []
    for lb in range(LATENT // WL):
        rows = jnp.concatenate(
            [qkv[lb * slab : (lb + 1) * slab], qkv[half + lb * slab : half + (lb + 1) * slab]], 0
        )
        differs = lat_differs + lev_differs if lb == LATENT // WL - 1 else lat_differs
        allowed = differs == 0.0
        outs = []
        for p in range(HEADS // 2):
            at = 2 * p * head_size
            query = rows[:, at : at + 2 * head_size]
            key = rows[:, width + at : width + at + 2 * head_size].astype(BF16)
            value = rows[:, 2 * width + at : 2 * width + at + 2 * head_size].astype(BF16)
            query = jnp.concatenate([jnp.where(lane, query, 0.0), jnp.where(lane, 0.0, query)], 0)
            scores = dot(query.astype(BF16), key, ((1,), (1,))) * head_size ** (-0.5)
            scores = jnp.where(allowed, scores, -1e30)
            weights = jnp.exp(scores - jnp.max(scores, -1, keepdims=True))
            probs = weights * (1.0 / jnp.sum(weights, -1, keepdims=True))
            out = dot(probs.astype(BF16), value)
            outs.append(jnp.where(lane, out[:size], out[size:]))
        mixed.append(jnp.concatenate(outs, 1))
    mixed = [m[:slab] for m in mixed] + [m[slab:] for m in mixed]
    return jnp.concatenate(mixed, 0).astype(BF16)


def window_body(lev_count, *refs):
    east, west = refs[:lev_count], refs[lev_count : 2 * lev_count]
    (w_key, w_value, query, w_agg_out, gain_attn, w_qkv, w_proj, gain_mlp) = refs[
        2 * lev_count : 2 * lev_count + 8
    ]
    resid_ref, normed2_ref, pool = refs[2 * lev_count + 8 :]
    latent = aggregate((east, west), None, query[...], w_key, w_value, w_agg_out, pool)
    mixed = window_attention(lev_count, latent, gain_attn, w_qkv)
    resid = (latent.astype(F32) + dot(mixed, w_proj[...])).astype(BF16)
    resid_ref[...] = resid
    normed2_ref[...] = layer_norm(resid.astype(F32), gain_mlp[...])


def mlp_body(resid, normed2, w_up, w_down, east_ref, west_ref):
    step = 512
    rows = normed2[...]
    total = resid[...].astype(F32)
    for n in range(w_up.shape[1] // step):
        inner = dot(rows, w_up[:, n * step : (n + 1) * step])
        _, t = gelu_parts(inner)
        active = (inner * (0.5 * (1.0 + t))).astype(BF16)
        total = total + dot(active, w_down[n * step : (n + 1) * step])
    total = total.astype(BF16)
    half = rows.shape[0] // 2
    east_ref[...] = total[:half]
    west_ref[...] = total[half:]


def grad_body(*refs):
    normed2 = refs[:4]
    own_e, own_w, peer_e, peer_w, w_up, w_down, send, keep, acc_up, acc_dn, n_half, c_half = refs[4:]
    me = lax.axis_index("lev")
    half_at = pl.multiple_of((me // 2) * 256, 256)
    piece = own_e.shape[0] // 2
    width = w_up.shape[0]
    cols = w_up.shape[1]
    step = 256
    model = acc_up.shape[0]
    rows, cots = [], []
    for k, (e, w, slot) in enumerate(
        ((own_e, own_w, 0), (own_e, own_w, 1), (peer_e, peer_w, 0), (peer_e, peer_w, 1))
    ):
        n = 2 * piece
        at = pl.ds(k * n, n)
        cot = jnp.concatenate(
            [e[slot * piece : (slot + 1) * piece], w[slot * piece : (slot + 1) * piece]], 0
        )
        rows.append(normed2[k][...])
        cots.append(cot)
        n_half[at] = normed2[k][:, pl.ds(half_at, model)]
        c_half[pl.ds(k * n, piece)] = e[slot * piece : (slot + 1) * piece, pl.ds(half_at, model)]
        c_half[pl.ds(k * n + piece, piece)] = w[
            slot * piece : (slot + 1) * piece, pl.ds(half_at, model)
        ]
    rows = jnp.concatenate(rows, 0)
    cots = jnp.concatenate(cots, 0)
    n_half_v = n_half[...]
    c_half_v = c_half[...]
    for n in range(cols // step):
        at = slice(n * step, (n + 1) * step)
        x = dot(rows, w_up[:, at])
        back = dot(cots, w_down[at], ((1,), (1,)))
        square, t = gelu_parts(x)
        cdf = 0.5 + 0.5 * t
        active = (x * cdf).astype(BF16)
        slope = (0.5 * 0.7978845608028654) + (1.5 * 0.7978845608028654 * 0.044715) * square
        dinner = (back * (cdf + x * ((1.0 - t * t) * slope))).astype(BF16)
        acc_up[:, at] = dot(n_half_v, dinner, ((0,), (0,)))
        acc_dn[:, at] = dot(c_half_v, active, ((0,), (0,)))
    quarter = model // 2
    core = lax.rem(me, 2)
    mine = pl.ds(pl.multiple_of(core * quarter, quarter), quarter)
    other = pl.ds(pl.multiple_of((1 - core) * quarter, quarter), quarter)
    keep[:quarter] = acc_up[mine]
    keep[quarter:] = acc_dn[mine]
    send[:quarter] = acc_up[other].astype(BF16)
    send[quarter:] = acc_dn[other].astype(BF16)


def split_body(groups, keep, recv, own_ref, *refs):
    outs, blocks = refs[:-1], refs[-1]
    cols = keep.shape[1] // groups
    for n in range(groups):
        at = slice(n * cols, (n + 1) * cols)
        blocks[n] = keep[:, at] + recv[:, at].astype(F32)
    me = lax.axis_index("tile") // 2
    own_ref[...] = blocks[me]
    for d in range(1, groups):
        outs[d - 1][...] = blocks[lax.rem(me + d, groups)].astype(BF16)


def total_body(own, *refs):
    received, (up_ref, dn_ref) = refs[:-2], refs[-2:]
    total = own[...]
    for part in received:
        total = total + part[...].astype(F32)
    half = total.shape[0] // 2
    up_ref[...] = total[:half]
    dn_ref[...] = total[half:]


def unpack_body(*refs):
    own, beside, core_own, core_beside, out_ref, scratch = refs
    lat = out_ref.shape[1]
    me = lax.axis_index("lev")
    half = LATENT * PIECE
    for part, d in ((own, 0), (beside, 2), (core_own, 1), (core_beside, 3)):
        scratch[...] = part[...].astype(F32)
        other = me ^ d
        for l in range(LATENT):
            for a in range(WA):
                row = lax.rem(other * WA + WA // 2 + a, lat)
                at = l * PIECE + a * HALF
                cells = jnp.concatenate(
                    [scratch[pl.ds(half + at, HALF)], scratch[pl.ds(at, HALF)]], 0
                )
                out_ref[(l + WL // 2) % LATENT, row] = cells.astype(BF16)


def exchanged(block, lev_step, tile_move):
    levs, tiles = lax.axis_size("lev"), lax.axis_size("tile")
    route = [
        (l * tiles + t, (l ^ lev_step) * tiles + tile_move(t)) for l in range(levs) for t in range(tiles)
    ]
    return lax.ppermute(block, ("lev", "tile"), route)


def per_device(
    levels,
    level_mask,
    w_key,
    w_value,
    latent_query,
    w_agg_out,
    gain_attn,
    w_qkv,
    w_proj,
    gain_mlp,
    w_up,
    w_down,
    cotangent,
):
    levs, tiles = lax.axis_size("lev"), lax.axis_size("tile")
    count, lat, lon, width = levels.shape
    hidden = w_up.shape[1]
    assert lat == levs * WA and lon == WO and levs == 4 and tiles % 2 == 0
    piece = count * PIECE
    rows = LATENT * PIECE
    window = 2 * rows
    groups = tiles // 2
    part = hidden // tiles
    quarter = width // levs

    west = lambda t: (t - 1) % tiles
    east = lambda t: (t + 1) % tiles
    same = lambda t: t
    peer = lambda t: t ^ 1
    next_pair = lambda t: (t - 2) % tiles if t % 2 == 0 else t

    packed = call(
        functools.partial(pack_levels_body, levs),
        [((piece, width), BF16)] * (2 * levs),
        [pltpu.VMEM((piece, width), F32)] * 2,
        smem_first=1,
        n_in=2,
        moved=3 * MIB,
    )(level_mask, levels)
    easts = [packed[0]] + [exchanged(packed[d], d, same) for d in range(1, levs)]
    wests = [exchanged(packed[levs + d], d, west) for d in range(levs)]

    cot_east, cot_west = call(
        pack_cot_body,
        [((window, width), BF16)] * 2,
        [pltpu.VMEM((window, width), F32)] * 2,
        n_in=1,
        moved=2 * MIB,
    )(cotangent)
    cot_own_w = exchanged(cot_west, 0, west)
    cot_peer_e = exchanged(cot_east, 0, peer)
    cot_peer_w = exchanged(cot_west, 0, next_pair)

    resid, normed2 = call(
        functools.partial(window_body, levs),
        [((window, width), BF16)] * 2,
        [pltpu.VMEM((window, width), F32)],
        n_in=2 * levs + 8,
        flops=4 * 10**9,
        moved=8 * MIB,
        vmem=50,
    )(
        *easts,
        *wests,
        w_key,
        w_value,
        latent_query,
        w_agg_out,
        gain_attn[None],
        w_qkv,
        w_proj,
        gain_mlp[None],
    )
    normed2_peer = exchanged(normed2, 0, peer)
    normed2_beside = exchanged(normed2, 2, same)
    normed2_far = exchanged(normed2, 2, peer)

    out_e, out_w = call(
        mlp_body,
        [((rows, width), BF16)] * 2,
        n_in=4,
        flops=2 * 10**9,
        moved=6 * MIB,
    )(resid, normed2, w_up, w_down)
    own_rows = jnp.concatenate([out_e, exchanged(out_w, 0, east)], 0)
    beside_rows = exchanged(own_rows, 2, same)
    core_own = exchanged(own_rows, 1, same)
    core_beside = exchanged(beside_rows, 1, same)

    parity = lax.rem(lax.axis_index("tile"), 2)
    up_part = lax.dynamic_index_in_dim(
        w_up.reshape(width, groups, 2, part), parity, 2, keepdims=False
    ).reshape(width, groups * part)
    down_part = lax.dynamic_index_in_dim(
        w_down.reshape(groups, 2, part, width), parity, 1, keepdims=False
    ).reshape(groups * part, width)
    send, keep = call(
        grad_body,
        [((2 * quarter, hidden // 2), BF16), ((2 * quarter, hidden // 2), F32)],
        [pltpu.VMEM((2 * quarter, hidden // 2), F32)] * 2
        + [pltpu.VMEM((4 * window, 2 * quarter), BF16)] * 2,
        n_in=10,
        flops=5 * 10**9,
        moved=8 * MIB,
        vmem=50,
    )(
        normed2,
        normed2_beside,
        normed2_peer,
        normed2_far,
        cot_east,
        cot_own_w,
        cot_peer_e,
        cot_peer_w,
        up_part,
        down_part,
    )
    recv = exchanged(send, 1, same)
    own, *sends = call(
        functools.partial(split_body, groups),
        [((2 * quarter, part), F32)] + [((2 * quarter, part), BF16)] * (groups - 1),
        [pltpu.VMEM((groups, 2 * quarter, part), F32)],
        n_in=2,
        moved=2 * MIB,
    )(keep, recv)
    received = [
        exchanged(block, 0, lambda t, d=d: (t + 2 * d) % tiles) for d, block in enumerate(sends, 1)
    ]
    grad_up, grad_down_t = call(
        total_body,
        [((quarter, part), F32)] * 2,
        n_in=groups,
        moved=1 * MIB,
    )(own, *received)
    encoded = call(
        unpack_body,
        [((LATENT, lat, lon, width), BF16)],
        [pltpu.VMEM((window, width), F32)],
        n_in=4,
        moved=3 * MIB,
    )(own_rows, beside_rows, core_own, core_beside)[0]
    return (encoded, grad_up, grad_down_t)


def solution(mesh):
    return jax.shard_map(
        per_device,
        mesh=mesh,
        in_specs=(
            P("lev", None, "tile", None),
            P("lev"),
            P(),
            P(),
            P(),
            P(),
            P(),
            P(),
            P(),
            P(),
            P(),
            P(),
            P(None, None, "tile", None),
        ),
        out_specs=(P(None, None, "tile", None), P("lev", "tile"), P("lev", "tile")),
        check_vma=False,
    )
```

profile of v0, /device:TPU:0, one launch (start us, length us, event | category | flops | bytes accessed | tf_op | source)
XLA Modules:
  0.0 93.7 jit_solution(9748895069504581235)
XLA Ops:
  0.7 1.9 %copy.16.lev_ref = bf16[4,24,12,512]{3,2,1,0:T(8,128)(2,1)S(1)} copy(bf16[4,24,12,512]{3,1,2,0:T(8,128)(2,1)} %param.13) | data formatting | bytes 2359296 | tf_op args[0]
  2.5 1.8 %shard_map.148 = (bf16[144,512]{1,0:T(8,128)(2,1)S(1)}, bf16[144,512]{1,0:T(8,128)(2,1)}, bf16[144,512]{1,0:T(8,128)(2,1)}, bf16[144,512]{1,0:T(8,128)(2,1)}, bf...) custom-call(s32[4]{0:T(128)S(1)} %copy-done.2, ...), custom_call_target="tpu_custom_call" | custom-call | bytes 3145728 | tf_op jit(solution)/shard_map/pallas_call | solution.py:339
  4.8 2.5 %collective-permute-start.1 = (bf16[144,512]{1,0:T(8,128)(2,1)}, bf16[144,512]{1,0:T(8,128)(2,1)S(1)}, u32[]{:S(2)}, u32[]{:S(2)}) collective-permute-start(bf16[144,512]{1,0:T(8,128)(2,1)} %get-tuple-element.27), channel_id=1, source_target_pairs={{0,16},{1,17},{2,18},{3,19},{4,20},{5,21},{6,22},{7,23},{8,24},{9,... | collective-permute-start | bytes 442376 | tf_op jit(solution)/shard_map/ppermute | solution.py:304
  7.5 4.7 %collective-permute-start.3 = (bf16[144,512]{1,0:T(8,128)(2,1)}, bf16[144,512]{1,0:T(8,128)(2,1)S(1)}, u32[]{:S(2)}, u32[]{:S(2)}) collective-permute-start(bf16[144,512]{1,0:T(8,128)(2,1)} %get-tuple-element.29), channel_id=1, source_target_pairs={{0,7},{1,0},{2,1},{3,2},{4,3},{5,4},{6,5},{7,6},{8,15},{9,8},{10,9... | collective-permute-start | bytes 442376 | tf_op jit(solution)/shard_map/ppermute | solution.py:304
  12.3 2.8 %reshape.20 = bf16[512,4,2,256]{3,2,1,0:T(2,128)(2,1)} reshape(bf16[512,2048]{1,0:T(8,128)(2,1)S(1)} %copy-done) | data formatting | bytes 4194304 | tf_op jit(solution)/shard_map/reshape | solution.py:399
  15.1 2.3 %collective-permute-start.5 = (bf16[144,512]{1,0:T(8,128)(2,1)S(1)}, bf16[144,512]{1,0:T(8,128)(2,1)S(1)}, u32[]{:S(2)}, u32[]{:S(2)}) collective-permute-start(bf16[144,512]{1,0:T(8,128)(2,1)S(1)} %get-tuple-element.31), channel_id=1, source_target_pairs={{0,23},{1,16},{2,17},{3,18},{4,19},{5,20},{6,21},{7,22},{8,31},{9,... | collective-permute-start | bytes 442376 | tf_op jit(solution)/shard_map/ppermute | solution.py:304
  17.7 8.2 %dynamic-slice_reduce_fusion = bf16[512,4,256]{2,1,0:T(4,128)(2,1)S(1)} fusion(bf16[512,4,2,256]{3,2,1,0:T(2,128)(2,1)} %reshape.20, s32[]{:T(128)S(6)} %select_n.6), kind=kLoop, calls=%fused_computation | loop fusion | bytes 2097156 | tf_op jit(solution)/shard_map/jit(dynamic_index_in_dim)/dynamic_slice | solution.py:398
  30.1 1.4 %collective-permute-start.14 = (bf16[288,512]{1,0:T(8,128)(2,1)S(1)}, bf16[288,512]{1,0:T(8,128)(2,1)S(1)}, u32[]{:S(2)}, u32[]{:S(2)}) collective-permute-start(bf16[288,512]{1,0:T(8,128)(2,1)S(1)} %get-tuple-element.38), channel_id=1, source_target_pairs={{0,7},{1,0},{2,1},{3,2},{4,3},{5,4},{6,5},{7,6},{8,15},{9,8},{10,9... | collective-permute-start | bytes 884744 | tf_op jit(solution)/shard_map/ppermute | solution.py:304
  31.4 2.5 %collective-permute-start.16 = (bf16[288,512]{1,0:T(8,128)(2,1)S(1)}, bf16[288,512]{1,0:T(8,128)(2,1)S(1)}, u32[]{:S(2)}, u32[]{:S(2)}) collective-permute-start(bf16[288,512]{1,0:T(8,128)(2,1)S(1)} %get-tuple-element.38), channel_id=1, source_target_pairs={{0,6},{1,1},{2,0},{3,3},{4,2},{5,5},{6,4},{7,7},{8,14},{9,9},{10,8... | collective-permute-start | bytes 884744 | tf_op jit(solution)/shard_map/ppermute | solution.py:304
  34.2 9.0 %shard_map.149 = (bf16[288,512]{1,0:T(8,128)(2,1)S(1)}, bf16[288,512]{1,0:T(8,128)(2,1)S(1)}) custom-call(bf16[144,512]{1,0:T(8,128)(2,1)S(1)} %get-tuple-element.25.refs_0_, bf16[144,512]{1,0:T(8,128)(2,1)S(1)} %collective-permute-done.refs_1_, bf16[144,512]{1,0:T(8,128)(2,1)S(1)} %collective-permute-done.1.refs_2_, ...), custom_call_target="tpu_custom_call" | custom-call | flops 4000000000 | bytes 8388608 | tf_op jit(solution)/shard_map/pallas_call | solution.py:361
  43.1 1.6 %collective-permute-start.11 = (bf16[288,512]{1,0:T(8,128)(2,1)S(1)}, bf16[288,512]{1,0:T(8,128)(2,1)S(1)}, u32[]{:S(2)}, u32[]{:S(2)}) collective-permute-start(bf16[288,512]{1,0:T(8,128)(2,1)S(1)} %get-tuple-element.34.normed2.refs_0_), channel_id=1, source_target_pairs={{0,16},{1,17},{2,18},{3,19},{4,20},{5,21},{6,22},{7,23},{8,24},{9,... | collective-permute-start | bytes 884744 | tf_op jit(solution)/shard_map/ppermute | solution.py:304
  44.7 2.0 %collective-permute-start.12 = (bf16[288,512]{1,0:T(8,128)(2,1)S(1)}, bf16[288,512]{1,0:T(8,128)(2,1)S(1)}, u32[]{:S(2)}, u32[]{:S(2)}) collective-permute-start(bf16[288,512]{1,0:T(8,128)(2,1)S(1)} %get-tuple-element.34.normed2.refs_0_), channel_id=1, source_target_pairs={{0,1},{1,0},{2,3},{3,2},{4,5},{5,4},{6,7},{7,6},{8,9},{9,8},{10,11... | collective-permute-start | bytes 884744 | tf_op jit(solution)/shard_map/ppermute | solution.py:304
  46.7 1.9 %shard_map.150 = (bf16[144,512]{1,0:T(8,128)(2,1)S(1)}, bf16[144,512]{1,0:T(8,128)(2,1)S(1)}) custom-call(bf16[288,512]{1,0:T(8,128)(2,1)S(1)} %get-tuple-element.33.resid, bf16[288,512]{1,0:T(8,128)(2,1)S(1)} %get-tuple-element.34.normed2.refs_0_, bf16[512,2048]{1,0:T(8,128)(2,1)S(1)} %copy-done, bf16[2048,512]{1,0:T(8,128)(2,1)S(1)} %copy-done.1), custom_call_target="tpu_custom_call" | custom-call | flops 2000000000 | bytes 6291456 | tf_op jit(solution)/shard_map/pallas_call | solution.py:385
  48.7 2.2 %collective-permute-start.7 = (bf16[144,512]{1,0:T(8,128)(2,1)S(1)}, bf16[144,512]{1,0:T(8,128)(2,1)S(1)}, u32[]{:S(2)}, u32[]{:S(2)}) collective-permute-start(bf16[144,512]{1,0:T(8,128)(2,1)S(1)} %get-tuple-element.36), channel_id=1, source_target_pairs={{0,1},{1,2},{2,3},{3,4},{4,5},{5,6},{6,7},{7,0},{8,9},{9,10},{10,1... | collective-permute-start | bytes 442376 | tf_op jit(solution)/shard_map/ppermute | solution.py:304
  52.2 5.6 %collective-permute-done.12.refs_2_ = bf16[288,512]{1,0:T(8,128)(2,1)S(1)} collective-permute-done((bf16[288,512]{1,0:T(8,128)(2,1)S(1)}, bf16[288,512]{1,0:T(8,128)(2,1)S(1)}, u32[]{:S(2)}, u32[]{:S(2)}) %collective-permute-start.12) | collective-permute-done | bytes 294944 | tf_op jit(solution)/shard_map/ppermute | solution.py:304
  57.8 4.7 %collective-permute-done.13.refs_3_ = bf16[288,512]{1,0:T(8,128)(2,1)S(1)} collective-permute-done((bf16[288,512]{1,0:T(8,128)(2,1)S(1)}, bf16[288,512]{1,0:T(8,128)(2,1)S(1)}, u32[]{:S(2)}, u32[]{:S(2)}) %collective-permute-start.13) | collective-permute-done | bytes 294944 | tf_op jit(solution)/shard_map/ppermute | solution.py:304
  62.5 7.2 %shard_map.153 = (bf16[256,1024]{1,0:T(8,128)(2,1)S(1)}, f32[256,1024]{1,0:T(8,128)S(1)}) custom-call(bf16[288,512]{1,0:T(8,128)(2,1)S(1)} %get-tuple-element.34.normed2.refs_0_, bf16[288,512]{1,0:T(8,128)(2,1)S(1)} %collective-permute-done.11.refs_1_, bf16[288,512]{1,0:T(8,128)(2,1)S(1)} %collective-permute-done.12.refs_2_, ...), custom_call_target="tpu_custom_call" | custom-call | flops 5000000000 | bytes 8388608 | tf_op jit(solution)/shard_map/pallas_call | solution.py:404
  69.8 1.6 %collective-permute-start.8 = (bf16[288,512]{1,0:T(8,128)(2,1)S(1)}, bf16[288,512]{1,0:T(8,128)(2,1)S(1)}, u32[]{:S(2)}, u32[]{:S(2)}) collective-permute-start(bf16[288,512]{1,0:T(8,128)(2,1)S(1)} %constant_dynamic-update-slice_fusion.refs_0_), channel_id=1, source_target_pairs={{0,16},{1,17},{2,18},{3,19},{4,20},{5,21},{6,22},{7,23},{8,24},{9,... | collective-permute-start | bytes 884744 | tf_op jit(solution)/shard_map/ppermute | solution.py:304
  71.7 7.6 %collective-permute-done.8.refs_1_ = bf16[288,512]{1,0:T(8,128)(2,1)S(1)} collective-permute-done((bf16[288,512]{1,0:T(8,128)(2,1)S(1)}, bf16[288,512]{1,0:T(8,128)(2,1)S(1)}, u32[]{:S(2)}, u32[]{:S(2)}) %collective-permute-start.8) | collective-permute-done | bytes 294944 | tf_op jit(solution)/shard_map/ppermute | solution.py:304
  79.5 1.6 %collective-permute-start.18 = (bf16[256,256]{1,0:T(8,128)(2,1)S(1)}, bf16[256,256]{1,0:T(8,128)(2,1)S(1)}, u32[]{:S(2)}, u32[]{:S(2)}) collective-permute-start(bf16[256,256]{1,0:T(8,128)(2,1)S(1)} %get-tuple-element.42), channel_id=1, source_target_pairs={{0,2},{1,3},{2,4},{3,5},{4,6},{5,7},{6,0},{7,1},{8,10},{9,11},{10,... | collective-permute-start | bytes 393224 | tf_op jit(solution)/shard_map/ppermute | solution.py:304
  81.1 2.6 %collective-permute-start.19 = (bf16[256,256]{1,0:T(8,128)(2,1)S(1)}, bf16[256,256]{1,0:T(8,128)(2,1)S(1)}, u32[]{:S(2)}, u32[]{:S(2)}) collective-permute-start(bf16[256,256]{1,0:T(8,128)(2,1)S(1)} %get-tuple-element.43), channel_id=1, source_target_pairs={{0,4},{1,5},{2,6},{3,7},{4,0},{5,1},{6,2},{7,3},{8,12},{9,13},{10,... | collective-permute-start | bytes 393224 | tf_op jit(solution)/shard_map/ppermute | solution.py:304
  83.7 1.3 %collective-permute-start.20 = (bf16[256,256]{1,0:T(8,128)(2,1)S(1)}, bf16[256,256]{1,0:T(8,128)(2,1)S(1)}, u32[]{:S(2)}, u32[]{:S(2)}) collective-permute-start(bf16[256,256]{1,0:T(8,128)(2,1)S(1)} %get-tuple-element.44), channel_id=1, source_target_pairs={{0,6},{1,7},{2,0},{3,1},{4,2},{5,3},{6,4},{7,5},{8,14},{9,15},{10,... | collective-permute-start | bytes 393224 | tf_op jit(solution)/shard_map/ppermute | solution.py:304
  85.5 1.7 %copy.20 = bf16[4,24,12,512]{3,1,2,0:T(8,128)(2,1)} copy(bf16[4,24,12,512]{3,2,1,0:T(8,128)(2,1)S(1)} %shard_map.151) | data formatting | bytes 2359296
  87.7 5.3 %collective-permute-done.19.refs_1_ = bf16[256,256]{1,0:T(8,128)(2,1)S(1)} collective-permute-done((bf16[256,256]{1,0:T(8,128)(2,1)S(1)}, bf16[256,256]{1,0:T(8,128)(2,1)S(1)}, u32[]{:S(2)}, u32[]{:S(2)}) %collective-permute-start.19) | collective-permute-done | bytes 131104 | tf_op jit(solution)/shard_map/ppermute | solution.py:304
  (57 shorter events, 8.8 us)
Async XLA Ops:
  0.6 11.7 %copy-start = (bf16[512,2048]{1,0:T(8,128)(2,1)S(1)}, bf16[512,2048]{1,0:T(8,128)(2,1)}, u32[]{:S(2)}) copy-start(bf16[512,2048]{1,0:T(8,128)(2,1)} %w_up.1) | copy-start | bytes 6291460
  4.3 10.7 %collective-permute-start = (bf16[144,512]{1,0:T(8,128)(2,1)}, bf16[144,512]{1,0:T(8,128)(2,1)S(1)}, u32[]{:S(2)}, u32[]{:S(2)}) collective-permute-start(bf16[144,512]{1,0:T(8,128)(2,1)} %get-tuple-element.26), channel_id=1, source_target_pairs={{0,8},{1,9},{2,10},{3,11},{4,12},{5,13},{6,14},{7,15},{8,0},{9,1},... | collective-permute-start | bytes 442376 | tf_op jit(solution)/shard_map/ppermute | solution.py:304
  4.8 12.6 %collective-permute-start.1 = (bf16[144,512]{1,0:T(8,128)(2,1)}, bf16[144,512]{1,0:T(8,128)(2,1)S(1)}, u32[]{:S(2)}, u32[]{:S(2)}) collective-permute-start(bf16[144,512]{1,0:T(8,128)(2,1)} %get-tuple-element.27), channel_id=1, source_target_pairs={{0,16},{1,17},{2,18},{3,19},{4,20},{5,21},{6,22},{7,23},{8,24},{9,... | collective-permute-start | bytes 442376 | tf_op jit(solution)/shard_map/ppermute | solution.py:304
  7.3 22.8 %collective-permute-start.2 = (bf16[144,512]{1,0:T(8,128)(2,1)}, bf16[144,512]{1,0:T(8,128)(2,1)S(1)}, u32[]{:S(2)}, u32[]{:S(2)}) collective-permute-start(bf16[144,512]{1,0:T(8,128)(2,1)} %get-tuple-element.28), channel_id=1, source_target_pairs={{0,24},{1,25},{2,26},{3,27},{4,28},{5,29},{6,30},{7,31},{8,16},{9,... | collective-permute-start | bytes 442376 | tf_op jit(solution)/shard_map/ppermute | solution.py:304
  7.5 24.0 %collective-permute-start.3 = (bf16[144,512]{1,0:T(8,128)(2,1)}, bf16[144,512]{1,0:T(8,128)(2,1)S(1)}, u32[]{:S(2)}, u32[]{:S(2)}) collective-permute-start(bf16[144,512]{1,0:T(8,128)(2,1)} %get-tuple-element.29), channel_id=1, source_target_pairs={{0,7},{1,0},{2,1},{3,2},{4,3},{5,4},{6,5},{7,6},{8,15},{9,8},{10,9... | collective-permute-start | bytes 442376 | tf_op jit(solution)/shard_map/ppermute | solution.py:304
  12.2 21.8 %collective-permute-start.4 = (bf16[144,512]{1,0:T(8,128)(2,1)S(1)}, bf16[144,512]{1,0:T(8,128)(2,1)S(1)}, u32[]{:S(2)}, u32[]{:S(2)}) collective-permute-start(bf16[144,512]{1,0:T(8,128)(2,1)S(1)} %get-tuple-element.30), channel_id=1, source_target_pairs={{0,15},{1,8},{2,9},{3,10},{4,11},{5,12},{6,13},{7,14},{8,7},{9,0},... | collective-permute-start | bytes 442376 | tf_op jit(solution)/shard_map/ppermute | solution.py:304
  15.1 19.0 %collective-permute-start.5 = (bf16[144,512]{1,0:T(8,128)(2,1)S(1)}, bf16[144,512]{1,0:T(8,128)(2,1)S(1)}, u32[]{:S(2)}, u32[]{:S(2)}) collective-permute-start(bf16[144,512]{1,0:T(8,128)(2,1)S(1)} %get-tuple-element.31), channel_id=1, source_target_pairs={{0,23},{1,16},{2,17},{3,18},{4,19},{5,20},{6,21},{7,22},{8,31},{9,... | collective-permute-start | bytes 442376 | tf_op jit(solution)/shard_map/ppermute | solution.py:304
  17.4 16.7 %collective-permute-start.6 = (bf16[144,512]{1,0:T(8,128)(2,1)S(1)}, bf16[144,512]{1,0:T(8,128)(2,1)S(1)}, u32[]{:S(2)}, u32[]{:S(2)}) collective-permute-start(bf16[144,512]{1,0:T(8,128)(2,1)S(1)} %get-tuple-element.32), channel_id=1, source_target_pairs={{0,31},{1,24},{2,25},{3,26},{4,27},{5,28},{6,29},{7,30},{8,23},{9,... | collective-permute-start | bytes 442376 | tf_op jit(solution)/shard_map/ppermute | solution.py:304
  27.9 6.2 %copy-start.3 = (bf16[512,512]{1,0:T(8,128)(2,1)S(1)}, bf16[512,512]{1,0:T(8,128)(2,1)}, u32[]{:S(2)}) copy-start(bf16[512,512]{1,0:T(8,128)(2,1)} %refs_8_.1) | copy-start | bytes 1572868
  27.9 6.2 %copy-start.4 = (bf16[512,512]{1,0:T(8,128)(2,1)S(1)}, bf16[512,512]{1,0:T(8,128)(2,1)}, u32[]{:S(2)}) copy-start(bf16[512,512]{1,0:T(8,128)(2,1)} %refs_9_.1) | copy-start | bytes 1572868
  30.1 16.6 %collective-permute-start.14 = (bf16[288,512]{1,0:T(8,128)(2,1)S(1)}, bf16[288,512]{1,0:T(8,128)(2,1)S(1)}, u32[]{:S(2)}, u32[]{:S(2)}) collective-permute-start(bf16[288,512]{1,0:T(8,128)(2,1)S(1)} %get-tuple-element.38), channel_id=1, source_target_pairs={{0,7},{1,0},{2,1},{3,2},{4,3},{5,4},{6,5},{7,6},{8,15},{9,8},{10,9... | collective-permute-start | bytes 884744 | tf_op jit(solution)/shard_map/ppermute | solution.py:304
  31.4 19.5 %collective-permute-start.16 = (bf16[288,512]{1,0:T(8,128)(2,1)S(1)}, bf16[288,512]{1,0:T(8,128)(2,1)S(1)}, u32[]{:S(2)}, u32[]{:S(2)}) collective-permute-start(bf16[288,512]{1,0:T(8,128)(2,1)S(1)} %get-tuple-element.38), channel_id=1, source_target_pairs={{0,6},{1,1},{2,0},{3,3},{4,2},{5,5},{6,4},{7,7},{8,14},{9,9},{10,8... | collective-permute-start | bytes 884744 | tf_op jit(solution)/shard_map/ppermute | solution.py:304
  34.0 14.7 %collective-permute-start.15 = (bf16[288,512]{1,0:T(8,128)(2,1)S(1)}, bf16[288,512]{1,0:T(8,128)(2,1)S(1)}, u32[]{:S(2)}, u32[]{:S(2)}) collective-permute-start(bf16[288,512]{1,0:T(8,128)(2,1)S(1)} %get-tuple-element.37.refs_4_), channel_id=1, source_target_pairs={{0,1},{1,0},{2,3},{3,2},{4,5},{5,4},{6,7},{7,6},{8,9},{9,8},{10,11... | collective-permute-start | bytes 884744 | tf_op jit(solution)/shard_map/ppermute | solution.py:304
  43.1 9.1 %collective-permute-start.11 = (bf16[288,512]{1,0:T(8,128)(2,1)S(1)}, bf16[288,512]{1,0:T(8,128)(2,1)S(1)}, u32[]{:S(2)}, u32[]{:S(2)}) collective-permute-start(bf16[288,512]{1,0:T(8,128)(2,1)S(1)} %get-tuple-element.34.normed2.refs_0_), channel_id=1, source_target_pairs={{0,16},{1,17},{2,18},{3,19},{4,20},{5,21},{6,22},{7,23},{8,24},{9,... | collective-permute-start | bytes 884744 | tf_op jit(solution)/shard_map/ppermute | solution.py:304
  44.7 13.1 %collective-permute-start.12 = (bf16[288,512]{1,0:T(8,128)(2,1)S(1)}, bf16[288,512]{1,0:T(8,128)(2,1)S(1)}, u32[]{:S(2)}, u32[]{:S(2)}) collective-permute-start(bf16[288,512]{1,0:T(8,128)(2,1)S(1)} %get-tuple-element.34.normed2.refs_0_), channel_id=1, source_target_pairs={{0,1},{1,0},{2,3},{3,2},{4,5},{5,4},{6,7},{7,6},{8,9},{9,8},{10,11... | collective-permute-start | bytes 884744 | tf_op jit(solution)/shard_map/ppermute | solution.py:304
  46.7 15.8 %collective-permute-start.13 = (bf16[288,512]{1,0:T(8,128)(2,1)S(1)}, bf16[288,512]{1,0:T(8,128)(2,1)S(1)}, u32[]{:S(2)}, u32[]{:S(2)}) collective-permute-start(bf16[288,512]{1,0:T(8,128)(2,1)S(1)} %get-tuple-element.34.normed2.refs_0_), channel_id=1, source_target_pairs={{0,17},{1,16},{2,19},{3,18},{4,21},{5,20},{6,23},{7,22},{8,25},{9,... | collective-permute-start | bytes 884744 | tf_op jit(solution)/shard_map/ppermute | solution.py:304
  48.7 21.1 %collective-permute-start.7 = (bf16[144,512]{1,0:T(8,128)(2,1)S(1)}, bf16[144,512]{1,0:T(8,128)(2,1)S(1)}, u32[]{:S(2)}, u32[]{:S(2)}) collective-permute-start(bf16[144,512]{1,0:T(8,128)(2,1)S(1)} %get-tuple-element.36), channel_id=1, source_target_pairs={{0,1},{1,2},{2,3},{3,4},{4,5},{5,6},{6,7},{7,0},{8,9},{9,10},{10,1... | collective-permute-start | bytes 442376 | tf_op jit(solution)/shard_map/ppermute | solution.py:304
  69.7 9.6 %collective-permute-start.17 = (bf16[256,1024]{1,0:T(8,128)(2,1)S(1)}, bf16[256,1024]{1,0:T(8,128)(2,1)S(1)}, u32[]{:S(2)}, u32[]{:S(2)}) collective-permute-start(bf16[256,1024]{1,0:T(8,128)(2,1)S(1)} %get-tuple-element.40), channel_id=1, source_target_pairs={{0,8},{1,9},{2,10},{3,11},{4,12},{5,13},{6,14},{7,15},{8,0},{9,1},... | collective-permute-start | bytes 1572872 | tf_op jit(solution)/shard_map/ppermute | solution.py:304
  69.8 9.5 %collective-permute-start.8 = (bf16[288,512]{1,0:T(8,128)(2,1)S(1)}, bf16[288,512]{1,0:T(8,128)(2,1)S(1)}, u32[]{:S(2)}, u32[]{:S(2)}) collective-permute-start(bf16[288,512]{1,0:T(8,128)(2,1)S(1)} %constant_dynamic-update-slice_fusion.refs_0_), channel_id=1, source_target_pairs={{0,16},{1,17},{2,18},{3,19},{4,20},{5,21},{6,22},{7,23},{8,24},{9,... | collective-permute-start | bytes 884744 | tf_op jit(solution)/shard_map/ppermute | solution.py:304
  71.5 13.6 %collective-permute-start.9 = (bf16[288,512]{1,0:T(8,128)(2,1)S(1)}, bf16[288,512]{1,0:T(8,128)(2,1)S(1)}, u32[]{:S(2)}, u32[]{:S(2)}) collective-permute-start(bf16[288,512]{1,0:T(8,128)(2,1)S(1)} %constant_dynamic-update-slice_fusion.refs_0_), channel_id=1, source_target_pairs={{0,8},{1,9},{2,10},{3,11},{4,12},{5,13},{6,14},{7,15},{8,0},{9,1},... | collective-permute-start | bytes 884744 | tf_op jit(solution)/shard_map/ppermute | solution.py:304
  79.3 5.8 %collective-permute-start.10 = (bf16[288,512]{1,0:T(8,128)(2,1)S(1)}, bf16[288,512]{1,0:T(8,128)(2,1)S(1)}, u32[]{:S(2)}, u32[]{:S(2)}) collective-permute-start(bf16[288,512]{1,0:T(8,128)(2,1)S(1)} %collective-permute-done.8.refs_1_), channel_id=1, source_target_pairs={{0,8},{1,9},{2,10},{3,11},{4,12},{5,13},{6,14},{7,15},{8,0},{9,1},... | collective-permute-start | bytes 884744 | tf_op jit(solution)/shard_map/ppermute | solution.py:304
  79.5 8.2 %collective-permute-start.18 = (bf16[256,256]{1,0:T(8,128)(2,1)S(1)}, bf16[256,256]{1,0:T(8,128)(2,1)S(1)}, u32[]{:S(2)}, u32[]{:S(2)}) collective-permute-start(bf16[256,256]{1,0:T(8,128)(2,1)S(1)} %get-tuple-element.42), channel_id=1, source_target_pairs={{0,2},{1,3},{2,4},{3,5},{4,6},{5,7},{6,0},{7,1},{8,10},{9,11},{10,... | collective-permute-start | bytes 393224 | tf_op jit(solution)/shard_map/ppermute | solution.py:304
  81.1 11.9 %collective-permute-start.19 = (bf16[256,256]{1,0:T(8,128)(2,1)S(1)}, bf16[256,256]{1,0:T(8,128)(2,1)S(1)}, u32[]{:S(2)}, u32[]{:S(2)}) collective-permute-start(bf16[256,256]{1,0:T(8,128)(2,1)S(1)} %get-tuple-element.43), channel_id=1, source_target_pairs={{0,4},{1,5},{2,6},{3,7},{4,0},{5,1},{6,2},{7,3},{8,12},{9,13},{10,... | collective-permute-start | bytes 393224 | tf_op jit(solution)/shard_map/ppermute | solution.py:304
  83.7 9.3 %collective-permute-start.20 = (bf16[256,256]{1,0:T(8,128)(2,1)S(1)}, bf16[256,256]{1,0:T(8,128)(2,1)S(1)}, u32[]{:S(2)}, u32[]{:S(2)}) collective-permute-start(bf16[256,256]{1,0:T(8,128)(2,1)S(1)} %get-tuple-element.44), channel_id=1, source_target_pairs={{0,6},{1,7},{2,0},{3,1},{4,2},{5,3},{6,4},{7,5},{8,14},{9,15},{10,... | collective-permute-start | bytes 393224 | tf_op jit(solution)/shard_map/ppermute | solution.py:304
  (8 other events, 36.1 us)
where the time goes:
time: 94.6 us; the launch traced here: 93.7 us
  starting transfers between devices  27.9 us (29%)
  waiting for transfers between devices  25 us (26%)
  Pallas kernels  21.5 us (23%)
  local copies, waits for them, and re-layouts  18.3 us (19%)
    ppermute x21, starting transfers between devices, exchanged(): return lax.ppermute(block, ('lev', 'tile'), route)  27.9 us
    ppermute x21, waiting for transfers between devices, exchanged(): return lax.ppermute(block, ('lev', 'tile'), route)  25 us
    pallas_call x1, Pallas kernels, per_device(): call(functools.partial(window_body, levs), [((window, width), BF16)] * 2,...  8.95 us
    dynamic_slice x1, local copies, waits for them, and re-layouts, per_device(): lax.dynamic_index_in_dim(w_up.reshape(width, groups, 2, part), parity, 2,...  8.15 us
    pallas_call x1, Pallas kernels, per_device(): call(grad_body, [((2 * quarter, hidden // 2), BF16), ((2 * quarter, hidde...  7.22 us
    unnamed x27, local copies, waits for them, and re-layouts  6.37 us
    reshape x1, local copies, waits for them, and re-layouts, per_device(): w_up.reshape(width, groups, 2, part)  2.75 us
    pallas_call x1, Pallas kernels, per_device(): call(mlp_body, [((rows, width), BF16)] * 2, n_in=4, flops=2 * 10 ** 9, mo...  1.93 us
  transfers between devices with their start and end apart: 21, of which 6 were waited for; matrix products, arithmetic and copies ran while one was open for 16% of the time, Pallas kernels for 20%

commit v1 on v0

v1 whole, which is shorter than its diff:
```python
import functools

import jax
import jax.numpy as jnp
from jax import lax
from jax.experimental import pallas as pl
from jax.experimental.pallas import tpu as pltpu
from jax.sharding import PartitionSpec as P

HEADS = 8
LATENT = 4
WL = 2
WA = 6
WO = 12
HALF = WO // 2
PIECE = WA * HALF
MARK = 2.0**40
F32 = jnp.float32
BF16 = jnp.bfloat16
MIB = 1 << 20


def dot(a, b, contract=((1,), (0,))):
    return lax.dot_general(a, b, (contract, ((), ())), preferred_element_type=F32)


def call(body, outs, scratch=(), vmem=40, flops=0, moved=0, n_in=1):
    return pl.pallas_call(
        body,
        out_shape=[jax.ShapeDtypeStruct(shape, dtype) for shape, dtype in outs],
        in_specs=[pl.BlockSpec(memory_space=pltpu.VMEM)] * n_in,
        out_specs=[pl.BlockSpec(memory_space=pltpu.VMEM)] * len(outs),
        scratch_shapes=list(scratch),
        compiler_params=pltpu.CompilerParams(vmem_limit_bytes=vmem * MIB),
        cost_estimate=pl.CostEstimate(flops=flops, bytes_accessed=moved, transcendentals=0),
    )


def layer_norm(rows, gain):
    mean = jnp.mean(rows, -1, keepdims=True)
    centred = rows - mean
    spread = jnp.mean(centred * centred, -1, keepdims=True)
    return (centred * lax.rsqrt(spread + 1e-05) * gain).astype(BF16)


def gelu_parts(x):
    square = x * x
    t = jnp.tanh(x * (0.7978845608028654 + 0.7978845608028654 * 0.044715 * square))
    return square, t


def lat_rolled(cells):
    return pltpu.roll(cells, cells.shape[0] - WA // 2, 0)


def pack_levels_body(lev_count, mask_ref, lev_ref, *refs):
    outs, blocks = refs[:-1], refs[-1]
    count = lev_ref.shape[0]
    me = lax.axis_index("lev")
    for j in range(count):
        live = jnp.broadcast_to(mask_ref[:, j : j + 1] > 0, lev_ref.shape[2:])
        for o in range(WO):
            cells = lat_rolled(jnp.where(live, lev_ref[j, o].astype(F32), MARK))
            half, at = 1 - o // HALF, j * PIECE + (o % HALF) * WA
            for i in range(lev_count):
                blocks[half * lev_count + i, pl.ds(at, WA)] = cells[i * WA : (i + 1) * WA]
    for half in range(2):
        for d in range(lev_count):
            outs[half * lev_count + d][...] = blocks[half * lev_count + (me ^ d)].astype(BF16)


def pack_cot_body(lev_count, cot_ref, east_ref, west_ref, blocks):
    me = lax.axis_index("lev")
    rows = LATENT * PIECE
    for l in range(LATENT):
        for o in range(WO):
            cells = lat_rolled(cot_ref[(l + WL // 2) % LATENT, o].astype(F32))
            half, at = 1 - o // HALF, l * PIECE + (o % HALF) * WA
            for i in range(lev_count):
                blocks[half * lev_count + i, pl.ds(at, WA)] = cells[i * WA : (i + 1) * WA]
    for half, ref in enumerate((east_ref, west_ref)):
        for slot in range(2):
            ref[slot * rows : (slot + 1) * rows] = blocks[
                half * lev_count + (me ^ (2 * slot))
            ].astype(BF16)


def aggregate_body(*refs):
    chunks, (query_ref, w_key, w_value, out_ref, pool) = refs[:-5], refs[-5:]
    width = w_key.shape[0]
    head_size = width // HEADS
    pairs = 2 * PIECE
    lanes = LATENT * HEADS
    owner = lax.broadcasted_iota(jnp.int32, (HEADS, width), 1) // head_size
    table = (owner == lax.broadcasted_iota(jnp.int32, (HEADS, width), 0)).astype(F32)
    query = query_ref[...].astype(F32)
    block_query = jnp.concatenate([table * query[l : l + 1] for l in range(LATENT)], 0)
    rows = jnp.concatenate([ref[...] for ref in chunks], 0)
    blocks = rows.shape[0] // pairs
    split = [slice(b * pairs, (b + 1) * pairs) for b in range(blocks)]
    keys = dot(rows, w_key[...]).astype(BF16)
    values = dot(rows, w_value[...]).astype(BF16).astype(F32)
    scores = dot(keys, block_query.astype(BF16), ((1,), (1,))) * head_size ** (-0.5)
    live = rows[:, :lanes].astype(F32) < MARK / 2
    scores = jnp.where(live, scores, -1e30)
    top = functools.reduce(jnp.maximum, [scores[at] for at in split])
    top = jnp.maximum(top, pltpu.roll(top, PIECE, 0))
    weights = [jnp.exp(scores[at] - top) * live[at].astype(F32) for at in split]
    total = functools.reduce(jnp.add, weights)
    total = total + pltpu.roll(total, PIECE, 0)
    inverse = 1.0 / total
    weights = jnp.concatenate([w * inverse for w in weights], 0)
    high = weights.astype(BF16)
    low = (weights - high.astype(F32)).astype(BF16)
    step = 256
    per = step // head_size
    for l in range(LATENT):
        slot = (l - WL // 2) % LATENT
        for n in range(width // step):
            head = lax.broadcasted_iota(jnp.int32, (lanes, step), 1) // head_size
            head = head + (l * HEADS + n * per)
            pick = (head == lax.broadcasted_iota(jnp.int32, (lanes, step), 0)).astype(BF16)
            at = slice(n * step, (n + 1) * step)
            prod = (dot(high, pick) + dot(low, pick)) * values[:, at]
            summed = functools.reduce(jnp.add, [prod[rows_at] for rows_at in split])
            summed = summed + pltpu.roll(summed, PIECE, 0)
            pool[pl.ds(slot * PIECE, PIECE), at] = summed[:PIECE]
    out_ref[...] = pool[...].astype(BF16)


def window_attention(lev_count, latent, gain, w_qkv):
    width = latent.shape[1]
    head_size = width // HEADS
    half = LATENT * PIECE
    slab = WL * PIECE
    size = 2 * slab
    normed = layer_norm(latent.astype(F32), gain[...])
    qkv = dot(normed, w_qkv[...])
    last = lax.axis_index("lev") == lev_count - 1
    shape = (2 * size, size)
    q_at = lax.rem(lax.broadcasted_iota(jnp.int32, shape, 0), slab)
    k_at = lax.rem(lax.broadcasted_iota(jnp.int32, shape, 1), slab)
    q_lat = lax.rem(q_at, WA) >= WA // 2
    k_lat = lax.rem(k_at, WA) >= WA // 2
    lat_differs = jnp.where(last, (q_lat != k_lat).astype(F32), 0.0)
    lev_differs = ((q_at >= PIECE) != (k_at >= PIECE)).astype(F32)
    lane = lax.broadcasted_iota(jnp.int32, (size, 2 * head_size), 1) < head_size
    mixed = []
    for lb in range(LATENT // WL):
        rows = jnp.concatenate(
            [qkv[lb * slab : (lb + 1) * slab], qkv[half + lb * slab : half + (lb + 1) * slab]], 0
        )
        differs = lat_differs + lev_differs if lb == LATENT // WL - 1 else lat_differs
        allowed = differs == 0.0
        outs = []
        for p in range(HEADS // 2):
            at = 2 * p * head_size
            query = rows[:, at : at + 2 * head_size]
            key = rows[:, width + at : width + at + 2 * head_size].astype(BF16)
            value = rows[:, 2 * width + at : 2 * width + at + 2 * head_size].astype(BF16)
            query = jnp.concatenate([jnp.where(lane, query, 0.0), jnp.where(lane, 0.0, query)], 0)
            scores = dot(query.astype(BF16), key, ((1,), (1,))) * head_size ** (-0.5)
            scores = jnp.where(allowed, scores, -1e30)
            weights = jnp.exp(scores - jnp.max(scores, -1, keepdims=True))
            probs = weights * (1.0 / jnp.sum(weights, -1, keepdims=True))
            out = dot(probs.astype(BF16), value)
            outs.append(jnp.where(lane, out[:size], out[size:]))
        mixed.append(jnp.concatenate(outs, 1))
    mixed = [m[:slab] for m in mixed] + [m[slab:] for m in mixed]
    return jnp.concatenate(mixed, 0).astype(BF16)


def window_body(
    lev_count,
    east,
    west,
    w_agg_out,
    gain_attn,
    w_qkv,
    w_proj,
    gain_mlp,
    resid_ref,
    normed2_ref,
):
    pooled = jnp.concatenate([east[...], west[...]], 0)
    latent = dot(pooled, w_agg_out[...]).astype(BF16)
    mixed = window_attention(lev_count, latent, gain_attn, w_qkv)
    resid = (latent.astype(F32) + dot(mixed, w_proj[...])).astype(BF16)
    resid_ref[...] = resid
    normed2_ref[...] = layer_norm(resid.astype(F32), gain_mlp[...])


def mlp_body(resid, normed2, w_up, w_down, east_ref, west_ref):
    step = 512
    rows = normed2[...]
    total = resid[...].astype(F32)
    for n in range(w_up.shape[1] // step):
        inner = dot(rows, w_up[:, n * step : (n + 1) * step])
        _, t = gelu_parts(inner)
        active = (inner * (0.5 * (1.0 + t))).astype(BF16)
        total = total + dot(active, w_down[n * step : (n + 1) * step])
    total = total.astype(BF16)
    half = rows.shape[0] // 2
    east_ref[...] = total[:half]
    west_ref[...] = total[half:]


def grad_body(chunks, last, cot_at, part, *refs):
    normed2 = refs[:chunks]
    cots = refs[chunks : chunks + 4]
    w_up, w_down = refs[chunks + 4 : chunks + 6]
    rest = refs[chunks + 6 :]
    n_half, c_half = rest[-2:]
    if last:
        sum_up, sum_dn, send, keep, acc_up, acc_dn = rest[:-2]
    else:
        acc_up, acc_dn = rest[:-2]
    me = lax.axis_index("lev")
    model, cols = acc_up.shape
    half_at = pl.ds(pl.multiple_of((me // 2) * model, model), model)
    piece = cots[0].shape[0] // 2
    rows, backs = [], []
    for k, (pair, slot) in enumerate(cot_at):
        at = slice(slot * piece, (slot + 1) * piece)
        rows.append(normed2[k][...])
        n_half[2 * k * piece : 2 * (k + 1) * piece] = normed2[k][:, half_at]
        for h in range(2):
            backs.append(cots[2 * pair + h][at])
            to = (2 * k + h) * piece
            c_half[to : to + piece] = cots[2 * pair + h][at, half_at]
    rows = jnp.concatenate(rows, 0)
    backs = jnp.concatenate(backs, 0)
    n_half_v = n_half[...]
    c_half_v = c_half[...]
    picked = w_up.shape[1] != cols
    step = part if picked else 256
    parity = lax.rem(lax.axis_index("tile"), 2)
    for n in range(cols // step):
        at = slice(n * step, (n + 1) * step)
        take = pl.ds(pl.multiple_of((2 * n + parity) * step, step), step) if picked else at
        x = dot(rows, w_up[:, take])
        back = dot(backs, w_down[take], ((1,), (1,)))
        square, t = gelu_parts(x)
        cdf = 0.5 + 0.5 * t
        active = (x * cdf).astype(BF16)
        slope = (0.5 * 0.7978845608028654) + (1.5 * 0.7978845608028654 * 0.044715) * square
        dinner = (back * (cdf + x * ((1.0 - t * t) * slope))).astype(BF16)
        up = dot(n_half_v, dinner, ((0,), (0,)))
        dn = dot(c_half_v, active, ((0,), (0,)))
        acc_up[:, at] = up + sum_up[:, at] if last else up
        acc_dn[:, at] = dn + sum_dn[:, at] if last else dn
    if last:
        quarter = model // 2
        core = lax.rem(me, 2)
        mine = pl.ds(pl.multiple_of(core * quarter, quarter), quarter)
        other = pl.ds(pl.multiple_of((1 - core) * quarter, quarter), quarter)
        keep[:quarter] = acc_up[mine]
        keep[quarter:] = acc_dn[mine]
        send[:quarter] = acc_up[other].astype(BF16)
        send[quarter:] = acc_dn[other].astype(BF16)


def split_body(groups, keep, recv, own_ref, *refs):
    outs, blocks = refs[:-1], refs[-1]
    cols = keep.shape[1] // groups
    for n in range(groups):
        at = slice(n * cols, (n + 1) * cols)
        blocks[n] = keep[:, at] + recv[:, at].astype(F32)
    me = lax.axis_index("tile") // 2
    own_ref[...] = blocks[me]
    for d in range(1, groups):
        outs[d - 1][...] = blocks[lax.rem(me + d, groups)].astype(BF16)


def total_body(own, *refs):
    received, (up_ref, dn_ref) = refs[:-2], refs[-2:]
    total = own[...]
    for part in received:
        total = total + part[...].astype(F32)
    half = total.shape[0] // 2
    up_ref[...] = total[:half]
    dn_ref[...] = total[half:]


def unpack_body(*refs):
    parts, out_ref, scratch, blocks = refs[:-3], refs[-3], refs[-2], refs[-1]
    me = lax.axis_index("lev")
    half = LATENT * PIECE
    for d, part in enumerate(parts):
        blocks[me ^ d] = part[...].astype(F32)
    for l in range(LATENT):
        for o in range(WO):
            at = (half if o < HALF else 0) + l * PIECE + (o % HALF) * WA
            cells = jnp.concatenate(
                [blocks[i, pl.ds(at, WA)] for i in range(len(parts))], 0
            )
            cells = pltpu.roll(cells, WA // 2, 0)
            out_ref[(l + WL // 2) % LATENT, o] = cells.astype(BF16)


def exchanged(block, lev_step, tile_move):
    levs, tiles = lax.axis_size("lev"), lax.axis_size("tile")
    route = [
        (l * tiles + t, (l ^ lev_step) * tiles + tile_move(t)) for l in range(levs) for t in range(tiles)
    ]
    return lax.ppermute(block, ("lev", "tile"), route)


def per_device(
    levels,
    level_mask,
    w_key,
    w_value,
    latent_query,
    w_agg_out,
    gain_attn,
    w_qkv,
    w_proj,
    gain_mlp,
    w_up,
    w_down,
    cotangent,
):
    levs, tiles = lax.axis_size("lev"), lax.axis_size("tile")
    count, lat, lon, width = levels.shape
    hidden = w_up.shape[1]
    assert lat == levs * WA and lon == WO and levs == 4 and tiles % 2 == 0
    piece = count * PIECE
    rows = LATENT * PIECE
    window = 2 * rows
    groups = tiles // 2
    part = hidden // tiles
    quarter = width // levs

    west = lambda t: (t - 1) % tiles
    east = lambda t: (t + 1) % tiles
    same = lambda t: t
    peer = lambda t: t ^ 1
    next_pair = lambda t: (t - 2) % tiles if t % 2 == 0 else t

    packed = call(
        functools.partial(pack_levels_body, levs),
        [((piece, width), BF16)] * (2 * levs),
        [pltpu.VMEM((2 * levs, piece, width), F32)],
        n_in=2,
        moved=3 * MIB,
        vmem=16,
    )(level_mask[None], levels.transpose(0, 2, 1, 3))
    easts = [packed[0]] + [exchanged(packed[d], d, same) for d in range(1, levs)]
    wests = [exchanged(packed[levs + d], d, west) for d in range(levs)]

    cot_east, cot_west = call(
        functools.partial(pack_cot_body, levs),
        [((window, width), BF16)] * 2,
        [pltpu.VMEM((2 * levs, rows, width), F32)],
        n_in=1,
        moved=2 * MIB,
        vmem=16,
    )(cotangent.transpose(0, 2, 1, 3))
    cot_own_w = exchanged(cot_west, 0, west)
    cot_peer_e = exchanged(cot_east, 0, peer)
    cot_peer_w = exchanged(cot_west, 0, next_pair)
    cots = (cot_east, cot_own_w, cot_peer_e, cot_peer_w)

    pooled = [
        call(
            aggregate_body,
            [((rows, width), BF16)],
            [pltpu.VMEM((rows, width), F32)],
            n_in=levs + 3,
            flops=10**9,
            moved=2 * MIB,
            vmem=16,
        )(*chunks, latent_query, w_key, w_value)[0]
        for chunks in (easts, wests)
    ]
    resid, normed2 = call(
        functools.partial(window_body, levs),
        [((window, width), BF16)] * 2,
        n_in=7,
        flops=2 * 10**9,
        moved=4 * MIB,
        vmem=24,
    )(*pooled, w_agg_out, gain_attn[None], w_qkv, w_proj, gain_mlp[None])
    normed2_peer = exchanged(normed2, 0, peer)
    normed2_beside = exchanged(normed2, 2, same)
    normed2_far = exchanged(normed2, 2, peer)

    out_e, out_w = call(
        mlp_body,
        [((rows, width), BF16)] * 2,
        n_in=4,
        flops=2 * 10**9,
        moved=6 * MIB,
        vmem=20,
    )(resid, normed2, w_up, w_down)
    own_rows = jnp.concatenate([out_e, exchanged(out_w, 0, east)], 0)
    all_rows = [own_rows] + [exchanged(own_rows, d, same) for d in range(1, levs)]

    if part % 128:
        parity = lax.rem(lax.axis_index("tile"), 2)
        w_up = lax.dynamic_index_in_dim(
            w_up.reshape(width, groups, 2, part), parity, 2, keepdims=False
        ).reshape(width, groups * part)
        w_down = lax.dynamic_index_in_dim(
            w_down.reshape(groups, 2, part, width), parity, 1, keepdims=False
        ).reshape(groups * part, width)
    sums = [((2 * quarter, hidden // 2), F32)] * 2
    halves = lambda n: [pltpu.VMEM((n * window, 2 * quarter), BF16)] * 2
    early = call(
        functools.partial(grad_body, 3, False, ((0, 0), (0, 1), (1, 0)), part),
        sums,
        halves(3),
        n_in=9,
        flops=4 * 10**9,
        moved=8 * MIB,
        vmem=32,
    )(normed2, normed2_beside, normed2_peer, *cots, w_up, w_down)
    send, keep = call(
        functools.partial(grad_body, 1, True, ((1, 1),), part),
        [((2 * quarter, hidden // 2), BF16), ((2 * quarter, hidden // 2), F32)],
        [pltpu.VMEM((2 * quarter, hidden // 2), F32)] * 2 + halves(1),
        n_in=9,
        flops=10**9,
        moved=8 * MIB,
        vmem=32,
    )(normed2_far, *cots, w_up, w_down, *early)
    recv = exchanged(send, 1, same)
    own, *sends = call(
        functools.partial(split_body, groups),
        [((2 * quarter, part), F32)] + [((2 * quarter, part), BF16)] * (groups - 1),
        [pltpu.VMEM((groups, 2 * quarter, part), F32)],
        n_in=2,
        moved=2 * MIB,
        vmem=32,
    )(keep, recv)
    received = [
        exchanged(block, 0, lambda t, d=d: (t + 2 * d) % tiles) for d, block in enumerate(sends, 1)
    ]
    grad_up, grad_down_t = call(
        total_body,
        [((quarter, part), F32)] * 2,
        n_in=groups,
        moved=1 * MIB,
        vmem=16,
    )(own, *received)
    encoded = call(
        unpack_body,
        [((LATENT, lon, lat, width), BF16)],
        [pltpu.VMEM((window, width), F32), pltpu.VMEM((levs, window, width), F32)],
        n_in=levs,
        moved=3 * MIB,
        vmem=24,
    )(*all_rows)[0]
    return (encoded.transpose(0, 2, 1, 3), grad_up, grad_down_t)


def solution(mesh):
    return jax.shard_map(
        per_device,
        mesh=mesh,
        in_specs=(
            P("lev", None, "tile", None),
            P("lev"),
            P(),
            P(),
            P(),
            P(),
            P(),
            P(),
            P(),
            P(),
            P(),
            P(),
            P(None, None, "tile", None),
        ),
        out_specs=(P(None, None, "tile", None), P("lev", "tile"), P("lev", "tile")),
        check_vma=False,
    )
```

time: 94.6 us -> 75.1 us (0.79)
  local copies, waits for them, and re-layouts: 18.3 us -> 2 us
  waiting for transfers between devices: 25 us -> 19.7 us
  starting transfers between devices: 27.9 us -> 32.4 us
  Pallas kernels: 21.5 us -> 19.9 us
    dynamic_slice x2 -> x0, local copies, waits for them, and re-layouts: 9.2 us -> none  [the longest x1 8.15 us: per_device(): lax.dynamic_index_in_dim(w_up.reshape(width, groups, 2, part), parity, 2,...]
    pallas_call x1, Pallas kernels: 8.95 us -> 2.78 us  [per_device(): call(functools.partial(window_body, levs), [((window, width), BF16)] * 2,...]
    pallas_call x4 -> x7, Pallas kernels: 8.65 us -> 14.3 us  [the longest x2 4.81 us: per_device(): call(aggregate_body, [((rows, width), BF16)], [pltpu.VMEM((rows, width),...]
    ppermute x21, waiting for transfers between devices: 25 us -> 19.7 us  [exchanged(): return lax.ppermute(block, ('lev', 'tile'), route)]
    ppermute x21, starting transfers between devices: 27.9 us -> 32.4 us  [exchanged(): return lax.ppermute(block, ('lev', 'tile'), route)]
    unnamed x27, local copies, waits for them, and re-layouts: 6.37 us -> 1.99 us
    reshape x1 -> x0, local copies, waits for them, and re-layouts: 2.75 us -> none  [per_device(): w_up.reshape(width, groups, 2, part)]
    pallas_call x1, Pallas kernels: 1.81 us -> 0.69 us  [per_device(): call(functools.partial(pack_levels_body, levs), [((piece, width), BF16)]...]
  transfers between devices with their start and end apart: 21 -> 21, of which waited for: 6 -> 9; matrix products, arithmetic and copies ran while one was open for 16% -> 0% of each run, Pallas kernels for 20% -> 25%
where the time goes in v1:
time: 75.1 us; the launch traced here: 74.9 us
  starting transfers between devices  32.4 us (43%)
  Pallas kernels  19.9 us (26%)
  waiting for transfers between devices  19.7 us (26%)
  local copies, waits for them, and re-layouts  2 us (3%)
  between operations  0.91 us (1%)
    ppermute x21, starting transfers between devices, exchanged(): return lax.ppermute(block, ('lev', 'tile'), route)  32.4 us
    ppermute x21, waiting for transfers between devices, exchanged(): return lax.ppermute(block, ('lev', 'tile'), route)  19.7 us
    pallas_call x2, Pallas kernels, per_device(): call(aggregate_body, [((rows, width), BF16)], [pltpu.VMEM((rows, width),...  4.81 us
    pallas_call x1, Pallas kernels, per_device(): call(functools.partial(grad_body, 3, False, ((0, 0), (0, 1), (1, 0)), par...  4.13 us
    pallas_call x1, Pallas kernels, per_device(): call(functools.partial(window_body, levs), [((window, width), BF16)] * 2,...  2.78 us
    pallas_call x1, Pallas kernels, per_device(): call(functools.partial(grad_body, 1, True, ((1, 1),), part), [((2 * quart...  2.54 us
    unnamed x27, local copies, waits for them, and re-layouts  1.99 us
    pallas_call x1, Pallas kernels, per_device(): call(mlp_body, [((rows, width), BF16)] * 2, n_in=4, flops=2 * 10 ** 9, mo...  1.93 us
  transfers between devices with their start and end apart: 21, of which 9 were waited for; matrix products, arithmetic and copies ran while one was open for 0% of the time, Pallas kernels for 25%

profile of v1, /device:TPU:0, one launch (start us, length us, event | category | flops | bytes accessed | tf_op | source)
XLA Modules:
  0.0 74.9 jit_solution(13075549252812876310)
XLA Ops:
  0.6 1.3 %copy-done.2 = bf16[4,24,12,512]{3,1,2,0:T(8,128)(2,1)S(1)} copy-done((bf16[4,24,12,512]{3,1,2,0:T(8,128)(2,1)S(1)}, bf16[4,24,12,512]{3,1,2,0:T(8,128)(2,1)}, u32[]{:S(2)}) %copy-start.2) | copy-done | bytes 1179672
  3.3 6.0 %collective-permute-start.3 = (bf16[144,512]{1,0:T(8,128)(2,1)S(1)}, bf16[144,512]{1,0:T(8,128)(2,1)S(1)}, u32[]{:S(2)}, u32[]{:S(2)}) collective-permute-start(bf16[144,512]{1,0:T(8,128)(2,1)S(1)} %get-tuple-element.31), channel_id=1, source_target_pairs={{0,7},{1,0},{2,1},{3,2},{4,3},{5,4},{6,5},{7,6},{8,15},{9,8},{10,9... | collective-permute-start | bytes 442376 | tf_op jit(solution)/shard_map/ppermute | solution.py:306
  9.3 2.0 %collective-permute-start.5 = (bf16[144,512]{1,0:T(8,128)(2,1)S(1)}, bf16[144,512]{1,0:T(8,128)(2,1)S(1)}, u32[]{:S(2)}, u32[]{:S(2)}) collective-permute-start(bf16[144,512]{1,0:T(8,128)(2,1)S(1)} %get-tuple-element.33), channel_id=1, source_target_pairs={{0,23},{1,16},{2,17},{3,18},{4,19},{5,20},{6,21},{7,22},{8,31},{9,... | collective-permute-start | bytes 442376 | tf_op jit(solution)/shard_map/ppermute | solution.py:306
  12.2 1.3 %collective-permute-done.3.refs_0_ = bf16[144,512]{1,0:T(8,128)(2,1)S(1)} collective-permute-done((bf16[144,512]{1,0:T(8,128)(2,1)S(1)}, bf16[144,512]{1,0:T(8,128)(2,1)S(1)}, u32[]{:S(2)}, u32[]{:S(2)}) %collective-permute-start.3) | collective-permute-done | bytes 147488 | tf_op jit(solution)/shard_map/ppermute | solution.py:306
  13.5 1.5 %collective-permute-start.1 = (bf16[144,512]{1,0:T(8,128)(2,1)S(1)}, bf16[144,512]{1,0:T(8,128)(2,1)S(1)}, u32[]{:S(2)}, u32[]{:S(2)}) collective-permute-start(bf16[144,512]{1,0:T(8,128)(2,1)S(1)} %get-tuple-element.29), channel_id=1, source_target_pairs={{0,16},{1,17},{2,18},{3,19},{4,20},{5,21},{6,22},{7,23},{8,24},{9,... | collective-permute-start | bytes 442376 | tf_op jit(solution)/shard_map/ppermute | solution.py:306
  15.1 1.6 %collective-permute-done.4.refs_1_ = bf16[144,512]{1,0:T(8,128)(2,1)S(1)} collective-permute-done((bf16[144,512]{1,0:T(8,128)(2,1)S(1)}, bf16[144,512]{1,0:T(8,128)(2,1)S(1)}, u32[]{:S(2)}, u32[]{:S(2)}) %collective-permute-start.4) | collective-permute-done | bytes 147488 | tf_op jit(solution)/shard_map/ppermute | solution.py:306
  17.2 2.7 %collective-permute-done.5.refs_2_ = bf16[144,512]{1,0:T(8,128)(2,1)S(1)} collective-permute-done((bf16[144,512]{1,0:T(8,128)(2,1)S(1)}, bf16[144,512]{1,0:T(8,128)(2,1)S(1)}, u32[]{:S(2)}, u32[]{:S(2)}) %collective-permute-start.5) | collective-permute-done | bytes 147488 | tf_op jit(solution)/shard_map/ppermute | solution.py:306
  19.9 6.2 %collective-permute-start.12 = (bf16[288,512]{1,0:T(8,128)(2,1)S(1)}, bf16[288,512]{1,0:T(8,128)(2,1)S(1)}, u32[]{:S(2)}, u32[]{:S(2)}) collective-permute-start(bf16[288,512]{1,0:T(8,128)(2,1)S(1)} %get-tuple-element.40), channel_id=1, source_target_pairs={{0,7},{1,0},{2,1},{3,2},{4,3},{5,4},{6,5},{7,6},{8,15},{9,8},{10,9... | collective-permute-start | bytes 884744 | tf_op jit(solution)/shard_map/ppermute | solution.py:306
  26.1 1.9 %collective-permute-start.14 = (bf16[288,512]{1,0:T(8,128)(2,1)S(1)}, bf16[288,512]{1,0:T(8,128)(2,1)S(1)}, u32[]{:S(2)}, u32[]{:S(2)}) collective-permute-start(bf16[288,512]{1,0:T(8,128)(2,1)S(1)} %get-tuple-element.40), channel_id=1, source_target_pairs={{0,6},{1,1},{2,0},{3,3},{4,2},{5,5},{6,4},{7,7},{8,14},{9,9},{10,8... | collective-permute-start | bytes 884744 | tf_op jit(solution)/shard_map/ppermute | solution.py:306
  28.1 2.4 %shard_map.150.west = bf16[144,512]{1,0:T(8,128)(2,1)S(1)} custom-call(bf16[144,512]{1,0:T(8,128)(2,1)S(1)} %collective-permute-done.3.refs_0_, bf16[144,512]{1,0:T(8,128)(2,1)S(1)} %collective-permute-done.4.refs_1_, bf16[144,512]{1,0:T(8,128)(2,1)S(1)} %collective-permute-done.5.refs_2_, bf16[144,512]{1,0:T(8,128)(2,1)S(1)} %collective-permute-done.6.refs_3_, ...), custom_call_target="tpu_custom_call" | custom-call | flops 1000000000 | bytes 2097152 | tf_op jit(solution)/shard_map/pallas_call | solution.py:366
  30.6 2.4 %shard_map.149.east = bf16[144,512]{1,0:T(8,128)(2,1)S(1)} custom-call(bf16[144,512]{1,0:T(8,128)(2,1)S(1)} %get-tuple-element.27.refs_0_, bf16[144,512]{1,0:T(8,128)(2,1)S(1)} %collective-permute-done.refs_1_, bf16[144,512]{1,0:T(8,128)(2,1)S(1)} %collective-permute-done.1.refs_2_, bf16[144,512]{1,0:T(8,128)(2,1)S(1)} %collective-permute-done.2.refs_3_, ...), custom_call_target="tpu_custom_call" | custom-call | flops 1000000000 | bytes 2097152 | tf_op jit(solution)/shard_map/pallas_call | solution.py:366
  33.1 2.8 %shard_map.151 = (bf16[288,512]{1,0:T(8,128)(2,1)S(1)}, bf16[288,512]{1,0:T(8,128)(2,1)S(1)}) custom-call(bf16[144,512]{1,0:T(8,128)(2,1)S(1)} %shard_map.149.east, bf16[144,512]{1,0:T(8,128)(2,1)S(1)} %shard_map.150.west, bf16[512,512]{1,0:T(8,128)(2,1)S(1)} %copy-done.8, f32[1,512]{1,0:T(1,128)S(1)} %bitcast.9, bf16[512,1536]{1,0:T(8,128)(2,1)S(1)} %copy-done.5, ...), custom_call_target="tpu_custom_call" | custom-call | flops 2000000000 | bytes 4194304 | tf_op jit(solution)/shard_map/pallas_call | solution.py:377
  36.5 2.0 %collective-permute-start.16 = (bf16[288,512]{1,0:T(8,128)(2,1)S(1)}, bf16[288,512]{1,0:T(8,128)(2,1)S(1)}, u32[]{:S(2)}, u32[]{:S(2)}) collective-permute-start(bf16[288,512]{1,0:T(8,128)(2,1)S(1)} %get-tuple-element.36.normed2.refs_0_), channel_id=1, source_target_pairs={{0,1},{1,0},{2,3},{3,2},{4,5},{5,4},{6,7},{7,6},{8,9},{9,8},{10,11... | collective-permute-start | bytes 884744 | tf_op jit(solution)/shard_map/ppermute | solution.py:306
  38.5 1.9 %shard_map.152 = (bf16[144,512]{1,0:T(8,128)(2,1)S(1)}, bf16[144,512]{1,0:T(8,128)(2,1)S(1)}) custom-call(bf16[288,512]{1,0:T(8,128)(2,1)S(1)} %get-tuple-element.35.resid, bf16[288,512]{1,0:T(8,128)(2,1)S(1)} %get-tuple-element.36.normed2.refs_0_, bf16[512,2048]{1,0:T(8,128)(2,1)S(1)} %copy-done, bf16[2048,512]{1,0:T(8,128)(2,1)S(1)} %copy-done.1), custom_call_target="tpu_custom_call" | custom-call | flops 2000000000 | bytes 6291456 | tf_op jit(solution)/shard_map/pallas_call | solution.py:389
  41.5 2.0 %collective-permute-start.7 = (bf16[144,512]{1,0:T(8,128)(2,1)S(1)}, bf16[144,512]{1,0:T(8,128)(2,1)S(1)}, u32[]{:S(2)}, u32[]{:S(2)}) collective-permute-start(bf16[144,512]{1,0:T(8,128)(2,1)S(1)} %get-tuple-element.38), channel_id=1, source_target_pairs={{0,1},{1,2},{2,3},{3,4},{4,5},{5,6},{6,7},{7,0},{8,9},{9,10},{10,1... | collective-permute-start | bytes 442376 | tf_op jit(solution)/shard_map/ppermute | solution.py:306
  44.4 5.1 %collective-permute-done.16.refs_2_ = bf16[288,512]{1,0:T(8,128)(2,1)S(1)} collective-permute-done((bf16[288,512]{1,0:T(8,128)(2,1)S(1)}, bf16[288,512]{1,0:T(8,128)(2,1)S(1)}, u32[]{:S(2)}, u32[]{:S(2)}) %collective-permute-start.16) | collective-permute-done | bytes 294944 | tf_op jit(solution)/shard_map/ppermute | solution.py:306
  49.4 4.1 %shard_map.155 = (f32[256,1024]{1,0:T(8,128)S(1)}, f32[256,1024]{1,0:T(8,128)S(1)}) custom-call(bf16[288,512]{1,0:T(8,128)(2,1)S(1)} %get-tuple-element.36.normed2.refs_0_, bf16[288,512]{1,0:T(8,128)(2,1)S(1)} %collective-permute-done.15.refs_1_, bf16[288,512]{1,0:T(8,128)(2,1)S(1)} %collective-permute-done.16.refs_2_, ...), custom_call_target="tpu_custom_call" | custom-call | flops 4000000000 | bytes 8388608 | tf_op jit(solution)/shard_map/pallas_call | solution.py:410
  53.6 2.5 %shard_map.156 = (bf16[256,1024]{1,0:T(8,128)(2,1)S(1)}, f32[256,1024]{1,0:T(8,128)S(1)}) custom-call(bf16[288,512]{1,0:T(8,128)(2,1)S(1)} %collective-permute-done.11.refs_0_, bf16[288,512]{1,0:T(8,128)(2,1)S(1)} %get-tuple-element.39.refs_3_.refs_1_, bf16[288,512]{1,0:T(8,128)(2,1)S(1)} %collective-permute-done.12.refs_4_.refs_2_, ...), custom_call_target="tpu_custom_call" | custom-call | flops 1000000000 | bytes 8388608 | tf_op jit(solution)/shard_map/pallas_call | solution.py:419
  56.3 1.7 %collective-permute-start.10 = (bf16[288,512]{1,0:T(8,128)(2,1)S(1)}, bf16[288,512]{1,0:T(8,128)(2,1)S(1)}, u32[]{:S(2)}, u32[]{:S(2)}) collective-permute-start(bf16[288,512]{1,0:T(8,128)(2,1)S(1)} %constant_dynamic-update-slice_fusion.refs_0_), channel_id=1, source_target_pairs={{0,24},{1,25},{2,26},{3,27},{4,28},{5,29},{6,30},{7,31},{8,16},{9,... | collective-permute-start | bytes 884744 | tf_op jit(solution)/shard_map/ppermute | solution.py:306
  58.7 2.1 %collective-permute-start.18 = (bf16[256,256]{1,0:T(8,128)(2,1)S(1)}, bf16[256,256]{1,0:T(8,128)(2,1)S(1)}, u32[]{:S(2)}, u32[]{:S(2)}) collective-permute-start(bf16[256,256]{1,0:T(8,128)(2,1)S(1)} %get-tuple-element.46), channel_id=1, source_target_pairs={{0,2},{1,3},{2,4},{3,5},{4,6},{5,7},{6,0},{7,1},{8,10},{9,11},{10,... | collective-permute-start | bytes 393224 | tf_op jit(solution)/shard_map/ppermute | solution.py:306
  62.1 3.3 %collective-permute-done.10.refs_3_ = bf16[288,512]{1,0:T(8,128)(2,1)S(1)} collective-permute-done((bf16[288,512]{1,0:T(8,128)(2,1)S(1)}, bf16[288,512]{1,0:T(8,128)(2,1)S(1)}, u32[]{:S(2)}, u32[]{:S(2)}) %collective-permute-start.10) | collective-permute-done | bytes 294944 | tf_op jit(solution)/shard_map/ppermute | solution.py:306
  65.4 2.5 %collective-permute-start.20 = (bf16[256,256]{1,0:T(8,128)(2,1)S(1)}, bf16[256,256]{1,0:T(8,128)(2,1)S(1)}, u32[]{:S(2)}, u32[]{:S(2)}) collective-permute-start(bf16[256,256]{1,0:T(8,128)(2,1)S(1)} %get-tuple-element.48), channel_id=1, source_target_pairs={{0,6},{1,7},{2,0},{3,1},{4,2},{5,3},{6,4},{7,5},{8,14},{9,15},{10,... | collective-permute-start | bytes 393224 | tf_op jit(solution)/shard_map/ppermute | solution.py:306
  67.8 4.2 %collective-permute-done.9.refs_2_ = bf16[288,512]{1,0:T(8,128)(2,1)S(1)} collective-permute-done((bf16[288,512]{1,0:T(8,128)(2,1)S(1)}, bf16[288,512]{1,0:T(8,128)(2,1)S(1)}, u32[]{:S(2)}, u32[]{:S(2)}) %collective-permute-start.9) | collective-permute-done | bytes 294944 | tf_op jit(solution)/shard_map/ppermute | solution.py:306
  72.0 1.6 %shard_map.153 = bf16[4,12,24,512]{3,2,1,0:T(8,128)(2,1)} custom-call(bf16[288,512]{1,0:T(8,128)(2,1)S(1)} %constant_dynamic-update-slice_fusion.refs_0_, bf16[288,512]{1,0:T(8,128)(2,1)S(1)} %collective-permute-done.8.refs_1_, bf16[288,512]{1,0:T(8,128)(2,1)S(1)} %collective-permute-done.9.refs_2_, bf16[288,512]{1,0:T(8,128)(2,1)S(1)} %collective-permute-done.10.refs_3_), custom_call_target="tpu_custom_call" | custom-call | bytes 3145728 | tf_op jit(solution)/shard_map/pallas_call | solution.py:447
  (57 shorter events, 8.9 us)
Async XLA Ops:
  2.6 25.5 %copy-start.6 = (bf16[512,512]{1,0:T(8,128)(2,1)S(1)}, bf16[512,512]{1,0:T(8,128)(2,1)}, u32[]{:S(2)}) copy-start(bf16[512,512]{1,0:T(8,128)(2,1)} %refs_5_.4) | copy-start | bytes 1572868
  2.6 25.5 %copy-start.7 = (bf16[512,512]{1,0:T(8,128)(2,1)S(1)}, bf16[512,512]{1,0:T(8,128)(2,1)}, u32[]{:S(2)}) copy-start(bf16[512,512]{1,0:T(8,128)(2,1)} %refs_6_.4) | copy-start | bytes 1572868
  2.6 25.5 %copy-start.10 = (bf16[4,512]{1,0:T(4,128)(2,1)S(1)}, bf16[4,512]{1,0:T(4,128)(2,1)}, u32[]{:S(2)}) copy-start(bf16[4,512]{1,0:T(4,128)(2,1)} %refs_4_.3) | copy-start | bytes 12292
  3.3 10.3 %collective-permute-start.3 = (bf16[144,512]{1,0:T(8,128)(2,1)S(1)}, bf16[144,512]{1,0:T(8,128)(2,1)S(1)}, u32[]{:S(2)}, u32[]{:S(2)}) collective-permute-start(bf16[144,512]{1,0:T(8,128)(2,1)S(1)} %get-tuple-element.31), channel_id=1, source_target_pairs={{0,7},{1,0},{2,1},{3,2},{4,3},{5,4},{6,5},{7,6},{8,15},{9,8},{10,9... | collective-permute-start | bytes 442376 | tf_op jit(solution)/shard_map/ppermute | solution.py:306
  9.3 7.4 %collective-permute-start.4 = (bf16[144,512]{1,0:T(8,128)(2,1)S(1)}, bf16[144,512]{1,0:T(8,128)(2,1)S(1)}, u32[]{:S(2)}, u32[]{:S(2)}) collective-permute-start(bf16[144,512]{1,0:T(8,128)(2,1)S(1)} %get-tuple-element.32), channel_id=1, source_target_pairs={{0,15},{1,8},{2,9},{3,10},{4,11},{5,12},{6,13},{7,14},{8,7},{9,0},... | collective-permute-start | bytes 442376 | tf_op jit(solution)/shard_map/ppermute | solution.py:306
  9.3 10.6 %collective-permute-start.5 = (bf16[144,512]{1,0:T(8,128)(2,1)S(1)}, bf16[144,512]{1,0:T(8,128)(2,1)S(1)}, u32[]{:S(2)}, u32[]{:S(2)}) collective-permute-start(bf16[144,512]{1,0:T(8,128)(2,1)S(1)} %get-tuple-element.33), channel_id=1, source_target_pairs={{0,23},{1,16},{2,17},{3,18},{4,19},{5,20},{6,21},{7,22},{8,31},{9,... | collective-permute-start | bytes 442376 | tf_op jit(solution)/shard_map/ppermute | solution.py:306
  11.3 14.8 %collective-permute-start.6 = (bf16[144,512]{1,0:T(8,128)(2,1)S(1)}, bf16[144,512]{1,0:T(8,128)(2,1)S(1)}, u32[]{:S(2)}, u32[]{:S(2)}) collective-permute-start(bf16[144,512]{1,0:T(8,128)(2,1)S(1)} %get-tuple-element.34), channel_id=1, source_target_pairs={{0,31},{1,24},{2,25},{3,26},{4,27},{5,28},{6,29},{7,30},{8,23},{9,... | collective-permute-start | bytes 442376 | tf_op jit(solution)/shard_map/ppermute | solution.py:306
  12.1 18.4 %collective-permute-start = (bf16[144,512]{1,0:T(8,128)(2,1)S(1)}, bf16[144,512]{1,0:T(8,128)(2,1)S(1)}, u32[]{:S(2)}, u32[]{:S(2)}) collective-permute-start(bf16[144,512]{1,0:T(8,128)(2,1)S(1)} %get-tuple-element.28), channel_id=1, source_target_pairs={{0,8},{1,9},{2,10},{3,11},{4,12},{5,13},{6,14},{7,15},{8,0},{9,1},... | collective-permute-start | bytes 442376 | tf_op jit(solution)/shard_map/ppermute | solution.py:306
  13.5 17.0 %collective-permute-start.1 = (bf16[144,512]{1,0:T(8,128)(2,1)S(1)}, bf16[144,512]{1,0:T(8,128)(2,1)S(1)}, u32[]{:S(2)}, u32[]{:S(2)}) collective-permute-start(bf16[144,512]{1,0:T(8,128)(2,1)S(1)} %get-tuple-element.29), channel_id=1, source_target_pairs={{0,16},{1,17},{2,18},{3,19},{4,20},{5,21},{6,22},{7,23},{8,24},{9,... | collective-permute-start | bytes 442376 | tf_op jit(solution)/shard_map/ppermute | solution.py:306
  16.7 13.9 %collective-permute-start.2 = (bf16[144,512]{1,0:T(8,128)(2,1)S(1)}, bf16[144,512]{1,0:T(8,128)(2,1)S(1)}, u32[]{:S(2)}, u32[]{:S(2)}) collective-permute-start(bf16[144,512]{1,0:T(8,128)(2,1)S(1)} %get-tuple-element.30), channel_id=1, source_target_pairs={{0,24},{1,25},{2,26},{3,27},{4,28},{5,29},{6,30},{7,31},{8,16},{9,... | collective-permute-start | bytes 442376 | tf_op jit(solution)/shard_map/ppermute | solution.py:306
  19.9 21.6 %collective-permute-start.12 = (bf16[288,512]{1,0:T(8,128)(2,1)S(1)}, bf16[288,512]{1,0:T(8,128)(2,1)S(1)}, u32[]{:S(2)}, u32[]{:S(2)}) collective-permute-start(bf16[288,512]{1,0:T(8,128)(2,1)S(1)} %get-tuple-element.40), channel_id=1, source_target_pairs={{0,7},{1,0},{2,1},{3,2},{4,3},{5,4},{6,5},{7,6},{8,15},{9,8},{10,9... | collective-permute-start | bytes 884744 | tf_op jit(solution)/shard_map/ppermute | solution.py:306
  26.1 17.4 %collective-permute-start.14 = (bf16[288,512]{1,0:T(8,128)(2,1)S(1)}, bf16[288,512]{1,0:T(8,128)(2,1)S(1)}, u32[]{:S(2)}, u32[]{:S(2)}) collective-permute-start(bf16[288,512]{1,0:T(8,128)(2,1)S(1)} %get-tuple-element.40), channel_id=1, source_target_pairs={{0,6},{1,1},{2,0},{3,3},{4,2},{5,5},{6,4},{7,7},{8,14},{9,9},{10,8... | collective-permute-start | bytes 884744 | tf_op jit(solution)/shard_map/ppermute | solution.py:306
  30.5 9.9 %collective-permute-start.13 = (bf16[288,512]{1,0:T(8,128)(2,1)S(1)}, bf16[288,512]{1,0:T(8,128)(2,1)S(1)}, u32[]{:S(2)}, u32[]{:S(2)}) collective-permute-start(bf16[288,512]{1,0:T(8,128)(2,1)S(1)} %get-tuple-element.39.refs_3_.refs_1_), channel_id=1, source_target_pairs={{0,1},{1,0},{2,3},{3,2},{4,5},{5,4},{6,7},{7,6},{8,9},{9,8},{10,11... | collective-permute-start | bytes 884744 | tf_op jit(solution)/shard_map/ppermute | solution.py:306
  35.9 8.5 %collective-permute-start.15 = (bf16[288,512]{1,0:T(8,128)(2,1)S(1)}, bf16[288,512]{1,0:T(8,128)(2,1)S(1)}, u32[]{:S(2)}, u32[]{:S(2)}) collective-permute-start(bf16[288,512]{1,0:T(8,128)(2,1)S(1)} %get-tuple-element.36.normed2.refs_0_), channel_id=1, source_target_pairs={{0,16},{1,17},{2,18},{3,19},{4,20},{5,21},{6,22},{7,23},{8,24},{9,... | collective-permute-start | bytes 884744 | tf_op jit(solution)/shard_map/ppermute | solution.py:306
  36.5 12.9 %collective-permute-start.16 = (bf16[288,512]{1,0:T(8,128)(2,1)S(1)}, bf16[288,512]{1,0:T(8,128)(2,1)S(1)}, u32[]{:S(2)}, u32[]{:S(2)}) collective-permute-start(bf16[288,512]{1,0:T(8,128)(2,1)S(1)} %get-tuple-element.36.normed2.refs_0_), channel_id=1, source_target_pairs={{0,1},{1,0},{2,3},{3,2},{4,5},{5,4},{6,7},{7,6},{8,9},{9,8},{10,11... | collective-permute-start | bytes 884744 | tf_op jit(solution)/shard_map/ppermute | solution.py:306
  40.4 13.2 %collective-permute-start.11 = (bf16[288,512]{1,0:T(8,128)(2,1)S(1)}, bf16[288,512]{1,0:T(8,128)(2,1)S(1)}, u32[]{:S(2)}, u32[]{:S(2)}) collective-permute-start(bf16[288,512]{1,0:T(8,128)(2,1)S(1)} %get-tuple-element.36.normed2.refs_0_), channel_id=1, source_target_pairs={{0,17},{1,16},{2,19},{3,18},{4,21},{5,20},{6,23},{7,22},{8,25},{9,... | collective-permute-start | bytes 884744 | tf_op jit(solution)/shard_map/ppermute | solution.py:306
  41.5 14.8 %collective-permute-start.7 = (bf16[144,512]{1,0:T(8,128)(2,1)S(1)}, bf16[144,512]{1,0:T(8,128)(2,1)S(1)}, u32[]{:S(2)}, u32[]{:S(2)}) collective-permute-start(bf16[144,512]{1,0:T(8,128)(2,1)S(1)} %get-tuple-element.38), channel_id=1, source_target_pairs={{0,1},{1,2},{2,3},{3,4},{4,5},{5,6},{6,7},{7,0},{8,9},{9,10},{10,1... | collective-permute-start | bytes 442376 | tf_op jit(solution)/shard_map/ppermute | solution.py:306
  56.2 2.3 %collective-permute-start.17 = (bf16[256,1024]{1,0:T(8,128)(2,1)S(1)}, bf16[256,1024]{1,0:T(8,128)(2,1)S(1)}, u32[]{:S(2)}, u32[]{:S(2)}) collective-permute-start(bf16[256,1024]{1,0:T(8,128)(2,1)S(1)} %get-tuple-element.44), channel_id=1, source_target_pairs={{0,8},{1,9},{2,10},{3,11},{4,12},{5,13},{6,14},{7,15},{8,0},{9,1},... | collective-permute-start | bytes 1572872 | tf_op jit(solution)/shard_map/ppermute | solution.py:306
  56.3 9.1 %collective-permute-start.10 = (bf16[288,512]{1,0:T(8,128)(2,1)S(1)}, bf16[288,512]{1,0:T(8,128)(2,1)S(1)}, u32[]{:S(2)}, u32[]{:S(2)}) collective-permute-start(bf16[288,512]{1,0:T(8,128)(2,1)S(1)} %constant_dynamic-update-slice_fusion.refs_0_), channel_id=1, source_target_pairs={{0,24},{1,25},{2,26},{3,27},{4,28},{5,29},{6,30},{7,31},{8,16},{9,... | collective-permute-start | bytes 884744 | tf_op jit(solution)/shard_map/ppermute | solution.py:306
  58.0 9.8 %collective-permute-start.8 = (bf16[288,512]{1,0:T(8,128)(2,1)S(1)}, bf16[288,512]{1,0:T(8,128)(2,1)S(1)}, u32[]{:S(2)}, u32[]{:S(2)}) collective-permute-start(bf16[288,512]{1,0:T(8,128)(2,1)S(1)} %constant_dynamic-update-slice_fusion.refs_0_), channel_id=1, source_target_pairs={{0,8},{1,9},{2,10},{3,11},{4,12},{5,13},{6,14},{7,15},{8,0},{9,1},... | collective-permute-start | bytes 884744 | tf_op jit(solution)/shard_map/ppermute | solution.py:306
  58.0 14.0 %collective-permute-start.9 = (bf16[288,512]{1,0:T(8,128)(2,1)S(1)}, bf16[288,512]{1,0:T(8,128)(2,1)S(1)}, u32[]{:S(2)}, u32[]{:S(2)}) collective-permute-start(bf16[288,512]{1,0:T(8,128)(2,1)S(1)} %constant_dynamic-update-slice_fusion.refs_0_), channel_id=1, source_target_pairs={{0,16},{1,17},{2,18},{3,19},{4,20},{5,21},{6,22},{7,23},{8,24},{9,... | collective-permute-start | bytes 884744 | tf_op jit(solution)/shard_map/ppermute | solution.py:306
  58.7 14.9 %collective-permute-start.18 = (bf16[256,256]{1,0:T(8,128)(2,1)S(1)}, bf16[256,256]{1,0:T(8,128)(2,1)S(1)}, u32[]{:S(2)}, u32[]{:S(2)}) collective-permute-start(bf16[256,256]{1,0:T(8,128)(2,1)S(1)} %get-tuple-element.46), channel_id=1, source_target_pairs={{0,2},{1,3},{2,4},{3,5},{4,6},{5,7},{6,0},{7,1},{8,10},{9,11},{10,... | collective-permute-start | bytes 393224 | tf_op jit(solution)/shard_map/ppermute | solution.py:306
  60.9 12.7 %collective-permute-start.19 = (bf16[256,256]{1,0:T(8,128)(2,1)S(1)}, bf16[256,256]{1,0:T(8,128)(2,1)S(1)}, u32[]{:S(2)}, u32[]{:S(2)}) collective-permute-start(bf16[256,256]{1,0:T(8,128)(2,1)S(1)} %get-tuple-element.47), channel_id=1, source_target_pairs={{0,4},{1,5},{2,6},{3,7},{4,0},{5,1},{6,2},{7,3},{8,12},{9,13},{10,... | collective-permute-start | bytes 393224 | tf_op jit(solution)/shard_map/ppermute | solution.py:306
  65.4 8.8 %collective-permute-start.20 = (bf16[256,256]{1,0:T(8,128)(2,1)S(1)}, bf16[256,256]{1,0:T(8,128)(2,1)S(1)}, u32[]{:S(2)}, u32[]{:S(2)}) collective-permute-start(bf16[256,256]{1,0:T(8,128)(2,1)S(1)} %get-tuple-element.48), channel_id=1, source_target_pairs={{0,6},{1,7},{2,0},{3,1},{4,2},{5,3},{6,4},{7,5},{8,14},{9,15},{10,... | collective-permute-start | bytes 393224 | tf_op jit(solution)/shard_map/ppermute | solution.py:306
  (10 other events, 39.1 us)

commit v2 on v1

v2 whole, which is shorter than its diff:
```python
import functools

import jax
import jax.numpy as jnp
from jax import lax
from jax.experimental import pallas as pl
from jax.experimental.pallas import tpu as pltpu
from jax.sharding import PartitionSpec as P

HEADS = 8
LATENT = 4
WL = 2
WA = 6
WO = 12
HALF = WO // 2
PIECE = WA * HALF
MARK = 2.0**40
PIECES = ((1, 1), (0, 1), (1, 0), (0, 0))
LSE_ROWS = 16
COTS = 5
FLOPS_PER_US = 3 * 10**9
MID_US = 4.0
MLP_US = 2.0
F32 = jnp.float32
BF16 = jnp.bfloat16
MIB = 1 << 20


def dot(a, b, contract=((1,), (0,))):
    return lax.dot_general(a, b, (contract, ((), ())), preferred_element_type=F32)


def body_name(body):
    while isinstance(body, functools.partial):
        body = body.func
    return body.__name__.removesuffix("_body")


def call(body, args, outs, scratch=(), vmem=16, after=None, hbm=False, us=0.2):
    count = len(args)
    after = () if after is None else after if isinstance(after, tuple) else (after,)
    args = (*args, *after)
    name = body_name(body)
    inner = body
    if after:
        body = lambda *refs: inner(*refs[:count], *refs[count + len(after) :])
    specs = [pl.BlockSpec(memory_space=pl.ANY if hbm else pltpu.VMEM)] * count
    specs += [pl.BlockSpec(memory_space=pl.ANY)] * len(after)
    return pl.pallas_call(
        body,
        out_shape=[jax.ShapeDtypeStruct(shape, dtype) for shape, dtype in outs],
        in_specs=specs,
        out_specs=[pl.BlockSpec(memory_space=pltpu.VMEM)] * len(outs),
        scratch_shapes=list(scratch),
        compiler_params=pltpu.CompilerParams(vmem_limit_bytes=vmem * MIB),
        name=name,
        cost_estimate=pl.CostEstimate(
            flops=int(us * FLOPS_PER_US), bytes_accessed=0, transcendentals=0
        ),
    )(*args)


def layer_norm(rows, gain):
    mean = jnp.mean(rows, -1, keepdims=True)
    centred = rows - mean
    spread = jnp.mean(centred * centred, -1, keepdims=True)
    return (centred * lax.rsqrt(spread + 1e-05) * gain).astype(BF16)


def gelu_parts(x):
    square = x * x
    t = jnp.tanh(x * (0.7978845608028654 + 0.7978845608028654 * 0.044715 * square))
    return square, t


def lat_rolled(cells):
    return pltpu.roll(cells, cells.shape[0] - WA // 2, 0)


def pack_levels_body(lev_count, mask_ref, lev_ref, own_ref, send_ref, blocks):
    count = lev_ref.shape[0]
    me = lax.axis_index("lev")
    for j in range(count):
        live = jnp.broadcast_to(mask_ref[:, j : j + 1] > 0, lev_ref.shape[2:])
        for o in range(WO):
            cells = lat_rolled(jnp.where(live, lev_ref[j, o].astype(F32), MARK))
            half, at = 1 - o // HALF, j * PIECE + (o % HALF) * WA
            for i in range(lev_count):
                blocks[half * lev_count + i, pl.ds(at, WA)] = cells[i * WA : (i + 1) * WA]
    rows = count * PIECE
    for k, (half, beside) in enumerate(PIECES):
        at = slice(k * rows, (k + 1) * rows)
        mine = me ^ (2 * beside)
        own_ref[at] = blocks[half * lev_count + mine].astype(BF16)
        send_ref[at] = blocks[half * lev_count + (mine ^ 1)].astype(BF16)


def pack_cot_body(lev_count, cot_ref, east_ref, west_ref, own_east_ref, own_west_ref, blocks):
    me = lax.axis_index("lev")
    rows = LATENT * PIECE
    for l in range(LATENT):
        for o in range(WO):
            cells = lat_rolled(cot_ref[(l + WL // 2) % LATENT, o].astype(F32))
            half, at = 1 - o // HALF, l * PIECE + (o % HALF) * WA
            for i in range(lev_count):
                blocks[half * lev_count + i, pl.ds(at, WA)] = cells[i * WA : (i + 1) * WA]
    for half, (ref, own_ref) in enumerate(((east_ref, own_east_ref), (west_ref, own_west_ref))):
        for slot in range(2):
            cells = blocks[half * lev_count + (me ^ (2 * slot))].astype(BF16)
            ref[slot * rows : (slot + 1) * rows] = cells
            if slot == 0:
                own_ref[...] = cells


def head_pick(lanes, step, first):
    head = lax.broadcasted_iota(jnp.int32, (2 * lanes, step), 1) // (step // HEADS) + first
    lane = lax.broadcasted_iota(jnp.int32, (2 * lanes, step), 0) % lanes
    return (head == lane).astype(BF16)


def two_parts(value):
    high = value.astype(BF16)
    return jnp.concatenate([high, (value - high.astype(F32)).astype(BF16)], 1)


def aggregate_body(k, own, recv, query_ref, w_key, w_value, out_ref, pool):
    width = w_key.shape[0]
    head_size = width // HEADS
    pairs = 2 * PIECE
    lanes = LATENT * HEADS
    owner = lax.broadcasted_iota(jnp.int32, (HEADS, width), 1) // head_size
    table = (owner == lax.broadcasted_iota(jnp.int32, (HEADS, width), 0)).astype(F32)
    query = query_ref[...].astype(F32)
    block_query = jnp.concatenate([table * query[l : l + 1] for l in range(LATENT)], 0)
    count = own.shape[0] // len(PIECES)
    at = slice(k * count, (k + 1) * count)
    rows = jnp.concatenate([own[at], recv[at]], 0)
    blocks = rows.shape[0] // pairs
    split = [slice(b * pairs, (b + 1) * pairs) for b in range(blocks)]
    keys = dot(rows, w_key[...]).astype(BF16)
    values = dot(rows, w_value[...]).astype(BF16).astype(F32)
    scores = dot(keys, block_query.astype(BF16), ((1,), (1,))) * head_size ** (-0.5)
    live = rows[:, :lanes].astype(F32) < MARK / 2
    scores = jnp.where(live, scores, -1e30)
    top = functools.reduce(jnp.maximum, [scores[at] for at in split])
    top = jnp.maximum(top, pltpu.roll(top, PIECE, 0))
    weights = [jnp.exp(scores[at] - top) * live[at].astype(F32) for at in split]
    total = functools.reduce(jnp.add, weights)
    total = total + pltpu.roll(total, PIECE, 0)
    inverse = 1.0 / total
    both = two_parts(jnp.concatenate([w * inverse for w in weights], 0))
    for l in range(LATENT):
        slot = (l - WL // 2) % LATENT
        prod = dot(both, head_pick(lanes, width, l * HEADS)) * values
        summed = functools.reduce(jnp.add, [prod[rows_at] for rows_at in split])
        summed = summed + pltpu.roll(summed, PIECE, 0)
        pool[pl.ds(slot * PIECE, PIECE)] = summed[:PIECE]
    rows = LATENT * PIECE
    out_ref[:rows] = pool[...].astype(BF16)
    lse = top + jnp.log(total)
    high = lse.astype(BF16).astype(F32)
    middle = (lse - high).astype(BF16).astype(F32)
    parts = jnp.concatenate([high, middle, lse - high - middle, jnp.zeros_like(lse)], 1)
    parts = [parts[g * LSE_ROWS : (g + 1) * LSE_ROWS] for g in range(3)]
    parts.append(jnp.zeros_like(parts[0]))
    out_ref[rows:] = jnp.concatenate(parts, 1).astype(BF16)


def combined(first, second, pool, left, right):
    rows = LATENT * PIECE
    lanes = LATENT * HEADS
    width = first.shape[1]
    lses = []
    for ref, rows_ref in ((first, left), (second, right)):
        rows_ref[...] = ref[:rows].astype(F32)
        parts = ref[rows:].astype(F32)
        group = 4 * lanes
        parts = jnp.concatenate([parts[:, g * group : (g + 1) * group] for g in range(3)], 0)
        lses.append(parts[:, :lanes] + parts[:, lanes : 2 * lanes] + parts[:, 2 * lanes : 3 * lanes])
    share = 1.0 / (1.0 + jnp.exp(lses[1] - lses[0]))
    both = two_parts(share)
    for l in range(LATENT):
        slot = (l - WL // 2) % LATENT
        at = pl.ds(slot * PIECE, PIECE)
        spread = dot(both, head_pick(lanes, width, l * HEADS))[:PIECE]
        pool[at] = spread * left[at] + (1.0 - spread) * right[at]
    return pool[...].astype(BF16)


def combine_body(first, second, out_ref, pool, left, right):
    out_ref[...] = combined(first, second, pool, left, right)


def window_attention(lev_count, latent, gain, w_qkv):
    width = latent.shape[1]
    head_size = width // HEADS
    half = LATENT * PIECE
    slab = WL * PIECE
    size = 2 * slab
    normed = layer_norm(latent.astype(F32), gain[...])
    qkv = dot(normed, w_qkv[...])
    last = lax.axis_index("lev") == lev_count - 1
    shape = (2 * size, size)
    q_at = lax.rem(lax.broadcasted_iota(jnp.int32, shape, 0), slab)
    k_at = lax.rem(lax.broadcasted_iota(jnp.int32, shape, 1), slab)
    q_lat = lax.rem(q_at, WA) >= WA // 2
    k_lat = lax.rem(k_at, WA) >= WA // 2
    lat_differs = jnp.where(last, (q_lat != k_lat).astype(F32), 0.0)
    lev_differs = ((q_at >= PIECE) != (k_at >= PIECE)).astype(F32)
    lane = lax.broadcasted_iota(jnp.int32, (size, 2 * head_size), 1) < head_size
    mixed = []
    for lb in range(LATENT // WL):
        rows = jnp.concatenate(
            [qkv[lb * slab : (lb + 1) * slab], qkv[half + lb * slab : half + (lb + 1) * slab]], 0
        )
        differs = lat_differs + lev_differs if lb == LATENT // WL - 1 else lat_differs
        allowed = differs == 0.0
        outs = []
        for p in range(HEADS // 2):
            at = 2 * p * head_size
            query = rows[:, at : at + 2 * head_size]
            key = rows[:, width + at : width + at + 2 * head_size].astype(BF16)
            value = rows[:, 2 * width + at : 2 * width + at + 2 * head_size].astype(BF16)
            query = jnp.concatenate([jnp.where(lane, query, 0.0), jnp.where(lane, 0.0, query)], 0)
            scores = dot(query.astype(BF16), key, ((1,), (1,))) * head_size ** (-0.5)
            scores = jnp.where(allowed, scores, -1e30)
            weights = jnp.exp(scores - jnp.max(scores, -1, keepdims=True))
            probs = weights * (1.0 / jnp.sum(weights, -1, keepdims=True))
            out = dot(probs.astype(BF16), value)
            outs.append(jnp.where(lane, out[:size], out[size:]))
        mixed.append(jnp.concatenate(outs, 1))
    mixed = [m[:slab] for m in mixed] + [m[slab:] for m in mixed]
    return jnp.concatenate(mixed, 0).astype(BF16)


def window_body(
    lev_count,
    east_own,
    east_beside,
    west,
    w_agg_out,
    gain_attn,
    w_qkv,
    w_proj,
    resid_ref,
    pool,
    left,
    right,
):
    pooled = [combined(east_own, east_beside, pool, left, right), west[...]]
    latent = dot(jnp.concatenate(pooled, 0), w_agg_out[...]).astype(BF16)
    mixed = window_attention(lev_count, latent, gain_attn, w_qkv)
    resid = (latent.astype(F32) + dot(mixed, w_proj[...])).astype(BF16)
    resid_ref[...] = resid


def mlp_body(resid, gain_mlp, w_up, w_down, east_ref, west_ref):
    step = 512
    half = resid.shape[0] // 2
    total = resid[...].astype(F32)
    rows = layer_norm(total, gain_mlp[...])
    for n in range(w_up.shape[1] // step):
        inner = dot(rows, w_up[:, n * step : (n + 1) * step])
        _, t = gelu_parts(inner)
        active = (inner * (0.5 * (1.0 + t))).astype(BF16)
        total = total + dot(active, w_down[n * step : (n + 1) * step])
    total = total.astype(BF16)
    east_ref[...] = total[:half]
    west_ref[...] = total[half:]


def grad_body(chunks, cot_at, adds, last, part, *refs):
    resid = refs[:chunks]
    count = COTS if adds else 2
    cots = refs[chunks : chunks + count]
    gain, w_up, w_down = refs[chunks + count : chunks + count + 3]
    rest = refs[chunks + count + 3 :]
    normed, n_half, c_half = rest[-3:]
    if adds:
        (sum_up, sum_dn), rest = rest[:2], rest[2:]
    if last:
        (send, keep), rest = rest[:2], rest[2:]
    acc_up, acc_dn = rest[:2]
    me = lax.axis_index("lev")
    model, cols = acc_up.shape
    half_at = pl.ds(pl.multiple_of((me // 2) * model, model), model)
    piece = LATENT * PIECE
    rows = [ref[...] for ref in resid]
    backs = []
    for k, (which, slot) in enumerate(cot_at):
        at = slice(slot * piece, (slot + 1) * piece)
        to = slice(k * piece, (k + 1) * piece)
        backs.append(cots[which][at])
        c_half[to] = cots[which][at, half_at]
    rows = layer_norm(jnp.concatenate(rows, 0).astype(F32), gain[...])
    backs = jnp.concatenate(backs, 0)
    normed[...] = rows
    n_half[...] = normed[:, half_at]
    n_half_v = n_half[...]
    c_half_v = c_half[...]
    picked = w_up.shape[1] != cols
    step = part if picked else 256
    parity = lax.rem(lax.axis_index("tile"), 2)
    for n in range(cols // step):
        at = slice(n * step, (n + 1) * step)
        take = pl.ds(pl.multiple_of((2 * n + parity) * step, step), step) if picked else at
        x = dot(rows, w_up[:, take])
        back = dot(backs, w_down[take], ((1,), (1,)))
        square, t = gelu_parts(x)
        cdf = 0.5 + 0.5 * t
        active = (x * cdf).astype(BF16)
        slope = (0.5 * 0.7978845608028654) + (1.5 * 0.7978845608028654 * 0.044715) * square
        dinner = (back * (cdf + x * ((1.0 - t * t) * slope))).astype(BF16)
        up = dot(n_half_v, dinner, ((0,), (0,)))
        dn = dot(c_half_v, active, ((0,), (0,)))
        acc_up[:, at] = up + sum_up[:, at] if adds else up
        acc_dn[:, at] = dn + sum_dn[:, at] if adds else dn
    if last:
        quarter = model // 2
        core = lax.rem(me, 2)
        mine = pl.ds(pl.multiple_of(core * quarter, quarter), quarter)
        other = pl.ds(pl.multiple_of((1 - core) * quarter, quarter), quarter)
        keep[:quarter] = acc_up[mine]
        keep[quarter:] = acc_dn[mine]
        send[:quarter] = acc_up[other].astype(BF16)
        send[quarter:] = acc_dn[other].astype(BF16)


def split_body(groups, keep, recv, own_ref, *refs):
    outs, blocks = refs[:-1], refs[-1]
    cols = keep.shape[1] // groups
    for n in range(groups):
        at = slice(n * cols, (n + 1) * cols)
        blocks[n] = keep[:, at] + recv[:, at].astype(F32)
    me = lax.axis_index("tile") // 2
    own_ref[...] = blocks[me]
    for d in range(1, groups):
        outs[d - 1][...] = blocks[lax.rem(me + d, groups)].astype(BF16)


def total_body(own, *refs):
    received, (up_ref, dn_ref) = refs[:-2], refs[-2:]
    total = own[...]
    for part in received:
        total = total + part[...].astype(F32)
    half = total.shape[0] // 2
    up_ref[...] = total[:half]
    dn_ref[...] = total[half:]


def join_body(first, second, out_ref):
    half = first.shape[0]
    out_ref[:half] = first[...]
    out_ref[half:] = second[...]


def join_all_body(own_e, beside_e, west, east_ref, joined_ref):
    join_body(own_e, beside_e, east_ref)
    half = east_ref.shape[0]
    joined_ref[:half] = east_ref[...]
    joined_ref[half:] = west[...]


def hand_on_body(first, second, other, joined_ref, other_ref):
    join_body(first, second, joined_ref)
    other_ref[...] = other[...]


def unpack_body(east, west, core, out_ref, mark_ref, blocks):
    mark_ref[...] = jnp.zeros_like(mark_ref)
    me = lax.axis_index("lev")
    half = LATENT * PIECE
    for d in range(2):
        at = slice(d * half, (d + 1) * half)
        then = slice((d + 2) * half, (d + 3) * half)
        blocks[me ^ (2 * d), :half] = east[at].astype(F32)
        blocks[me ^ (2 * d), half:] = west[at].astype(F32)
        blocks[me ^ (2 * d) ^ 1, :half] = core[at].astype(F32)
        blocks[me ^ (2 * d) ^ 1, half:] = core[then].astype(F32)
    for l in range(LATENT):
        for o in range(WO):
            at = (half if o < HALF else 0) + l * PIECE + (o % HALF) * WA
            cells = jnp.concatenate(
                [blocks[i, pl.ds(at, WA)] for i in range(blocks.shape[0])], 0
            )
            cells = pltpu.roll(cells, WA // 2, 0)
            out_ref[(l + WL // 2) % LATENT, o] = cells.astype(BF16)


def exchanged(block, lev_step, tile_move):
    levs, tiles = lax.axis_size("lev"), lax.axis_size("tile")
    route = [
        (l * tiles + t, (l ^ lev_step) * tiles + tile_move(t)) for l in range(levs) for t in range(tiles)
    ]
    return lax.ppermute(block, ("lev", "tile"), route)


def per_device(
    levels,
    level_mask,
    w_key,
    w_value,
    latent_query,
    w_agg_out,
    gain_attn,
    w_qkv,
    w_proj,
    gain_mlp,
    w_up,
    w_down,
    cotangent,
):
    levs, tiles = lax.axis_size("lev"), lax.axis_size("tile")
    count, lat, lon, width = levels.shape
    hidden = w_up.shape[1]
    assert lat == levs * WA and lon == WO and levs == 4 and tiles % 2 == 0
    piece = count * PIECE
    rows = LATENT * PIECE
    window = 2 * rows
    groups = tiles // 2
    part = hidden // tiles
    quarter = width // levs

    west = lambda t: (t - 1) % tiles
    east = lambda t: (t + 1) % tiles
    same = lambda t: t
    peer = lambda t: t ^ 1
    next_pair = lambda t: (t - 2) % tiles if t % 2 == 0 else t

    cot_east, cot_west, cot_east_own, cot_west_own = call(
        functools.partial(pack_cot_body, levs),
        (cotangent.transpose(0, 2, 1, 3),),
        [((window, width), BF16)] * 2 + [((rows, width), BF16)] * 2,
        [pltpu.VMEM((2 * levs, rows, width), F32)],
        us=0.5,
    )
    cot_peer_e = exchanged(cot_east_own, 0, peer)
    cot_own_w = exchanged(cot_west_own, 0, west)
    own_raw, send_raw = call(
        functools.partial(pack_levels_body, levs),
        (level_mask[None], levels.transpose(0, 2, 1, 3)),
        [((len(PIECES) * piece, width), BF16)] * 2,
        [pltpu.VMEM((2 * levs, piece, width), F32)],
        after=cot_east,
        us=0.7,
    )
    recv_raw = exchanged(send_raw, 1, same)
    weights = (latent_query, w_key, w_value)
    aggregated = lambda k, after: call(
        functools.partial(aggregate_body, k),
        (own_raw, recv_raw, *weights),
        [((rows + LSE_ROWS, width), BF16)],
        [pltpu.VMEM((rows, width), F32)],
        after=after,
        us=1.3,
    )[0]
    pooled = [aggregated(0, None)]
    west_beside = exchanged(pooled[0], 2, same)
    pooled.append(aggregated(1, pooled[0]))
    east_beside = exchanged(pooled[1], 2, same)
    pooled.append(aggregated(2, pooled[1]))
    pooled_w = call(
        combine_body,
        (pooled[2], west_beside),
        [((rows, width), BF16)],
        [pltpu.VMEM((rows, width), F32)] * 3,
        us=0.4,
    )[0]
    pooled.append(aggregated(3, pooled_w))
    pooled_w = exchanged(pooled_w, 0, west)
    cot_joined, cot_west = call(
        hand_on_body,
        (cot_own_w, cot_peer_e, cot_west),
        [((window, width), BF16)] * 2,
        vmem=8,
        after=pooled[3],
    )
    cot_peer_w = exchanged(cot_west, 0, next_pair)
    cots = (cot_east, cot_own_w, cot_peer_e, cot_peer_w, exchanged(cot_joined, 2, same))

    resid = call(
        functools.partial(window_body, levs),
        (
            pooled[3],
            east_beside,
            pooled_w,
            w_agg_out,
            gain_attn[None],
            w_qkv,
            w_proj,
        ),
        [((window, width), BF16)],
        [pltpu.VMEM((rows, width), F32)] * 3,
        vmem=24,
        after=cot_joined,
        us=3.0,
    )[0]
    beside = exchanged(resid, 2, same)
    across = exchanged(resid, 0, peer)
    far = [exchanged(beside[:rows], 0, peer), exchanged(across[rows:], 2, same)]

    gain_mlp = gain_mlp[None]
    mlp = lambda pieces, after: call(
        mlp_body,
        (pieces, gain_mlp, w_up, w_down),
        [((rows, width), BF16)] * 2,
        vmem=20,
        after=after,
        us=MLP_US,
    )
    up_part, down_part = w_up, w_down
    if part % 128:
        parity = lax.rem(lax.axis_index("tile"), 2)
        up_part = lax.dynamic_index_in_dim(
            w_up.reshape(width, groups, 2, part), parity, 2, keepdims=False
        ).reshape(width, groups * part)
        down_part = lax.dynamic_index_in_dim(
            w_down.reshape(groups, 2, part, width), parity, 1, keepdims=False
        ).reshape(groups * part, width)
    sums = [((2 * quarter, hidden // 2), F32)] * 2
    scratch = lambda n: [pltpu.VMEM((n * rows, width), BF16)] + [
        pltpu.VMEM((n * rows, 2 * quarter), BF16)
    ] * 2
    own_at, far_at = ((0, 0), (1, 0)), ((4, 1), (3, 1))
    middle_at = ((0, 1), (4, 0), (2, 0), (3, 0))
    own_e, own_w = mlp(resid, cots[:2])
    so_far = call(
        functools.partial(grad_body, 1, own_at, False, False, part),
        (resid, *cots[:2], gain_mlp, up_part, down_part),
        sums,
        scratch(2),
        vmem=24,
        after=own_e,
        us=2.2,
    )
    beside_e, beside_w = mlp(beside, (so_far[0], *cots[3:]))
    out_w = exchanged(
        call(join_body, (own_w, beside_w), [((window, width), BF16)], vmem=8)[0], 0, east
    )
    so_far = call(
        functools.partial(grad_body, 2, middle_at, True, False, part),
        (beside, across, *cots, gain_mlp, up_part, down_part, *so_far),
        sums,
        scratch(4),
        vmem=24,
        after=beside_e,
        us=MID_US,
    )
    out_e, chip_rows = call(
        join_all_body,
        (own_e, beside_e, out_w),
        [((window, width), BF16), ((2 * window, width), BF16)],
        vmem=8,
        after=so_far[0],
    )
    send, keep = call(
        functools.partial(grad_body, 2, far_at, True, True, part),
        (*far, *cots, gain_mlp, up_part, down_part, *so_far),
        [((2 * quarter, hidden // 2), BF16), ((2 * quarter, hidden // 2), F32)],
        [pltpu.VMEM((2 * quarter, hidden // 2), F32)] * 2 + scratch(2),
        vmem=24,
        after=chip_rows,
        us=2.6,
    )
    recv = exchanged(send, 1, same)
    own, *sends = call(
        functools.partial(split_body, groups),
        (keep, recv),
        [((2 * quarter, part), F32)] + [((2 * quarter, part), BF16)] * (groups - 1),
        [pltpu.VMEM((groups, 2 * quarter, part), F32)],
        vmem=32,
    )
    received = [
        exchanged(block, 0, lambda t, d=d: (t + 2 * d) % tiles) for d, block in enumerate(sends, 1)
    ]
    core_rows = exchanged(chip_rows, 1, same)
    encoded, mark = call(
        unpack_body,
        (out_e, out_w, core_rows),
        [((LATENT, lon, lat, width), BF16), ((8, 128), F32)],
        [pltpu.VMEM((levs, window, width), F32)],
        vmem=24, us=1.6
    )
    grad_up, grad_down_t = call(
        total_body, (own, *received), [((quarter, part), F32)] * 2, after=mark, us=0.7
    )
    return (encoded.transpose(0, 2, 1, 3), grad_up, grad_down_t)


def solution(mesh):
    return jax.shard_map(
        per_device,
        mesh=mesh,
        in_specs=(
            P("lev", None, "tile", None),
            P("lev"),
            P(),
            P(),
            P(),
            P(),
            P(),
            P(),
            P(),
            P(),
            P(),
            P(),
            P(None, None, "tile", None),
        ),
        out_specs=(P(None, None, "tile", None), P("lev", "tile"), P("lev", "tile")),
        check_vma=False,
    )
```

time: 75.1 us -> 70.8 us (0.943)
  starting transfers between devices: 32.4 us -> 26.1 us
  Pallas kernels: 19.9 us -> 25.2 us
  waiting for transfers between devices: 19.7 us -> 16.3 us
    ppermute x21 -> x18, starting transfers between devices: 32.4 us -> 26.1 us  [exchanged(): return lax.ppermute(block, ('lev', 'tile'), route)]
    pallas_call x11 -> x19, Pallas kernels: 19.9 us -> 25.2 us  [call(): pl.pallas_call(body, out_shape=[jax.ShapeDtypeStruct(shape, dtype) for sh...]
    ppermute x21 -> x18, waiting for transfers between devices: 19.7 us -> 16.3 us  [exchanged(): return lax.ppermute(block, ('lev', 'tile'), route)]
    unnamed x27 -> x26, local copies, waits for them, and re-layouts: 1.99 us -> 2.08 us
  transfers between devices with their start and end apart: 21 -> 18, of which waited for: 9 -> 7; matrix products, arithmetic and copies ran while one was open for 0% -> 0% of each run, Pallas kernels for 25% -> 33%
where the time goes in v2:
time: 70.8 us; the launch traced here: 70.6 us
  starting transfers between devices  26.1 us (37%)
  Pallas kernels  25.2 us (36%)
  waiting for transfers between devices  16.3 us (23%)
  local copies, waits for them, and re-layouts  2.11 us (3%)
  between operations  0.92 us (1%)
    ppermute x18, starting transfers between devices, exchanged(): return lax.ppermute(block, ('lev', 'tile'), route)  26.1 us
    pallas_call x19, Pallas kernels, call(): pl.pallas_call(body, out_shape=[jax.ShapeDtypeStruct(shape, dtype) for sh...  25.2 us
    ppermute x18, waiting for transfers between devices, exchanged(): return lax.ppermute(block, ('lev', 'tile'), route)  16.3 us
    unnamed x26, local copies, waits for them, and re-layouts  2.08 us
  transfers between devices with their start and end apart: 18, of which 7 were waited for; matrix products, arithmetic and copies ran while one was open for 0% of the time, Pallas kernels for 33%

profile of v2, /device:TPU:0, one launch (start us, length us, event | category | flops | bytes accessed | tf_op | source)
XLA Modules:
  0.0 70.6 jit_solution(13360348754163629016)
XLA Ops:
  4.4 5.6 %collective-permute-start.4 = (bf16[144,512]{1,0:T(8,128)(2,1)S(1)}, bf16[144,512]{1,0:T(8,128)(2,1)S(1)}, u32[]{:S(2)}, u32[]{:S(2)}) collective-permute-start(bf16[144,512]{1,0:T(8,128)(2,1)S(1)} %get-tuple-element.34), channel_id=1, source_target_pairs={{0,7},{1,0},{2,1},{3,2},{4,3},{5,4},{6,5},{7,6},{8,15},{9,8},{10,9... | collective-permute-start | bytes 442376 | tf_op jit(solution)/shard_map/ppermute | solution.py:395
  10.0 1.3 %aggregate.4.refs_5_ = bf16[160,512]{1,0:T(8,128)(2,1)S(1)} custom-call(bf16[576,512]{1,0:T(8,128)(2,1)S(1)} %get-tuple-element.32.own.refs_0_, bf16[576,512]{1,0:T(8,128)(2,1)S(1)} %collective-permute-done.recv.refs_1_, bf16[4,512]{1,0:T(4,128)(2,1)S(1)} %copy-done.9, bf16[512,512]{1,0:T(8,128)(2,1)S(1)} %copy-done.5, bf16[512,512]{1,0:T(8,128)(2,1)S(1)} %copy-done.6), custom_call_target="tpu_custom_call" | custom-call | flops 3900000000 | tf_op jit(solution)/shard_map/aggregate/pallas_call | solution.py:49
  11.3 1.6 %collective-permute-start.1 = (bf16[160,512]{1,0:T(8,128)(2,1)S(1)}, bf16[160,512]{1,0:T(8,128)(2,1)S(1)}, u32[]{:S(2)}, u32[]{:S(2)}) collective-permute-start(bf16[160,512]{1,0:T(8,128)(2,1)S(1)} %aggregate.4.refs_5_), channel_id=1, source_target_pairs={{0,16},{1,17},{2,18},{3,19},{4,20},{5,21},{6,22},{7,23},{8,24},{9,... | collective-permute-start | bytes 491528 | tf_op jit(solution)/shard_map/ppermute | solution.py:395
  16.0 2.4 %collective-permute-done.1.second = bf16[160,512]{1,0:T(8,128)(2,1)S(1)} collective-permute-done((bf16[160,512]{1,0:T(8,128)(2,1)S(1)}, bf16[160,512]{1,0:T(8,128)(2,1)S(1)}, u32[]{:S(2)}, u32[]{:S(2)}) %collective-permute-start.1) | collective-permute-done | bytes 163872 | tf_op jit(solution)/shard_map/ppermute | solution.py:395
  18.8 2.0 %collective-permute-start.3 = (bf16[144,512]{1,0:T(8,128)(2,1)S(1)}, bf16[144,512]{1,0:T(8,128)(2,1)S(1)}, u32[]{:S(2)}, u32[]{:S(2)}) collective-permute-start(bf16[144,512]{1,0:T(8,128)(2,1)S(1)} %combine.1.refs_5_), channel_id=1, source_target_pairs={{0,7},{1,0},{2,1},{3,2},{4,3},{5,4},{6,5},{7,6},{8,15},{9,8},{10,9... | collective-permute-start | bytes 442376 | tf_op jit(solution)/shard_map/ppermute | solution.py:395
  22.1 2.7 %collective-permute-start.7 = (bf16[288,512]{1,0:T(8,128)(2,1)S(1)}, bf16[288,512]{1,0:T(8,128)(2,1)S(1)}, u32[]{:S(2)}, u32[]{:S(2)}) collective-permute-start(bf16[288,512]{1,0:T(8,128)(2,1)S(1)} %get-tuple-element.40), channel_id=1, source_target_pairs={{0,6},{1,1},{2,0},{3,3},{4,2},{5,5},{6,4},{7,7},{8,14},{9,9},{10,8... | collective-permute-start | bytes 884744 | tf_op jit(solution)/shard_map/ppermute | solution.py:395
  24.8 1.6 %collective-permute-start.8 = (bf16[288,512]{1,0:T(8,128)(2,1)S(1)}, bf16[288,512]{1,0:T(8,128)(2,1)S(1)}, u32[]{:S(2)}, u32[]{:S(2)}) collective-permute-start(bf16[288,512]{1,0:T(8,128)(2,1)S(1)} %get-tuple-element.37.refs_7_), channel_id=1, source_target_pairs={{0,16},{1,17},{2,18},{3,19},{4,20},{5,21},{6,22},{7,23},{8,24},{9,... | collective-permute-start | bytes 884744 | tf_op jit(solution)/shard_map/ppermute | solution.py:395
  26.5 2.9 %window.1.refs_0_ = bf16[288,512]{1,0:T(8,128)(2,1)S(1)} custom-call(bf16[160,512]{1,0:T(8,128)(2,1)S(1)} %aggregate.7.refs_3_.refs_0_, bf16[160,512]{1,0:T(8,128)(2,1)S(1)} %collective-permute-done.2.refs_1_, bf16[144,512]{1,0:T(8,128)(2,1)S(1)} %collective-permute-done.3.refs_2_, bf16[512,512]{1,0:T(8,128)(2,1)S(1)} %copy-done.7, f32[1,512]{1,0:T(1,128)S(1)} %bitcast.8, ...), custom_call_target="tpu_custom_call" | custom-call | flops 8999999488 | tf_op jit(solution)/shard_map/window/pallas_call | solution.py:49
  29.9 2.0 %collective-permute-start.10 = (bf16[288,512]{1,0:T(8,128)(2,1)S(1)}, bf16[288,512]{1,0:T(8,128)(2,1)S(1)}, u32[]{:S(2)}, u32[]{:S(2)}) collective-permute-start(bf16[288,512]{1,0:T(8,128)(2,1)S(1)} %window.1.refs_0_), channel_id=1, source_target_pairs={{0,1},{1,0},{2,3},{3,2},{4,5},{5,4},{6,7},{7,6},{8,9},{9,8},{10,11... | collective-permute-start | bytes 884744 | tf_op jit(solution)/shard_map/ppermute | solution.py:395
  32.0 2.2 %mlp.2 = (bf16[144,512]{1,0:T(8,128)(2,1)S(1)}, bf16[144,512]{1,0:T(8,128)(2,1)S(1)}) custom-call(bf16[288,512]{1,0:T(8,128)(2,1)S(1)} %window.1.refs_0_, f32[1,512]{1,0:T(1,128)S(1)} %bitcast.9, bf16[512,2048]{1,0:T(8,128)(2,1)S(1)} %copy-done, bf16[2048,512]{1,0:T(8,128)(2,1)S(1)} %copy-done.1, ...), custom_call_target="tpu_custom_call" | custom-call | flops 6000000000 | tf_op jit(solution)/shard_map/mlp/pallas_call | solution.py:49
  34.1 2.4 %grad.3 = (f32[256,1024]{1,0:T(8,128)S(1)}, f32[256,1024]{1,0:T(8,128)S(1)}) custom-call(bf16[288,512]{1,0:T(8,128)(2,1)S(1)} %window.1.refs_0_, bf16[288,512]{1,0:T(8,128)(2,1)S(1)} %get-tuple-element.31.refs_2_.refs_4_.refs_1_, bf16[144,512]{1,0:T(8,128)(2,1)S(1)} %collective-permute-done.4.refs_0_.refs_5_.refs_2_.refs_3_, f32[1,512]{1,0:T(1,128)S(1)} %bitcast.10, ...), custom_call_target="tpu_custom_call" | custom-call | flops 6600000000 | tf_op jit(solution)/shard_map/grad/pallas_call | solution.py:49
  36.6 1.5 %collective-permute-done.6.refs_0_ = bf16[288,512]{1,0:T(8,128)(2,1)S(1)} collective-permute-done((bf16[288,512]{1,0:T(8,128)(2,1)S(1)}, bf16[288,512]{1,0:T(8,128)(2,1)S(1)}, u32[]{:S(2)}, u32[]{:S(2)}) %collective-permute-start.6) | collective-permute-done | bytes 294944 | tf_op jit(solution)/shard_map/ppermute | solution.py:395
  38.0 2.2 %mlp.3 = (bf16[144,512]{1,0:T(8,128)(2,1)S(1)}, bf16[144,512]{1,0:T(8,128)(2,1)S(1)}) custom-call(bf16[288,512]{1,0:T(8,128)(2,1)S(1)} %collective-permute-done.6.refs_0_, f32[1,512]{1,0:T(1,128)S(1)} %bitcast.11, bf16[512,2048]{1,0:T(8,128)(2,1)S(1)} %copy-done, bf16[2048,512]{1,0:T(8,128)(2,1)S(1)} %copy-done.1, ...), custom_call_target="tpu_custom_call" | custom-call | flops 6000000000 | tf_op jit(solution)/shard_map/mlp/pallas_call | solution.py:49
  40.5 3.1 %collective-permute-start.12 = (bf16[144,512]{1,0:T(8,128)(2,1)S(1)}, bf16[144,512]{1,0:T(8,128)(2,1)S(1)}, u32[]{:S(2)}, u32[]{:S(2)}) collective-permute-start(bf16[144,512]{1,0:T(8,128)(2,1)S(1)} %slice.8), channel_id=1, source_target_pairs={{0,1},{1,0},{2,3},{3,2},{4,5},{5,4},{6,7},{7,6},{8,9},{9,8},{10,11... | collective-permute-start | bytes 442376 | tf_op jit(solution)/shard_map/ppermute | solution.py:395
  43.6 1.6 %collective-permute-start.13 = (bf16[144,512]{1,0:T(8,128)(2,1)S(1)}, bf16[144,512]{1,0:T(8,128)(2,1)S(1)}, u32[]{:S(2)}, u32[]{:S(2)}) collective-permute-start(bf16[144,512]{1,0:T(8,128)(2,1)S(1)} %slice.9), channel_id=1, source_target_pairs={{0,16},{1,17},{2,18},{3,19},{4,20},{5,21},{6,22},{7,23},{8,24},{9,... | collective-permute-start | bytes 442376 | tf_op jit(solution)/shard_map/ppermute | solution.py:395
  45.2 3.6 %grad.4 = (f32[256,1024]{1,0:T(8,128)S(1)}, f32[256,1024]{1,0:T(8,128)S(1)}) custom-call(bf16[288,512]{1,0:T(8,128)(2,1)S(1)} %collective-permute-done.6.refs_0_, bf16[288,512]{1,0:T(8,128)(2,1)S(1)} %collective-permute-done.10.refs_1_, bf16[288,512]{1,0:T(8,128)(2,1)S(1)} %get-tuple-element.31.refs_2_.refs_4_.refs_1_, ...), custom_call_target="tpu_custom_call" | custom-call | flops 12000000000 | tf_op jit(solution)/shard_map/grad/pallas_call | solution.py:49
  48.8 1.5 %collective-permute-done.9.refs_2_.west = bf16[288,512]{1,0:T(8,128)(2,1)S(1)} collective-permute-done((bf16[288,512]{1,0:T(8,128)(2,1)S(1)}, bf16[288,512]{1,0:T(8,128)(2,1)S(1)}, u32[]{:S(2)}, u32[]{:S(2)}) %collective-permute-start.9) | collective-permute-done | bytes 294944 | tf_op jit(solution)/shard_map/ppermute | solution.py:395
  50.5 1.3 %collective-permute-done.12.refs_0_ = bf16[144,512]{1,0:T(8,128)(2,1)S(1)} collective-permute-done((bf16[144,512]{1,0:T(8,128)(2,1)S(1)}, bf16[144,512]{1,0:T(8,128)(2,1)S(1)}, u32[]{:S(2)}, u32[]{:S(2)}) %collective-permute-start.12) | collective-permute-done | bytes 147488 | tf_op jit(solution)/shard_map/ppermute | solution.py:395
  51.8 2.7 %grad.5 = (bf16[256,1024]{1,0:T(8,128)(2,1)S(1)}, f32[256,1024]{1,0:T(8,128)S(1)}) custom-call(bf16[144,512]{1,0:T(8,128)(2,1)S(1)} %collective-permute-done.12.refs_0_, bf16[144,512]{1,0:T(8,128)(2,1)S(1)} %collective-permute-done.13.refs_1_, bf16[288,512]{1,0:T(8,128)(2,1)S(1)} %get-tuple-element.31.refs_2_.refs_4_.refs_1_, ...), custom_call_target="tpu_custom_call" | custom-call | flops 7800000000 | tf_op jit(solution)/shard_map/grad/pallas_call | solution.py:49
  54.6 1.9 %collective-permute-done.14.recv = bf16[256,1024]{1,0:T(8,128)(2,1)S(1)} collective-permute-done((bf16[256,1024]{1,0:T(8,128)(2,1)S(1)}, bf16[256,1024]{1,0:T(8,128)(2,1)S(1)}, u32[]{:S(2)}, u32[]{:S(2)}) %collective-permute-start.14) | collective-permute-done | bytes 524320 | tf_op jit(solution)/shard_map/ppermute | solution.py:395
  57.8 2.8 %collective-permute-start.17 = (bf16[256,256]{1,0:T(8,128)(2,1)S(1)}, bf16[256,256]{1,0:T(8,128)(2,1)S(1)}, u32[]{:S(2)}, u32[]{:S(2)}) collective-permute-start(bf16[256,256]{1,0:T(8,128)(2,1)S(1)} %get-tuple-element.55), channel_id=1, source_target_pairs={{0,6},{1,7},{2,0},{3,1},{4,2},{5,3},{6,4},{7,5},{8,14},{9,15},{10,... | collective-permute-start | bytes 393224 | tf_op jit(solution)/shard_map/ppermute | solution.py:395
  60.7 1.6 %unpack.1 = (bf16[4,12,24,512]{3,2,1,0:T(8,128)(2,1)}, f32[8,128]{1,0:T(8,128)S(1)}) custom-call(bf16[288,512]{1,0:T(8,128)(2,1)S(1)} %get-tuple-element.46.east, bf16[288,512]{1,0:T(8,128)(2,1)S(1)} %collective-permute-done.9.refs_2_.west, bf16[576,512]{1,0:T(8,128)(2,1)S(1)} %collective-permute-done.11.core), custom_call_target="tpu_custom_call" | custom-call | flops 4800000000 | tf_op jit(solution)/shard_map/unpack/pallas_call | solution.py:49
  62.3 2.8 %collective-permute-done.15.refs_1_ = bf16[256,256]{1,0:T(8,128)(2,1)S(1)} collective-permute-done((bf16[256,256]{1,0:T(8,128)(2,1)S(1)}, bf16[256,256]{1,0:T(8,128)(2,1)S(1)}, u32[]{:S(2)}, u32[]{:S(2)}) %collective-permute-start.15) | collective-permute-done | bytes 131104 | tf_op jit(solution)/shard_map/ppermute | solution.py:395
  65.0 4.8 %collective-permute-done.16.refs_2_ = bf16[256,256]{1,0:T(8,128)(2,1)S(1)} collective-permute-done((bf16[256,256]{1,0:T(8,128)(2,1)S(1)}, bf16[256,256]{1,0:T(8,128)(2,1)S(1)}, u32[]{:S(2)}, u32[]{:S(2)}) %collective-permute-start.16) | collective-permute-done | bytes 131104 | tf_op jit(solution)/shard_map/ppermute | solution.py:395
  (59 shorter events, 11.7 us)
Async XLA Ops:
  3.2 6.8 %copy-start.5 = (bf16[512,512]{1,0:T(8,128)(2,1)S(1)}, bf16[512,512]{1,0:T(8,128)(2,1)}, u32[]{:S(2)}) copy-start(bf16[512,512]{1,0:T(8,128)(2,1)} %refs_3_.8) | copy-start | bytes 1572868
  3.2 6.8 %copy-start.6 = (bf16[512,512]{1,0:T(8,128)(2,1)S(1)}, bf16[512,512]{1,0:T(8,128)(2,1)}, u32[]{:S(2)}) copy-start(bf16[512,512]{1,0:T(8,128)(2,1)} %refs_4_.6) | copy-start | bytes 1572868
  3.2 6.8 %copy-start.9 = (bf16[4,512]{1,0:T(4,128)(2,1)S(1)}, bf16[4,512]{1,0:T(4,128)(2,1)}, u32[]{:S(2)}) copy-start(bf16[4,512]{1,0:T(4,128)(2,1)} %refs_2_.7) | copy-start | bytes 12292
  3.9 6.1 %collective-permute-start = (bf16[576,512]{1,0:T(8,128)(2,1)S(1)}, bf16[576,512]{1,0:T(8,128)(2,1)S(1)}, u32[]{:S(2)}, u32[]{:S(2)}) collective-permute-start(bf16[576,512]{1,0:T(8,128)(2,1)S(1)} %get-tuple-element.33), channel_id=1, source_target_pairs={{0,8},{1,9},{2,10},{3,11},{4,12},{5,13},{6,14},{7,15},{8,0},{9,1},... | collective-permute-start | bytes 1769480 | tf_op jit(solution)/shard_map/ppermute | solution.py:395
  4.4 17.6 %collective-permute-start.4 = (bf16[144,512]{1,0:T(8,128)(2,1)S(1)}, bf16[144,512]{1,0:T(8,128)(2,1)S(1)}, u32[]{:S(2)}, u32[]{:S(2)}) collective-permute-start(bf16[144,512]{1,0:T(8,128)(2,1)S(1)} %get-tuple-element.34), channel_id=1, source_target_pairs={{0,7},{1,0},{2,1},{3,2},{4,3},{5,4},{6,5},{7,6},{8,15},{9,8},{10,9... | collective-permute-start | bytes 442376 | tf_op jit(solution)/shard_map/ppermute | solution.py:395
  10.0 12.1 %collective-permute-start.5 = (bf16[144,512]{1,0:T(8,128)(2,1)S(1)}, bf16[144,512]{1,0:T(8,128)(2,1)S(1)}, u32[]{:S(2)}, u32[]{:S(2)}) collective-permute-start(bf16[144,512]{1,0:T(8,128)(2,1)S(1)} %get-tuple-element.35), channel_id=1, source_target_pairs={{0,1},{1,0},{2,3},{3,2},{4,5},{5,4},{6,7},{7,6},{8,9},{9,8},{10,11... | collective-permute-start | bytes 442376 | tf_op jit(solution)/shard_map/ppermute | solution.py:395
  11.3 7.1 %collective-permute-start.1 = (bf16[160,512]{1,0:T(8,128)(2,1)S(1)}, bf16[160,512]{1,0:T(8,128)(2,1)S(1)}, u32[]{:S(2)}, u32[]{:S(2)}) collective-permute-start(bf16[160,512]{1,0:T(8,128)(2,1)S(1)} %aggregate.4.refs_5_), channel_id=1, source_target_pairs={{0,16},{1,17},{2,18},{3,19},{4,20},{5,21},{6,22},{7,23},{8,24},{9,... | collective-permute-start | bytes 491528 | tf_op jit(solution)/shard_map/ppermute | solution.py:395
  14.1 12.2 %collective-permute-start.2 = (bf16[160,512]{1,0:T(8,128)(2,1)S(1)}, bf16[160,512]{1,0:T(8,128)(2,1)S(1)}, u32[]{:S(2)}, u32[]{:S(2)}) collective-permute-start(bf16[160,512]{1,0:T(8,128)(2,1)S(1)} %aggregate.5.refs_5_), channel_id=1, source_target_pairs={{0,16},{1,17},{2,18},{3,19},{4,20},{5,21},{6,22},{7,23},{8,24},{9,... | collective-permute-start | bytes 491528 | tf_op jit(solution)/shard_map/ppermute | solution.py:395
  18.8 7.6 %collective-permute-start.3 = (bf16[144,512]{1,0:T(8,128)(2,1)S(1)}, bf16[144,512]{1,0:T(8,128)(2,1)S(1)}, u32[]{:S(2)}, u32[]{:S(2)}) collective-permute-start(bf16[144,512]{1,0:T(8,128)(2,1)S(1)} %combine.1.refs_5_), channel_id=1, source_target_pairs={{0,7},{1,0},{2,1},{3,2},{4,3},{5,4},{6,5},{7,6},{8,15},{9,8},{10,9... | collective-permute-start | bytes 442376 | tf_op jit(solution)/shard_map/ppermute | solution.py:395
  20.7 5.7 %copy-start.8 = (bf16[512,512]{1,0:T(8,128)(2,1)S(1)}, bf16[512,512]{1,0:T(8,128)(2,1)}, u32[]{:S(2)}) copy-start(bf16[512,512]{1,0:T(8,128)(2,1)} %refs_6_.1) | copy-start | bytes 1572868
  22.1 14.4 %collective-permute-start.7 = (bf16[288,512]{1,0:T(8,128)(2,1)S(1)}, bf16[288,512]{1,0:T(8,128)(2,1)S(1)}, u32[]{:S(2)}, u32[]{:S(2)}) collective-permute-start(bf16[288,512]{1,0:T(8,128)(2,1)S(1)} %get-tuple-element.40), channel_id=1, source_target_pairs={{0,6},{1,1},{2,0},{3,3},{4,2},{5,5},{6,4},{7,7},{8,14},{9,9},{10,8... | collective-permute-start | bytes 884744 | tf_op jit(solution)/shard_map/ppermute | solution.py:395
  24.8 11.8 %collective-permute-start.8 = (bf16[288,512]{1,0:T(8,128)(2,1)S(1)}, bf16[288,512]{1,0:T(8,128)(2,1)S(1)}, u32[]{:S(2)}, u32[]{:S(2)}) collective-permute-start(bf16[288,512]{1,0:T(8,128)(2,1)S(1)} %get-tuple-element.37.refs_7_), channel_id=1, source_target_pairs={{0,16},{1,17},{2,18},{3,19},{4,20},{5,21},{6,22},{7,23},{8,24},{9,... | collective-permute-start | bytes 884744 | tf_op jit(solution)/shard_map/ppermute | solution.py:395
  26.4 5.6 %copy-start = (bf16[512,2048]{1,0:T(8,128)(2,1)S(1)}, bf16[512,2048]{1,0:T(8,128)(2,1)}, u32[]{:S(2)}) copy-start(bf16[512,2048]{1,0:T(8,128)(2,1)} %refs_8_.3) | copy-start | bytes 6291460
  26.4 5.5 %copy-start.1 = (bf16[2048,512]{1,0:T(8,128)(2,1)S(1)}, bf16[2048,512]{1,0:T(8,128)(2,1)}, u32[]{:S(2)}) copy-start(bf16[2048,512]{1,0:T(8,128)(2,1)} %refs_9_.3) | copy-start | bytes 6291460
  29.4 8.6 %collective-permute-start.6 = (bf16[288,512]{1,0:T(8,128)(2,1)S(1)}, bf16[288,512]{1,0:T(8,128)(2,1)S(1)}, u32[]{:S(2)}, u32[]{:S(2)}) collective-permute-start(bf16[288,512]{1,0:T(8,128)(2,1)S(1)} %window.1.refs_0_), channel_id=1, source_target_pairs={{0,16},{1,17},{2,18},{3,19},{4,20},{5,21},{6,22},{7,23},{8,24},{9,... | collective-permute-start | bytes 884744 | tf_op jit(solution)/shard_map/ppermute | solution.py:395
  29.9 13.7 %collective-permute-start.10 = (bf16[288,512]{1,0:T(8,128)(2,1)S(1)}, bf16[288,512]{1,0:T(8,128)(2,1)S(1)}, u32[]{:S(2)}, u32[]{:S(2)}) collective-permute-start(bf16[288,512]{1,0:T(8,128)(2,1)S(1)} %window.1.refs_0_), channel_id=1, source_target_pairs={{0,1},{1,0},{2,3},{3,2},{4,5},{5,4},{6,7},{7,6},{8,9},{9,8},{10,11... | collective-permute-start | bytes 884744 | tf_op jit(solution)/shard_map/ppermute | solution.py:395
  40.2 10.1 %collective-permute-start.9 = (bf16[288,512]{1,0:T(8,128)(2,1)S(1)}, bf16[288,512]{1,0:T(8,128)(2,1)S(1)}, u32[]{:S(2)}, u32[]{:S(2)}) collective-permute-start(bf16[288,512]{1,0:T(8,128)(2,1)S(1)} %join.1), channel_id=1, source_target_pairs={{0,1},{1,2},{2,3},{3,4},{4,5},{5,6},{6,7},{7,0},{8,9},{9,10},{10,1... | collective-permute-start | bytes 884744 | tf_op jit(solution)/shard_map/ppermute | solution.py:395
  40.5 11.3 %collective-permute-start.12 = (bf16[144,512]{1,0:T(8,128)(2,1)S(1)}, bf16[144,512]{1,0:T(8,128)(2,1)S(1)}, u32[]{:S(2)}, u32[]{:S(2)}) collective-permute-start(bf16[144,512]{1,0:T(8,128)(2,1)S(1)} %slice.8), channel_id=1, source_target_pairs={{0,1},{1,0},{2,3},{3,2},{4,5},{5,4},{6,7},{7,6},{8,9},{9,8},{10,11... | collective-permute-start | bytes 442376 | tf_op jit(solution)/shard_map/ppermute | solution.py:395
  43.6 8.2 %collective-permute-start.13 = (bf16[144,512]{1,0:T(8,128)(2,1)S(1)}, bf16[144,512]{1,0:T(8,128)(2,1)S(1)}, u32[]{:S(2)}, u32[]{:S(2)}) collective-permute-start(bf16[144,512]{1,0:T(8,128)(2,1)S(1)} %slice.9), channel_id=1, source_target_pairs={{0,16},{1,17},{2,18},{3,19},{4,20},{5,21},{6,22},{7,23},{8,24},{9,... | collective-permute-start | bytes 442376 | tf_op jit(solution)/shard_map/ppermute | solution.py:395
  50.4 10.3 %collective-permute-start.11 = (bf16[576,512]{1,0:T(8,128)(2,1)S(1)}, bf16[576,512]{1,0:T(8,128)(2,1)S(1)}, u32[]{:S(2)}, u32[]{:S(2)}) collective-permute-start(bf16[576,512]{1,0:T(8,128)(2,1)S(1)} %get-tuple-element.47.refs_12_), channel_id=1, source_target_pairs={{0,8},{1,9},{2,10},{3,11},{4,12},{5,13},{6,14},{7,15},{8,0},{9,1},... | collective-permute-start | bytes 1769480 | tf_op jit(solution)/shard_map/ppermute | solution.py:395
  54.5 2.0 %collective-permute-start.14 = (bf16[256,1024]{1,0:T(8,128)(2,1)S(1)}, bf16[256,1024]{1,0:T(8,128)(2,1)S(1)}, u32[]{:S(2)}, u32[]{:S(2)}) collective-permute-start(bf16[256,1024]{1,0:T(8,128)(2,1)S(1)} %get-tuple-element.51), channel_id=1, source_target_pairs={{0,8},{1,9},{2,10},{3,11},{4,12},{5,13},{6,14},{7,15},{8,0},{9,1},... | collective-permute-start | bytes 1572872 | tf_op jit(solution)/shard_map/ppermute | solution.py:395
  56.7 8.3 %collective-permute-start.15 = (bf16[256,256]{1,0:T(8,128)(2,1)S(1)}, bf16[256,256]{1,0:T(8,128)(2,1)S(1)}, u32[]{:S(2)}, u32[]{:S(2)}) collective-permute-start(bf16[256,256]{1,0:T(8,128)(2,1)S(1)} %get-tuple-element.53), channel_id=1, source_target_pairs={{0,2},{1,3},{2,4},{3,5},{4,6},{5,7},{6,0},{7,1},{8,10},{9,11},{10,... | collective-permute-start | bytes 393224 | tf_op jit(solution)/shard_map/ppermute | solution.py:395
  57.7 12.1 %collective-permute-start.16 = (bf16[256,256]{1,0:T(8,128)(2,1)S(1)}, bf16[256,256]{1,0:T(8,128)(2,1)S(1)}, u32[]{:S(2)}, u32[]{:S(2)}) collective-permute-start(bf16[256,256]{1,0:T(8,128)(2,1)S(1)} %get-tuple-element.54), channel_id=1, source_target_pairs={{0,4},{1,5},{2,6},{3,7},{4,0},{5,1},{6,2},{7,3},{8,12},{9,13},{10,... | collective-permute-start | bytes 393224 | tf_op jit(solution)/shard_map/ppermute | solution.py:395
  57.8 12.0 %collective-permute-start.17 = (bf16[256,256]{1,0:T(8,128)(2,1)S(1)}, bf16[256,256]{1,0:T(8,128)(2,1)S(1)}, u32[]{:S(2)}, u32[]{:S(2)}) collective-permute-start(bf16[256,256]{1,0:T(8,128)(2,1)S(1)} %get-tuple-element.55), channel_id=1, source_target_pairs={{0,6},{1,7},{2,0},{3,1},{4,2},{5,3},{6,4},{7,5},{8,14},{9,15},{10,... | collective-permute-start | bytes 393224 | tf_op jit(solution)/shard_map/ppermute | solution.py:395
  (7 other events, 22.5 us)

commit v3 on v2

--- a/solution.py
+++ b/solution.py
@@ -15,12 +15,8 @@
 HALF = WO // 2
 PIECE = WA * HALF
 MARK = 2.0**40
-PIECES = ((1, 1), (0, 1), (1, 0), (0, 0))
-LSE_ROWS = 16
-COTS = 5
 FLOPS_PER_US = 3 * 10**9
-MID_US = 4.0
-MLP_US = 2.0
+ACROSS_US = 0.05
 F32 = jnp.float32
 BF16 = jnp.bfloat16
 MIB = 1 << 20
@@ -77,7 +73,8 @@
     return pltpu.roll(cells, cells.shape[0] - WA // 2, 0)
 
 
-def pack_levels_body(lev_count, mask_ref, lev_ref, own_ref, send_ref, blocks):
+def pack_levels_body(lev_count, mask_ref, lev_ref, *refs):
+    outs, core_ref, blocks = refs[:-2], refs[-2], refs[-1]
     count = lev_ref.shape[0]
     me = lax.axis_index("lev")
     for j in range(count):
@@ -88,11 +85,10 @@
             for i in range(lev_count):
                 blocks[half * lev_count + i, pl.ds(at, WA)] = cells[i * WA : (i + 1) * WA]
     rows = count * PIECE
-    for k, (half, beside) in enumerate(PIECES):
-        at = slice(k * rows, (k + 1) * rows)
-        mine = me ^ (2 * beside)
-        own_ref[at] = blocks[half * lev_count + mine].astype(BF16)
-        send_ref[at] = blocks[half * lev_count + (mine ^ 1)].astype(BF16)
+    for half in range(2):
+        for n, d in enumerate((0, 2, 3)):
+            outs[3 * half + n][...] = blocks[half * lev_count + (me ^ d)].astype(BF16)
+        core_ref[half * rows : (half + 1) * rows] = blocks[half * lev_count + (me ^ 1)].astype(BF16)
 
 
 def pack_cot_body(lev_count, cot_ref, east_ref, west_ref, own_east_ref, own_west_ref, blocks):
@@ -123,7 +119,7 @@
     return jnp.concatenate([high, (value - high.astype(F32)).astype(BF16)], 1)
 
 
-def aggregate_body(k, own, recv, query_ref, w_key, w_value, out_ref, pool):
+def aggregate_body(half, own, beside, far, core, query_ref, w_key, w_value, out_ref, pool):
     width = w_key.shape[0]
     head_size = width // HEADS
     pairs = 2 * PIECE
@@ -132,9 +128,9 @@
     table = (owner == lax.broadcasted_iota(jnp.int32, (HEADS, width), 0)).astype(F32)
     query = query_ref[...].astype(F32)
     block_query = jnp.concatenate([table * query[l : l + 1] for l in range(LATENT)], 0)
-    count = own.shape[0] // len(PIECES)
-    at = slice(k * count, (k + 1) * count)
-    rows = jnp.concatenate([own[at], recv[at]], 0)
+    count = own.shape[0]
+    rows = [own[...], beside[...], far[...], core[half * count : (half + 1) * count]]
+    rows = jnp.concatenate(rows, 0)
     blocks = rows.shape[0] // pairs
     split = [slice(b * pairs, (b + 1) * pairs) for b in range(blocks)]
     keys = dot(rows, w_key[...]).astype(BF16)
@@ -155,40 +151,7 @@
         summed = functools.reduce(jnp.add, [prod[rows_at] for rows_at in split])
         summed = summed + pltpu.roll(summed, PIECE, 0)
         pool[pl.ds(slot * PIECE, PIECE)] = summed[:PIECE]
-    rows = LATENT * PIECE
-    out_ref[:rows] = pool[...].astype(BF16)
-    lse = top + jnp.log(total)
-    high = lse.astype(BF16).astype(F32)
-    middle = (lse - high).astype(BF16).astype(F32)
-    parts = jnp.concatenate([high, middle, lse - high - middle, jnp.zeros_like(lse)], 1)
-    parts = [parts[g * LSE_ROWS : (g + 1) * LSE_ROWS] for g in range(3)]
-    parts.append(jnp.zeros_like(parts[0]))
-    out_ref[rows:] = jnp.concatenate(parts, 1).astype(BF16)
-
-
-def combined(first, second, pool, left, right):
-    rows = LATENT * PIECE
-    lanes = LATENT * HEADS
-    width = first.shape[1]
-    lses = []
-    for ref, rows_ref in ((first, left), (second, right)):
-        rows_ref[...] = ref[:rows].astype(F32)
-        parts = ref[rows:].astype(F32)
-        group = 4 * lanes
-        parts = jnp.concatenate([parts[:, g * group : (g + 1) * group] for g in range(3)], 0)
-        lses.append(parts[:, :lanes] + parts[:, lanes : 2 * lanes] + parts[:, 2 * lanes : 3 * lanes])
-    share = 1.0 / (1.0 + jnp.exp(lses[1] - lses[0]))
-    both = two_parts(share)
-    for l in range(LATENT):
-        slot = (l - WL // 2) % LATENT
-        at = pl.ds(slot * PIECE, PIECE)
-        spread = dot(both, head_pick(lanes, width, l * HEADS))[:PIECE]
-        pool[at] = spread * left[at] + (1.0 - spread) * right[at]
-    return pool[...].astype(BF16)
-
-
-def combine_body(first, second, out_ref, pool, left, right):
-    out_ref[...] = combined(first, second, pool, left, right)
+    out_ref[...] = pool[...].astype(BF16)
 
 
 def window_attention(lev_count, latent, gain, w_qkv):
@@ -233,22 +196,9 @@
     return jnp.concatenate(mixed, 0).astype(BF16)
 
 
-def window_body(
-    lev_count,
-    east_own,
-    east_beside,
-    west,
-    w_agg_out,
-    gain_attn,
-    w_qkv,
-    w_proj,
-    resid_ref,
-    pool,
-    left,
-    right,
-):
-    pooled = [combined(east_own, east_beside, pool, left, right), west[...]]
-    latent = dot(jnp.concatenate(pooled, 0), w_agg_out[...]).astype(BF16)
+def window_body(lev_count, east, west, w_agg_out, gain_attn, w_qkv, w_proj, resid_ref):
+    pooled = jnp.concatenate([east[...], west[...]], 0)
+    latent = dot(pooled, w_agg_out[...]).astype(BF16)
     mixed = window_attention(lev_count, latent, gain_attn, w_qkv)
     resid = (latent.astype(F32) + dot(mixed, w_proj[...])).astype(BF16)
     resid_ref[...] = resid
@@ -271,10 +221,10 @@
 
 def grad_body(chunks, cot_at, adds, last, part, *refs):
     resid = refs[:chunks]
-    count = COTS if adds else 2
-    cots = refs[chunks : chunks + count]
-    gain, w_up, w_down = refs[chunks + count : chunks + count + 3]
-    rest = refs[chunks + count + 3 :]
+    count = chunks + 1 + max(which for which, _ in cot_at)
+    cots = refs[chunks:count]
+    gain, w_up, w_down = refs[count : count + 3]
+    rest = refs[count + 3 :]
     normed, n_half, c_half = rest[-3:]
     if adds:
         (sum_up, sum_dn), rest = rest[:2], rest[2:]
@@ -326,8 +276,9 @@
         send[quarter:] = acc_dn[other].astype(BF16)
 
 
-def split_body(groups, keep, recv, own_ref, *refs):
+def split_body(groups, keep, recv, chip_rows, own_ref, rows_ref, *refs):
     outs, blocks = refs[:-1], refs[-1]
+    rows_ref[...] = chip_rows[...]
     cols = keep.shape[1] // groups
     for n in range(groups):
         at = slice(n * cols, (n + 1) * cols)
@@ -335,7 +286,7 @@
     me = lax.axis_index("tile") // 2
     own_ref[...] = blocks[me]
     for d in range(1, groups):
-        outs[d - 1][...] = blocks[lax.rem(me + d, groups)].astype(BF16)
+        outs[d - 1][...] = blocks[me ^ d].astype(BF16)
 
 
 def total_body(own, *refs):
@@ -354,29 +305,28 @@
     out_ref[half:] = second[...]
 
 
-def join_all_body(own_e, beside_e, west, east_ref, joined_ref):
-    join_body(own_e, beside_e, east_ref)
-    half = east_ref.shape[0]
-    joined_ref[:half] = east_ref[...]
-    joined_ref[half:] = west[...]
-
-
-def hand_on_body(first, second, other, joined_ref, other_ref):
-    join_body(first, second, joined_ref)
-    other_ref[...] = other[...]
-
-
-def unpack_body(east, west, core, out_ref, mark_ref, blocks):
+def assemble_body(*refs):
+    at = 0
+    for ref in refs[:-1]:
+        refs[-1][at : at + ref.shape[0]] = ref[...]
+        at += ref.shape[0]
+
+
+def copy_body(*refs):
+    half = len(refs) // 2
+    for source, target in zip(refs[:half], refs[half:]):
+        target[...] = source[...]
+
+
+def unpack_body(own, core, out_ref, mark_ref, blocks):
     mark_ref[...] = jnp.zeros_like(mark_ref)
     me = lax.axis_index("lev")
     half = LATENT * PIECE
-    for d in range(2):
-        at = slice(d * half, (d + 1) * half)
-        then = slice((d + 2) * half, (d + 3) * half)
-        blocks[me ^ (2 * d), :half] = east[at].astype(F32)
-        blocks[me ^ (2 * d), half:] = west[at].astype(F32)
-        blocks[me ^ (2 * d) ^ 1, :half] = core[at].astype(F32)
-        blocks[me ^ (2 * d) ^ 1, half:] = core[then].astype(F32)
+    for first, rows in ((me, own), (me ^ 1, core)):
+        for d in range(2):
+            for h in range(2):
+                at = (2 * h + d) * half
+                blocks[first ^ (2 * d), h * half : (h + 1) * half] = rows[at : at + half].astype(F32)
     for l in range(LATENT):
         for o in range(WO):
             at = (half if o < HALF else 0) + l * PIECE + (o % HALF) * WA
@@ -436,61 +386,46 @@
     )
     cot_peer_e = exchanged(cot_east_own, 0, peer)
     cot_own_w = exchanged(cot_west_own, 0, west)
-    own_raw, send_raw = call(
+    *pieces, core = call(
         functools.partial(pack_levels_body, levs),
         (level_mask[None], levels.transpose(0, 2, 1, 3)),
-        [((len(PIECES) * piece, width), BF16)] * 2,
+        [((piece, width), BF16)] * 6 + [((2 * piece, width), BF16)],
         [pltpu.VMEM((2 * levs, piece, width), F32)],
         after=cot_east,
         us=0.7,
     )
-    recv_raw = exchanged(send_raw, 1, same)
-    weights = (latent_query, w_key, w_value)
-    aggregated = lambda k, after: call(
-        functools.partial(aggregate_body, k),
-        (own_raw, recv_raw, *weights),
-        [((rows + LSE_ROWS, width), BF16)],
+    core = exchanged(core, 1, same)
+    pieces[1:3] = call(
+        copy_body, pieces[1:3], [((piece, width), BF16)] * 2, vmem=8, after=core
+    )
+    east_raw, west_raw = [
+        (own, exchanged(beside, 2, same), exchanged(far, 3, same), core)
+        for own, beside, far in (pieces[:3], pieces[3:])
+    ]
+    aggregated = lambda half, chunks, after: call(
+        functools.partial(aggregate_body, half),
+        (*chunks, latent_query, w_key, w_value),
+        [((rows, width), BF16)],
         [pltpu.VMEM((rows, width), F32)],
         after=after,
-        us=1.3,
+        us=2.1,
     )[0]
-    pooled = [aggregated(0, None)]
-    west_beside = exchanged(pooled[0], 2, same)
-    pooled.append(aggregated(1, pooled[0]))
-    east_beside = exchanged(pooled[1], 2, same)
-    pooled.append(aggregated(2, pooled[1]))
-    pooled_w = call(
-        combine_body,
-        (pooled[2], west_beside),
-        [((rows, width), BF16)],
-        [pltpu.VMEM((rows, width), F32)] * 3,
-        us=0.4,
+    west_pooled = aggregated(1, west_raw, None)
+    pooled_e = aggregated(0, east_raw, west_pooled)
+    pooled_w = exchanged(west_pooled, 0, west)
+    cot_joined = call(
+        join_body,
+        (cot_own_w, cot_peer_e),
+        [((window, width), BF16)],
+        vmem=8,
+        after=west_pooled,
     )[0]
-    pooled.append(aggregated(3, pooled_w))
-    pooled_w = exchanged(pooled_w, 0, west)
-    cot_joined, cot_west = call(
-        hand_on_body,
-        (cot_own_w, cot_peer_e, cot_west),
-        [((window, width), BF16)] * 2,
-        vmem=8,
-        after=pooled[3],
-    )
-    cot_peer_w = exchanged(cot_west, 0, next_pair)
-    cots = (cot_east, cot_own_w, cot_peer_e, cot_peer_w, exchanged(cot_joined, 2, same))
+    cot_beside = exchanged(cot_joined, 2, same)
 
     resid = call(
         functools.partial(window_body, levs),
-        (
-            pooled[3],
-            east_beside,
-            pooled_w,
-            w_agg_out,
-            gain_attn[None],
-            w_qkv,
-            w_proj,
-        ),
+        (pooled_e, pooled_w, w_agg_out, gain_attn[None], w_qkv, w_proj),
         [((window, width), BF16)],
-        [pltpu.VMEM((rows, width), F32)] * 3,
         vmem=24,
         after=cot_joined,
         us=3.0,
@@ -500,14 +435,6 @@
     far = [exchanged(beside[:rows], 0, peer), exchanged(across[rows:], 2, same)]
 
     gain_mlp = gain_mlp[None]
-    mlp = lambda pieces, after: call(
-        mlp_body,
-        (pieces, gain_mlp, w_up, w_down),
-        [((rows, width), BF16)] * 2,
-        vmem=20,
-        after=after,
-        us=MLP_US,
-    )
     up_part, down_part = w_up, w_down
     if part % 128:
         parity = lax.rem(lax.axis_index("tile"), 2)
@@ -521,62 +448,84 @@
     scratch = lambda n: [pltpu.VMEM((n * rows, width), BF16)] + [
         pltpu.VMEM((n * rows, 2 * quarter), BF16)
     ] * 2
-    own_at, far_at = ((0, 0), (1, 0)), ((4, 1), (3, 1))
-    middle_at = ((0, 1), (4, 0), (2, 0), (3, 0))
-    own_e, own_w = mlp(resid, cots[:2])
+    mlp = lambda piece, after, us: call(
+        mlp_body,
+        (piece, gain_mlp, w_up, w_down),
+        [((rows, width), BF16)] * 2,
+        vmem=20,
+        after=after,
+        us=us,
+    )
+    weights = (gain_mlp, up_part, down_part)
+    own_at, middle_at, far_at = (
+        ((0, 0), (1, 0)),
+        ((0, 1), (1, 0), (2, 0), (3, 0)),
+        ((0, 1), (1, 1)),
+    )
     so_far = call(
         functools.partial(grad_body, 1, own_at, False, False, part),
-        (resid, *cots[:2], gain_mlp, up_part, down_part),
+        (resid, cot_east, cot_own_w, *weights),
         sums,
         scratch(2),
         vmem=24,
-        after=own_e,
+        after=cot_beside,
         us=2.2,
     )
-    beside_e, beside_w = mlp(beside, (so_far[0], *cots[3:]))
+    cot_west = call(
+        copy_body, (cot_west,), [((window, width), BF16)], vmem=8, after=so_far[0]
+    )[0]
+    cot_peer_w = exchanged(cot_west, 0, next_pair)
+    own_out, own_w = mlp(resid, cot_west, 2.0)
+    beside_out, beside_w = mlp(beside, (own_w, across), 3.0)
     out_w = exchanged(
         call(join_body, (own_w, beside_w), [((window, width), BF16)], vmem=8)[0], 0, east
     )
     so_far = call(
         functools.partial(grad_body, 2, middle_at, True, False, part),
-        (beside, across, *cots, gain_mlp, up_part, down_part, *so_far),
+        (
+            *(beside, across),
+            *(cot_east, cot_beside, cot_peer_e, cot_peer_w),
+            *weights,
+            *so_far,
+        ),
         sums,
         scratch(4),
         vmem=24,
-        after=beside_e,
-        us=MID_US,
-    )
-    out_e, chip_rows = call(
-        join_all_body,
-        (own_e, beside_e, out_w),
-        [((window, width), BF16), ((2 * window, width), BF16)],
-        vmem=8,
-        after=so_far[0],
+        after=beside_out,
+        us=ACROSS_US,
     )
     send, keep = call(
         functools.partial(grad_body, 2, far_at, True, True, part),
-        (*far, *cots, gain_mlp, up_part, down_part, *so_far),
+        (*far, cot_beside, cot_peer_w, *weights, *so_far),
         [((2 * quarter, hidden // 2), BF16), ((2 * quarter, hidden // 2), F32)],
         [pltpu.VMEM((2 * quarter, hidden // 2), F32)] * 2 + scratch(2),
         vmem=24,
-        after=chip_rows,
         us=2.6,
     )
+    chip_rows = call(
+        assemble_body,
+        (own_out, beside_out, out_w),
+        [((2 * window, width), BF16)],
+        vmem=8,
+        after=send,
+        us=3.5,
+    )[0]
     recv = exchanged(send, 1, same)
-    own, *sends = call(
+    own, chip_rows, *sends = call(
         functools.partial(split_body, groups),
-        (keep, recv),
-        [((2 * quarter, part), F32)] + [((2 * quarter, part), BF16)] * (groups - 1),
+        (keep, recv, chip_rows),
+        [((2 * quarter, part), F32), ((2 * window, width), BF16)]
+        + [((2 * quarter, part), BF16)] * (groups - 1),
         [pltpu.VMEM((groups, 2 * quarter, part), F32)],
         vmem=32,
     )
     received = [
-        exchanged(block, 0, lambda t, d=d: (t + 2 * d) % tiles) for d, block in enumerate(sends, 1)
+        exchanged(block, 0, lambda t, d=d: t ^ (2 * d)) for d, block in enumerate(sends, 1)
     ]
     core_rows = exchanged(chip_rows, 1, same)
     encoded, mark = call(
         unpack_body,
-        (out_e, out_w, core_rows),
+        (chip_rows, core_rows),
         [((LATENT, lon, lat, width), BF16), ((8, 128), F32)],
         [pltpu.VMEM((levs, window, width), F32)],
         vmem=24, us=1.6

time: 70.8 us -> 70.1 us (level)
  starting transfers between devices: 26.1 us -> 31.2 us
  waiting for transfers between devices: 16.3 us -> 12 us
  Pallas kernels: 25.2 us -> 23.7 us
    ppermute x18 -> x20, starting transfers between devices: 26.1 us -> 31.2 us  [exchanged(): return lax.ppermute(block, ('lev', 'tile'), route)]
    ppermute x18 -> x20, waiting for transfers between devices: 16.3 us -> 12 us  [exchanged(): return lax.ppermute(block, ('lev', 'tile'), route)]
    pallas_call x19 -> x18, Pallas kernels: 25.2 us -> 23.7 us  [call(): pl.pallas_call(body, out_shape=[jax.ShapeDtypeStruct(shape, dtype) for sh...]
  transfers between devices with their start and end apart: 18 -> 20, of which waited for: 7 -> 6; matrix products, arithmetic and copies ran while one was open for 0% -> 0% of each run, Pallas kernels for 33% -> 31%
where the time goes in v3:
time: 70.1 us; the launch traced here: 69.9 us
  starting transfers between devices  31.2 us (45%)
  Pallas kernels  23.7 us (34%)
  waiting for transfers between devices  12 us (17%)
  local copies, waits for them, and re-layouts  2.11 us (3%)
  between operations  0.92 us (1%)
    ppermute x20, starting transfers between devices, exchanged(): return lax.ppermute(block, ('lev', 'tile'), route)  31.2 us
    pallas_call x18, Pallas kernels, call(): pl.pallas_call(body, out_shape=[jax.ShapeDtypeStruct(shape, dtype) for sh...  23.7 us
    ppermute x20, waiting for transfers between devices, exchanged(): return lax.ppermute(block, ('lev', 'tile'), route)  12 us
    unnamed x26, local copies, waits for them, and re-layouts  2.09 us
  transfers between devices with their start and end apart: 20, of which 6 were waited for; matrix products, arithmetic and copies ran while one was open for 0% of the time, Pallas kernels for 31%

profile of v3, /device:TPU:0, one launch (start us, length us, event | category | flops | bytes accessed | tf_op | source)
XLA Modules:
  0.0 69.9 jit_solution(439261524899962727)
XLA Ops:
  0.6 1.3 %copy-done.4 = bf16[4,24,12,512]{3,1,2,0:T(8,128)(2,1)S(1)} copy-done((bf16[4,24,12,512]{3,1,2,0:T(8,128)(2,1)S(1)}, bf16[4,24,12,512]{3,1,2,0:T(8,128)(2,1)}, u32[]{:S(2)}) %copy-start.4) | copy-done | bytes 1179672
  4.4 2.6 %collective-permute-start.3 = (bf16[144,512]{1,0:T(8,128)(2,1)S(1)}, bf16[144,512]{1,0:T(8,128)(2,1)S(1)}, u32[]{:S(2)}, u32[]{:S(2)}) collective-permute-start(bf16[144,512]{1,0:T(8,128)(2,1)S(1)} %get-tuple-element.43), channel_id=1, source_target_pairs={{0,16},{1,17},{2,18},{3,19},{4,20},{5,21},{6,22},{7,23},{8,24},{9,... | collective-permute-start | bytes 442376 | tf_op jit(solution)/shard_map/ppermute | solution.py:345
  7.1 4.7 %collective-permute-start.6 = (bf16[144,512]{1,0:T(8,128)(2,1)S(1)}, bf16[144,512]{1,0:T(8,128)(2,1)S(1)}, u32[]{:S(2)}, u32[]{:S(2)}) collective-permute-start(bf16[144,512]{1,0:T(8,128)(2,1)S(1)} %get-tuple-element.45), channel_id=1, source_target_pairs={{0,7},{1,0},{2,1},{3,2},{4,3},{5,4},{6,5},{7,6},{8,15},{9,8},{10,9... | collective-permute-start | bytes 442376 | tf_op jit(solution)/shard_map/ppermute | solution.py:345
  11.9 1.6 %collective-permute-start.1 = (bf16[144,512]{1,0:T(8,128)(2,1)S(1)}, bf16[144,512]{1,0:T(8,128)(2,1)S(1)}, u32[]{:S(2)}, u32[]{:S(2)}) collective-permute-start(bf16[144,512]{1,0:T(8,128)(2,1)S(1)} %get-tuple-element.40), channel_id=1, source_target_pairs={{0,16},{1,17},{2,18},{3,19},{4,20},{5,21},{6,22},{7,23},{8,24},{9,... | collective-permute-start | bytes 442376 | tf_op jit(solution)/shard_map/ppermute | solution.py:345
  14.4 2.1 %aggregate.2.refs_7_.refs_2_ = bf16[144,512]{1,0:T(8,128)(2,1)S(1)} custom-call(bf16[144,512]{1,0:T(8,128)(2,1)S(1)} %get-tuple-element.42.own, bf16[144,512]{1,0:T(8,128)(2,1)S(1)} %collective-permute-done.3.beside, bf16[144,512]{1,0:T(8,128)(2,1)S(1)} %collective-permute-done.4.far, bf16[288,512]{1,0:T(8,128)(2,1)S(1)} %collective-permute-done.refs_2_.core.refs_3_, ...), custom_call_target="tpu_custom_call" | custom-call | flops 6300000256 | tf_op jit(solution)/shard_map/aggregate/pallas_call | solution.py:45
  16.5 4.6 %collective-permute-start.5 = (bf16[144,512]{1,0:T(8,128)(2,1)S(1)}, bf16[144,512]{1,0:T(8,128)(2,1)S(1)}, u32[]{:S(2)}, u32[]{:S(2)}) collective-permute-start(bf16[144,512]{1,0:T(8,128)(2,1)S(1)} %aggregate.2.refs_7_.refs_2_), channel_id=1, source_target_pairs={{0,7},{1,0},{2,1},{3,2},{4,3},{5,4},{6,5},{7,6},{8,15},{9,8},{10,9... | collective-permute-start | bytes 442376 | tf_op jit(solution)/shard_map/ppermute | solution.py:345
  21.1 1.6 %collective-permute-start.12 = (bf16[288,512]{1,0:T(8,128)(2,1)S(1)}, bf16[288,512]{1,0:T(8,128)(2,1)S(1)}, u32[]{:S(2)}, u32[]{:S(2)}) collective-permute-start(bf16[288,512]{1,0:T(8,128)(2,1)S(1)} %join.2.refs_6_), channel_id=1, source_target_pairs={{0,16},{1,17},{2,18},{3,19},{4,20},{5,21},{6,22},{7,23},{8,24},{9,... | collective-permute-start | bytes 884744 | tf_op jit(solution)/shard_map/ppermute | solution.py:345
  22.8 2.1 %aggregate.3.refs_0_ = bf16[144,512]{1,0:T(8,128)(2,1)S(1)} custom-call(bf16[144,512]{1,0:T(8,128)(2,1)S(1)} %get-tuple-element.36.refs_0_, bf16[144,512]{1,0:T(8,128)(2,1)S(1)} %collective-permute-done.1.refs_1_, bf16[144,512]{1,0:T(8,128)(2,1)S(1)} %collective-permute-done.2.refs_2_, bf16[288,512]{1,0:T(8,128)(2,1)S(1)} %collective-permute-done.refs_2_.core.refs_3_, ...), custom_call_target="tpu_custom_call" | custom-call | flops 6300000256 | tf_op jit(solution)/shard_map/aggregate/pallas_call | solution.py:45
  25.4 2.6 %window.1.refs_0_ = bf16[288,512]{1,0:T(8,128)(2,1)S(1)} custom-call(bf16[144,512]{1,0:T(8,128)(2,1)S(1)} %aggregate.3.refs_0_, bf16[144,512]{1,0:T(8,128)(2,1)S(1)} %collective-permute-done.5.refs_1_, bf16[512,512]{1,0:T(8,128)(2,1)S(1)} %copy-done.8, f32[1,512]{1,0:T(1,128)S(1)} %bitcast.13, bf16[512,1536]{1,0:T(8,128)(2,1)S(1)} %copy-done.3, ...), custom_call_target="tpu_custom_call" | custom-call | flops 8999999488 | tf_op jit(solution)/shard_map/window/pallas_call | solution.py:45
  28.0 1.6 %collective-permute-start.8 = (bf16[288,512]{1,0:T(8,128)(2,1)S(1)}, bf16[288,512]{1,0:T(8,128)(2,1)S(1)}, u32[]{:S(2)}, u32[]{:S(2)}) collective-permute-start(bf16[288,512]{1,0:T(8,128)(2,1)S(1)} %window.1.refs_0_), channel_id=1, source_target_pairs={{0,16},{1,17},{2,18},{3,19},{4,20},{5,21},{6,22},{7,23},{8,24},{9,... | collective-permute-start | bytes 884744 | tf_op jit(solution)/shard_map/ppermute | solution.py:345
  29.6 1.2 %collective-permute-done.12.refs_6_.refs_3_.refs_2_ = bf16[288,512]{1,0:T(8,128)(2,1)S(1)} collective-permute-done((bf16[288,512]{1,0:T(8,128)(2,1)S(1)}, bf16[288,512]{1,0:T(8,128)(2,1)S(1)}, u32[]{:S(2)}, u32[]{:S(2)}) %collective-permute-start.12) | collective-permute-done | bytes 294944 | tf_op jit(solution)/shard_map/ppermute | solution.py:345
  30.9 2.4 %grad.3 = (f32[256,1024]{1,0:T(8,128)S(1)}, f32[256,1024]{1,0:T(8,128)S(1)}) custom-call(bf16[288,512]{1,0:T(8,128)(2,1)S(1)} %window.1.refs_0_, bf16[288,512]{1,0:T(8,128)(2,1)S(1)} %get-tuple-element.35.refs_2_.refs_1_, bf16[144,512]{1,0:T(8,128)(2,1)S(1)} %collective-permute-done.6.refs_0_.refs_2_, f32[1,512]{1,0:T(1,128)S(1)} %bitcast.6, ...), custom_call_target="tpu_custom_call" | custom-call | flops 6600000000 | tf_op jit(solution)/shard_map/grad/pallas_call | solution.py:45
  33.3 6.5 %collective-permute-start.13 = (bf16[288,512]{1,0:T(8,128)(2,1)S(1)}, bf16[288,512]{1,0:T(8,128)(2,1)S(1)}, u32[]{:S(2)}, u32[]{:S(2)}) collective-permute-start(bf16[288,512]{1,0:T(8,128)(2,1)S(1)} %copy.19.refs_4_), channel_id=1, source_target_pairs={{0,6},{1,1},{2,0},{3,3},{4,2},{5,5},{6,4},{7,7},{8,14},{9,9},{10,8... | collective-permute-start | bytes 884744 | tf_op jit(solution)/shard_map/ppermute | solution.py:345
  39.9 2.2 %mlp.2 = (bf16[144,512]{1,0:T(8,128)(2,1)S(1)}, bf16[144,512]{1,0:T(8,128)(2,1)S(1)}) custom-call(bf16[288,512]{1,0:T(8,128)(2,1)S(1)} %window.1.refs_0_, f32[1,512]{1,0:T(1,128)S(1)} %bitcast.7, bf16[512,2048]{1,0:T(8,128)(2,1)S(1)} %copy-done, bf16[2048,512]{1,0:T(8,128)(2,1)S(1)} %copy-done.1, bf16[288,512]{1,0:T(8,128)(2,1)S(1)} %copy.19.refs_4_), custom_call_target="tpu_custom_call" | custom-call | flops 6000000000 | tf_op jit(solution)/shard_map/mlp/pallas_call | solution.py:45
  42.7 2.2 %mlp.3 = (bf16[144,512]{1,0:T(8,128)(2,1)S(1)}, bf16[144,512]{1,0:T(8,128)(2,1)S(1)}) custom-call(bf16[288,512]{1,0:T(8,128)(2,1)S(1)} %collective-permute-done.8.refs_0_, f32[1,512]{1,0:T(1,128)S(1)} %bitcast.8, bf16[512,2048]{1,0:T(8,128)(2,1)S(1)} %copy-done, bf16[2048,512]{1,0:T(8,128)(2,1)S(1)} %copy-done.1, ...), custom_call_target="tpu_custom_call" | custom-call | flops 8999999488 | tf_op jit(solution)/shard_map/mlp/pallas_call | solution.py:45
  44.9 2.1 %collective-permute-start.15 = (bf16[288,512]{1,0:T(8,128)(2,1)S(1)}, bf16[288,512]{1,0:T(8,128)(2,1)S(1)}, u32[]{:S(2)}, u32[]{:S(2)}) collective-permute-start(bf16[288,512]{1,0:T(8,128)(2,1)S(1)} %join.3), channel_id=1, source_target_pairs={{0,1},{1,2},{2,3},{3,4},{4,5},{5,6},{6,7},{7,0},{8,9},{9,10},{10,1... | collective-permute-start | bytes 884744 | tf_op jit(solution)/shard_map/ppermute | solution.py:345
  47.0 3.5 %grad.4 = (f32[256,1024]{1,0:T(8,128)S(1)}, f32[256,1024]{1,0:T(8,128)S(1)}) custom-call(bf16[288,512]{1,0:T(8,128)(2,1)S(1)} %collective-permute-done.8.refs_0_, bf16[288,512]{1,0:T(8,128)(2,1)S(1)} %collective-permute-done.10.refs_5_.refs_1_, bf16[288,512]{1,0:T(8,128)(2,1)S(1)} %get-tuple-element.35.refs_2_.refs_1_, ...), custom_call_target="tpu_custom_call" | custom-call | flops 150000000 | tf_op jit(solution)/shard_map/grad/pallas_call | solution.py:45
  50.6 2.7 %grad.5 = (bf16[256,1024]{1,0:T(8,128)(2,1)S(1)}, f32[256,1024]{1,0:T(8,128)S(1)}) custom-call(bf16[144,512]{1,0:T(8,128)(2,1)S(1)} %collective-permute-done.9.refs_0_, bf16[144,512]{1,0:T(8,128)(2,1)S(1)} %collective-permute-done.11.refs_1_, bf16[288,512]{1,0:T(8,128)(2,1)S(1)} %collective-permute-done.12.refs_6_.refs_3_.refs_2_, ...), custom_call_target="tpu_custom_call" | custom-call | flops 7800000000 | tf_op jit(solution)/shard_map/grad/pallas_call | solution.py:45
  53.3 2.2 %collective-permute-done.15.refs_2_ = bf16[288,512]{1,0:T(8,128)(2,1)S(1)} collective-permute-done((bf16[288,512]{1,0:T(8,128)(2,1)S(1)}, bf16[288,512]{1,0:T(8,128)(2,1)S(1)}, u32[]{:S(2)}, u32[]{:S(2)}) %collective-permute-start.15) | collective-permute-done | bytes 294944 | tf_op jit(solution)/shard_map/ppermute | solution.py:345
  56.0 3.1 %collective-permute-start.18 = (bf16[256,256]{1,0:T(8,128)(2,1)S(1)}, bf16[256,256]{1,0:T(8,128)(2,1)S(1)}, u32[]{:S(2)}, u32[]{:S(2)}) collective-permute-start(bf16[256,256]{1,0:T(8,128)(2,1)S(1)} %get-tuple-element.62), channel_id=1, source_target_pairs={{0,4},{1,5},{2,6},{3,7},{4,0},{5,1},{6,2},{7,3},{8,12},{9,13},{10,... | collective-permute-start | bytes 393224 | tf_op jit(solution)/shard_map/ppermute | solution.py:345
  59.2 1.2 %collective-permute-start.19 = (bf16[256,256]{1,0:T(8,128)(2,1)S(1)}, bf16[256,256]{1,0:T(8,128)(2,1)S(1)}, u32[]{:S(2)}, u32[]{:S(2)}) collective-permute-start(bf16[256,256]{1,0:T(8,128)(2,1)S(1)} %get-tuple-element.63), channel_id=1, source_target_pairs={{0,6},{1,7},{2,4},{3,5},{4,2},{5,3},{6,0},{7,1},{8,14},{9,15},{10,... | collective-permute-start | bytes 393224 | tf_op jit(solution)/shard_map/ppermute | solution.py:345
  60.4 1.6 %unpack.1 = (bf16[4,12,24,512]{3,2,1,0:T(8,128)(2,1)}, f32[8,128]{1,0:T(8,128)S(1)}) custom-call(bf16[576,512]{1,0:T(8,128)(2,1)S(1)} %get-tuple-element.58.own, bf16[576,512]{1,0:T(8,128)(2,1)S(1)} %collective-permute-done.16.core), custom_call_target="tpu_custom_call" | custom-call | flops 4800000000 | tf_op jit(solution)/shard_map/unpack/pallas_call | solution.py:45
  62.0 2.3 %collective-permute-done.17.refs_1_ = bf16[256,256]{1,0:T(8,128)(2,1)S(1)} collective-permute-done((bf16[256,256]{1,0:T(8,128)(2,1)S(1)}, bf16[256,256]{1,0:T(8,128)(2,1)S(1)}, u32[]{:S(2)}, u32[]{:S(2)}) %collective-permute-start.17) | collective-permute-done | bytes 131104 | tf_op jit(solution)/shard_map/ppermute | solution.py:345
  64.3 4.9 %collective-permute-done.18.refs_2_ = bf16[256,256]{1,0:T(8,128)(2,1)S(1)} collective-permute-done((bf16[256,256]{1,0:T(8,128)(2,1)S(1)}, bf16[256,256]{1,0:T(8,128)(2,1)S(1)}, u32[]{:S(2)}, u32[]{:S(2)}) %collective-permute-start.18) | collective-permute-done | bytes 131104 | tf_op jit(solution)/shard_map/ppermute | solution.py:345
  (62 shorter events, 6.0 us)
Async XLA Ops:
  3.9 10.5 %copy-start.6 = (bf16[512,512]{1,0:T(8,128)(2,1)S(1)}, bf16[512,512]{1,0:T(8,128)(2,1)}, u32[]{:S(2)}) copy-start(bf16[512,512]{1,0:T(8,128)(2,1)} %refs_5_.4) | copy-start | bytes 1572868
  3.9 10.5 %copy-start.7 = (bf16[512,512]{1,0:T(8,128)(2,1)S(1)}, bf16[512,512]{1,0:T(8,128)(2,1)}, u32[]{:S(2)}) copy-start(bf16[512,512]{1,0:T(8,128)(2,1)} %refs_6_.2) | copy-start | bytes 1572868
  3.9 10.5 %copy-start.10 = (bf16[4,512]{1,0:T(4,128)(2,1)S(1)}, bf16[4,512]{1,0:T(4,128)(2,1)}, u32[]{:S(2)}) copy-start(bf16[4,512]{1,0:T(4,128)(2,1)} %refs_4_.3) | copy-start | bytes 12292
  3.9 7.9 %collective-permute-start = (bf16[288,512]{1,0:T(8,128)(2,1)S(1)}, bf16[288,512]{1,0:T(8,128)(2,1)S(1)}, u32[]{:S(2)}, u32[]{:S(2)}) collective-permute-start(bf16[288,512]{1,0:T(8,128)(2,1)S(1)} %get-tuple-element.39), channel_id=1, source_target_pairs={{0,8},{1,9},{2,10},{3,11},{4,12},{5,13},{6,14},{7,15},{8,0},{9,1},... | collective-permute-start | bytes 884744 | tf_op jit(solution)/shard_map/ppermute | solution.py:345
  4.4 9.0 %collective-permute-start.3 = (bf16[144,512]{1,0:T(8,128)(2,1)S(1)}, bf16[144,512]{1,0:T(8,128)(2,1)S(1)}, u32[]{:S(2)}, u32[]{:S(2)}) collective-permute-start(bf16[144,512]{1,0:T(8,128)(2,1)S(1)} %get-tuple-element.43), channel_id=1, source_target_pairs={{0,16},{1,17},{2,18},{3,19},{4,20},{5,21},{6,22},{7,23},{8,24},{9,... | collective-permute-start | bytes 442376 | tf_op jit(solution)/shard_map/ppermute | solution.py:345
  7.0 7.3 %collective-permute-start.4 = (bf16[144,512]{1,0:T(8,128)(2,1)S(1)}, bf16[144,512]{1,0:T(8,128)(2,1)S(1)}, u32[]{:S(2)}, u32[]{:S(2)}) collective-permute-start(bf16[144,512]{1,0:T(8,128)(2,1)S(1)} %get-tuple-element.44), channel_id=1, source_target_pairs={{0,24},{1,25},{2,26},{3,27},{4,28},{5,29},{6,30},{7,31},{8,16},{9,... | collective-permute-start | bytes 442376 | tf_op jit(solution)/shard_map/ppermute | solution.py:345
  7.1 14.0 %collective-permute-start.6 = (bf16[144,512]{1,0:T(8,128)(2,1)S(1)}, bf16[144,512]{1,0:T(8,128)(2,1)S(1)}, u32[]{:S(2)}, u32[]{:S(2)}) collective-permute-start(bf16[144,512]{1,0:T(8,128)(2,1)S(1)} %get-tuple-element.45), channel_id=1, source_target_pairs={{0,7},{1,0},{2,1},{3,2},{4,3},{5,4},{6,5},{7,6},{8,15},{9,8},{10,9... | collective-permute-start | bytes 442376 | tf_op jit(solution)/shard_map/ppermute | solution.py:345
  11.8 9.3 %collective-permute-start.7 = (bf16[144,512]{1,0:T(8,128)(2,1)S(1)}, bf16[144,512]{1,0:T(8,128)(2,1)S(1)}, u32[]{:S(2)}, u32[]{:S(2)}) collective-permute-start(bf16[144,512]{1,0:T(8,128)(2,1)S(1)} %get-tuple-element.46), channel_id=1, source_target_pairs={{0,1},{1,0},{2,3},{3,2},{4,5},{5,4},{6,7},{7,6},{8,9},{9,8},{10,11... | collective-permute-start | bytes 442376 | tf_op jit(solution)/shard_map/ppermute | solution.py:345
  11.9 10.9 %collective-permute-start.1 = (bf16[144,512]{1,0:T(8,128)(2,1)S(1)}, bf16[144,512]{1,0:T(8,128)(2,1)S(1)}, u32[]{:S(2)}, u32[]{:S(2)}) collective-permute-start(bf16[144,512]{1,0:T(8,128)(2,1)S(1)} %get-tuple-element.40), channel_id=1, source_target_pairs={{0,16},{1,17},{2,18},{3,19},{4,20},{5,21},{6,22},{7,23},{8,24},{9,... | collective-permute-start | bytes 442376 | tf_op jit(solution)/shard_map/ppermute | solution.py:345
  13.4 9.3 %collective-permute-start.2 = (bf16[144,512]{1,0:T(8,128)(2,1)S(1)}, bf16[144,512]{1,0:T(8,128)(2,1)S(1)}, u32[]{:S(2)}, u32[]{:S(2)}) collective-permute-start(bf16[144,512]{1,0:T(8,128)(2,1)S(1)} %get-tuple-element.41), channel_id=1, source_target_pairs={{0,24},{1,25},{2,26},{3,27},{4,28},{5,29},{6,30},{7,31},{8,16},{9,... | collective-permute-start | bytes 442376 | tf_op jit(solution)/shard_map/ppermute | solution.py:345
  16.5 8.8 %collective-permute-start.5 = (bf16[144,512]{1,0:T(8,128)(2,1)S(1)}, bf16[144,512]{1,0:T(8,128)(2,1)S(1)}, u32[]{:S(2)}, u32[]{:S(2)}) collective-permute-start(bf16[144,512]{1,0:T(8,128)(2,1)S(1)} %aggregate.2.refs_7_.refs_2_), channel_id=1, source_target_pairs={{0,7},{1,0},{2,1},{3,2},{4,3},{5,4},{6,5},{7,6},{8,15},{9,8},{10,9... | collective-permute-start | bytes 442376 | tf_op jit(solution)/shard_map/ppermute | solution.py:345
  21.1 9.7 %collective-permute-start.12 = (bf16[288,512]{1,0:T(8,128)(2,1)S(1)}, bf16[288,512]{1,0:T(8,128)(2,1)S(1)}, u32[]{:S(2)}, u32[]{:S(2)}) collective-permute-start(bf16[288,512]{1,0:T(8,128)(2,1)S(1)} %join.2.refs_6_), channel_id=1, source_target_pairs={{0,16},{1,17},{2,18},{3,19},{4,20},{5,21},{6,22},{7,23},{8,24},{9,... | collective-permute-start | bytes 884744 | tf_op jit(solution)/shard_map/ppermute | solution.py:345
  25.3 5.6 %copy-start = (bf16[512,2048]{1,0:T(8,128)(2,1)S(1)}, bf16[512,2048]{1,0:T(8,128)(2,1)}, u32[]{:S(2)}) copy-start(bf16[512,2048]{1,0:T(8,128)(2,1)} %refs_5_.7) | copy-start | bytes 6291460
  28.0 14.1 %collective-permute-start.10 = (bf16[288,512]{1,0:T(8,128)(2,1)S(1)}, bf16[288,512]{1,0:T(8,128)(2,1)S(1)}, u32[]{:S(2)}, u32[]{:S(2)}) collective-permute-start(bf16[288,512]{1,0:T(8,128)(2,1)S(1)} %window.1.refs_0_), channel_id=1, source_target_pairs={{0,1},{1,0},{2,3},{3,2},{4,5},{5,4},{6,7},{7,6},{8,9},{9,8},{10,11... | collective-permute-start | bytes 884744 | tf_op jit(solution)/shard_map/ppermute | solution.py:345
  28.0 14.6 %collective-permute-start.8 = (bf16[288,512]{1,0:T(8,128)(2,1)S(1)}, bf16[288,512]{1,0:T(8,128)(2,1)S(1)}, u32[]{:S(2)}, u32[]{:S(2)}) collective-permute-start(bf16[288,512]{1,0:T(8,128)(2,1)S(1)} %window.1.refs_0_), channel_id=1, source_target_pairs={{0,16},{1,17},{2,18},{3,19},{4,20},{5,21},{6,22},{7,23},{8,24},{9,... | collective-permute-start | bytes 884744 | tf_op jit(solution)/shard_map/ppermute | solution.py:345
  33.3 13.7 %collective-permute-start.13 = (bf16[288,512]{1,0:T(8,128)(2,1)S(1)}, bf16[288,512]{1,0:T(8,128)(2,1)S(1)}, u32[]{:S(2)}, u32[]{:S(2)}) collective-permute-start(bf16[288,512]{1,0:T(8,128)(2,1)S(1)} %copy.19.refs_4_), channel_id=1, source_target_pairs={{0,6},{1,1},{2,0},{3,3},{4,2},{5,5},{6,4},{7,7},{8,14},{9,9},{10,8... | collective-permute-start | bytes 884744 | tf_op jit(solution)/shard_map/ppermute | solution.py:345
  42.1 8.5 %collective-permute-start.11 = (bf16[144,512]{1,0:T(8,128)(2,1)S(1)}, bf16[144,512]{1,0:T(8,128)(2,1)S(1)}, u32[]{:S(2)}, u32[]{:S(2)}) collective-permute-start(bf16[144,512]{1,0:T(8,128)(2,1)S(1)} %slice.9), channel_id=1, source_target_pairs={{0,16},{1,17},{2,18},{3,19},{4,20},{5,21},{6,22},{7,23},{8,24},{9,... | collective-permute-start | bytes 442376 | tf_op jit(solution)/shard_map/ppermute | solution.py:345
  42.6 7.9 %collective-permute-start.9 = (bf16[144,512]{1,0:T(8,128)(2,1)S(1)}, bf16[144,512]{1,0:T(8,128)(2,1)S(1)}, u32[]{:S(2)}, u32[]{:S(2)}) collective-permute-start(bf16[144,512]{1,0:T(8,128)(2,1)S(1)} %slice.8), channel_id=1, source_target_pairs={{0,1},{1,0},{2,3},{3,2},{4,5},{5,4},{6,7},{7,6},{8,9},{9,8},{10,11... | collective-permute-start | bytes 442376 | tf_op jit(solution)/shard_map/ppermute | solution.py:345
  44.9 10.7 %collective-permute-start.15 = (bf16[288,512]{1,0:T(8,128)(2,1)S(1)}, bf16[288,512]{1,0:T(8,128)(2,1)S(1)}, u32[]{:S(2)}, u32[]{:S(2)}) collective-permute-start(bf16[288,512]{1,0:T(8,128)(2,1)S(1)} %join.3), channel_id=1, source_target_pairs={{0,1},{1,2},{2,3},{3,4},{4,5},{5,6},{6,7},{7,0},{8,9},{9,10},{10,1... | collective-permute-start | bytes 884744 | tf_op jit(solution)/shard_map/ppermute | solution.py:345
  53.3 2.4 %collective-permute-start.14 = (bf16[256,1024]{1,0:T(8,128)(2,1)S(1)}, bf16[256,1024]{1,0:T(8,128)(2,1)S(1)}, u32[]{:S(2)}, u32[]{:S(2)}) collective-permute-start(bf16[256,1024]{1,0:T(8,128)(2,1)S(1)} %get-tuple-element.55.refs_3_), channel_id=1, source_target_pairs={{0,8},{1,9},{2,10},{3,11},{4,12},{5,13},{6,14},{7,15},{8,0},{9,1},... | collective-permute-start | bytes 1572872 | tf_op jit(solution)/shard_map/ppermute | solution.py:345
  55.9 4.5 %collective-permute-start.16 = (bf16[576,512]{1,0:T(8,128)(2,1)S(1)}, bf16[576,512]{1,0:T(8,128)(2,1)S(1)}, u32[]{:S(2)}, u32[]{:S(2)}) collective-permute-start(bf16[576,512]{1,0:T(8,128)(2,1)S(1)} %get-tuple-element.58.own), channel_id=1, source_target_pairs={{0,8},{1,9},{2,10},{3,11},{4,12},{5,13},{6,14},{7,15},{8,0},{9,1},... | collective-permute-start | bytes 1769480 | tf_op jit(solution)/shard_map/ppermute | solution.py:345
  56.0 8.3 %collective-permute-start.17 = (bf16[256,256]{1,0:T(8,128)(2,1)S(1)}, bf16[256,256]{1,0:T(8,128)(2,1)S(1)}, u32[]{:S(2)}, u32[]{:S(2)}) collective-permute-start(bf16[256,256]{1,0:T(8,128)(2,1)S(1)} %get-tuple-element.61), channel_id=1, source_target_pairs={{0,2},{1,3},{2,0},{3,1},{4,6},{5,7},{6,4},{7,5},{8,10},{9,11},{10,... | collective-permute-start | bytes 393224 | tf_op jit(solution)/shard_map/ppermute | solution.py:345
  56.0 13.1 %collective-permute-start.18 = (bf16[256,256]{1,0:T(8,128)(2,1)S(1)}, bf16[256,256]{1,0:T(8,128)(2,1)S(1)}, u32[]{:S(2)}, u32[]{:S(2)}) collective-permute-start(bf16[256,256]{1,0:T(8,128)(2,1)S(1)} %get-tuple-element.62), channel_id=1, source_target_pairs={{0,4},{1,5},{2,6},{3,7},{4,0},{5,1},{6,2},{7,3},{8,12},{9,13},{10,... | collective-permute-start | bytes 393224 | tf_op jit(solution)/shard_map/ppermute | solution.py:345
  59.2 10.0 %collective-permute-start.19 = (bf16[256,256]{1,0:T(8,128)(2,1)S(1)}, bf16[256,256]{1,0:T(8,128)(2,1)S(1)}, u32[]{:S(2)}, u32[]{:S(2)}) collective-permute-start(bf16[256,256]{1,0:T(8,128)(2,1)S(1)} %get-tuple-element.63), channel_id=1, source_target_pairs={{0,6},{1,7},{2,4},{3,5},{4,2},{5,3},{6,0},{7,1},{8,14},{9,15},{10,... | collective-permute-start | bytes 393224 | tf_op jit(solution)/shard_map/ppermute | solution.py:345
  (9 other events, 25.1 us)

commit v4 on v3

--- a/solution.py
+++ b/solution.py
@@ -73,14 +73,13 @@
     return pltpu.roll(cells, cells.shape[0] - WA // 2, 0)
 
 
-def pack_levels_body(lev_count, mask_ref, lev_ref, *refs):
+def pack_levels_body(lev_count, lev_ref, *refs):
     outs, core_ref, blocks = refs[:-2], refs[-2], refs[-1]
     count = lev_ref.shape[0]
     me = lax.axis_index("lev")
     for j in range(count):
-        live = jnp.broadcast_to(mask_ref[:, j : j + 1] > 0, lev_ref.shape[2:])
         for o in range(WO):
-            cells = lat_rolled(jnp.where(live, lev_ref[j, o].astype(F32), MARK))
+            cells = lat_rolled(lev_ref[j, o].astype(F32))
             half, at = 1 - o // HALF, j * PIECE + (o % HALF) * WA
             for i in range(lev_count):
                 blocks[half * lev_count + i, pl.ds(at, WA)] = cells[i * WA : (i + 1) * WA]
@@ -246,8 +245,8 @@
     backs = jnp.concatenate(backs, 0)
     normed[...] = rows
     n_half[...] = normed[:, half_at]
-    n_half_v = n_half[...]
-    c_half_v = c_half[...]
+    n_half_v = n_half[...].T
+    c_half_v = c_half[...].T
     picked = w_up.shape[1] != cols
     step = part if picked else 256
     parity = lax.rem(lax.axis_index("tile"), 2)
@@ -261,8 +260,8 @@
         active = (x * cdf).astype(BF16)
         slope = (0.5 * 0.7978845608028654) + (1.5 * 0.7978845608028654 * 0.044715) * square
         dinner = (back * (cdf + x * ((1.0 - t * t) * slope))).astype(BF16)
-        up = dot(n_half_v, dinner, ((0,), (0,)))
-        dn = dot(c_half_v, active, ((0,), (0,)))
+        up = dot(n_half_v, dinner)
+        dn = dot(c_half_v, active)
         acc_up[:, at] = up + sum_up[:, at] if adds else up
         acc_dn[:, at] = dn + sum_dn[:, at] if adds else dn
     if last:
@@ -285,8 +284,8 @@
         blocks[n] = keep[:, at] + recv[:, at].astype(F32)
     me = lax.axis_index("tile") // 2
     own_ref[...] = blocks[me]
-    for d in range(1, groups):
-        outs[d - 1][...] = blocks[me ^ d].astype(BF16)
+    for n, d in enumerate(range(groups - 1, 0, -1)):
+        outs[n][...] = blocks[me ^ d].astype(BF16)
 
 
 def total_body(own, *refs):
@@ -377,31 +376,31 @@
     peer = lambda t: t ^ 1
     next_pair = lambda t: (t - 2) % tiles if t % 2 == 0 else t
 
+    marked = jnp.where((level_mask > 0)[:, None, None, None], levels, MARK).astype(BF16)
+    marked = marked.transpose(0, 2, 1, 3)
+    *pieces, core = call(
+        functools.partial(pack_levels_body, levs),
+        (marked,),
+        [((piece, width), BF16)] * 6 + [((2 * piece, width), BF16)],
+        [pltpu.VMEM((2 * levs, piece, width), F32)],
+        us=0.7,
+    )
     cot_east, cot_west, cot_east_own, cot_west_own = call(
         functools.partial(pack_cot_body, levs),
         (cotangent.transpose(0, 2, 1, 3),),
         [((window, width), BF16)] * 2 + [((rows, width), BF16)] * 2,
         [pltpu.VMEM((2 * levs, rows, width), F32)],
+        after=pieces[0],
         us=0.5,
     )
     cot_peer_e = exchanged(cot_east_own, 0, peer)
     cot_own_w = exchanged(cot_west_own, 0, west)
-    *pieces, core = call(
-        functools.partial(pack_levels_body, levs),
-        (level_mask[None], levels.transpose(0, 2, 1, 3)),
-        [((piece, width), BF16)] * 6 + [((2 * piece, width), BF16)],
-        [pltpu.VMEM((2 * levs, piece, width), F32)],
-        after=cot_east,
-        us=0.7,
-    )
     core = exchanged(core, 1, same)
+    west_raw = (pieces[3], exchanged(pieces[4], 2, same), exchanged(pieces[5], 3, same), core)
     pieces[1:3] = call(
-        copy_body, pieces[1:3], [((piece, width), BF16)] * 2, vmem=8, after=core
-    )
-    east_raw, west_raw = [
-        (own, exchanged(beside, 2, same), exchanged(far, 3, same), core)
-        for own, beside, far in (pieces[:3], pieces[3:])
-    ]
+        copy_body, pieces[1:3], [((piece, width), BF16)] * 2, vmem=8, after=(core, west_raw[2])
+    )
+    east_raw = (pieces[0], exchanged(pieces[1], 2, same), exchanged(pieces[2], 3, same), core)
     aggregated = lambda half, chunks, after: call(
         functools.partial(aggregate_body, half),
         (*chunks, latent_query, w_key, w_value),
@@ -520,7 +519,8 @@
         vmem=32,
     )
     received = [
-        exchanged(block, 0, lambda t, d=d: t ^ (2 * d)) for d, block in enumerate(sends, 1)
+        exchanged(block, 0, lambda t, d=d: t ^ (2 * d))
+        for d, block in zip(range(groups - 1, 0, -1), sends)
     ]
     core_rows = exchanged(chip_rows, 1, same)
     encoded, mark = call(

time: 70.1 us -> 68.3 us (0.974)
  waiting for transfers between devices: 12 us -> 9.41 us
  other arithmetic: 0 us -> 2.11 us
  local copies, waits for them, and re-layouts: 2.11 us -> 0.09 us
  starting transfers between devices: 31.2 us -> 32 us
    ppermute x20, waiting for transfers between devices: 12 us -> 9.41 us  [exchanged(): return lax.ppermute(block, ('lev', 'tile'), route)]
    unnamed x26 -> x22, local copies, waits for them, and re-layouts: 2.09 us -> 0.07 us
    transpose x0 -> x1, other arithmetic: none -> 1.45 us  [per_device(): marked = marked.transpose(0, 2, 1, 3)]
    ppermute x20, starting transfers between devices: 31.2 us -> 32 us  [exchanged(): return lax.ppermute(block, ('lev', 'tile'), route)]
  transfers between devices with their start and end apart: 20 -> 20, of which waited for: 6 -> 5; matrix products, arithmetic and copies ran while one was open for 0% -> 0% of each run, Pallas kernels for 31% -> 32%
where the time goes in v4:
time: 68.3 us; the launch traced here: 68.1 us
  starting transfers between devices  32 us (47%)
  Pallas kernels  23.5 us (34%)
  waiting for transfers between devices  9.41 us (14%)
  other arithmetic  2.11 us (3%)
  between operations  0.95 us (1%)
    ppermute x20, starting transfers between devices, exchanged(): return lax.ppermute(block, ('lev', 'tile'), route)  32 us
    pallas_call x18, Pallas kernels, call(): pl.pallas_call(body, out_shape=[jax.ShapeDtypeStruct(shape, dtype) for sh...  23.5 us
    ppermute x20, waiting for transfers between devices, exchanged(): return lax.ppermute(block, ('lev', 'tile'), route)  9.41 us
    transpose x1, other arithmetic, per_device(): marked = marked.transpose(0, 2, 1, 3)  1.45 us
  transfers between devices with their start and end apart: 20, of which 5 were waited for; matrix products, arithmetic and copies ran while one was open for 0% of the time, Pallas kernels for 32%

profile of v4, /device:TPU:0, one launch (start us, length us, event | category | flops | bytes accessed | tf_op | source)
XLA Modules:
  0.0 68.1 jit_solution(12324237927005834772)
XLA Ops:
  1.3 1.4 %select_bitcast_fusion.lev_ref = bf16[4,12,24,512]{3,2,1,0:T(8,128)(2,1)S(1)} fusion(bf16[4,24,12,512]{3,1,2,0:T(8,128)(2,1)} %param.13, pred[4]{0:T(512)(128)(4,1)S(1)} %broadcast_compare_fusion), kind=kLoop, calls=%fused_computation | loop fusion | flops 589824 | bytes 2359300 | tf_op jit(solution)/shard_map/transpose | solution.py:380
  3.8 2.6 %collective-permute-start.1 = (bf16[144,512]{1,0:T(8,128)(2,1)S(1)}, bf16[144,512]{1,0:T(8,128)(2,1)S(1)}, u32[]{:S(2)}, u32[]{:S(2)}) collective-permute-start(bf16[144,512]{1,0:T(8,128)(2,1)S(1)} %get-tuple-element.39), channel_id=1, source_target_pairs={{0,24},{1,25},{2,26},{3,27},{4,28},{5,29},{6,30},{7,31},{8,16},{9,... | collective-permute-start | bytes 442376 | tf_op jit(solution)/shard_map/ppermute | solution.py:344
  7.1 5.0 %collective-permute-start.6 = (bf16[144,512]{1,0:T(8,128)(2,1)S(1)}, bf16[144,512]{1,0:T(8,128)(2,1)S(1)}, u32[]{:S(2)}, u32[]{:S(2)}) collective-permute-start(bf16[144,512]{1,0:T(8,128)(2,1)S(1)} %get-tuple-element.44), channel_id=1, source_target_pairs={{0,7},{1,0},{2,1},{3,2},{4,3},{5,4},{6,5},{7,6},{8,15},{9,8},{10,9... | collective-permute-start | bytes 442376 | tf_op jit(solution)/shard_map/ppermute | solution.py:344
  12.1 1.6 %collective-permute-start.2 = (bf16[144,512]{1,0:T(8,128)(2,1)S(1)}, bf16[144,512]{1,0:T(8,128)(2,1)S(1)}, u32[]{:S(2)}, u32[]{:S(2)}) collective-permute-start(bf16[144,512]{1,0:T(8,128)(2,1)S(1)} %get-tuple-element.40), channel_id=1, source_target_pairs={{0,16},{1,17},{2,18},{3,19},{4,20},{5,21},{6,22},{7,23},{8,24},{9,... | collective-permute-start | bytes 442376 | tf_op jit(solution)/shard_map/ppermute | solution.py:344
  14.0 2.1 %aggregate.2.refs_7_.refs_2_ = bf16[144,512]{1,0:T(8,128)(2,1)S(1)} custom-call(bf16[144,512]{1,0:T(8,128)(2,1)S(1)} %get-tuple-element.42.own, bf16[144,512]{1,0:T(8,128)(2,1)S(1)} %collective-permute-done.4.beside, bf16[144,512]{1,0:T(8,128)(2,1)S(1)} %collective-permute-done.1.refs_3_.far, bf16[288,512]{1,0:T(8,128)(2,1)S(1)} %collective-permute-done.refs_2_.core.refs_3_, ...), custom_call_target="tpu_custom_call" | custom-call | flops 6300000256 | tf_op jit(solution)/shard_map/aggregate/pallas_call | solution.py:45
  16.2 4.8 %collective-permute-start.5 = (bf16[144,512]{1,0:T(8,128)(2,1)S(1)}, bf16[144,512]{1,0:T(8,128)(2,1)S(1)}, u32[]{:S(2)}, u32[]{:S(2)}) collective-permute-start(bf16[144,512]{1,0:T(8,128)(2,1)S(1)} %aggregate.2.refs_7_.refs_2_), channel_id=1, source_target_pairs={{0,7},{1,0},{2,1},{3,2},{4,3},{5,4},{6,5},{7,6},{8,15},{9,8},{10,9... | collective-permute-start | bytes 442376 | tf_op jit(solution)/shard_map/ppermute | solution.py:344
  21.0 1.6 %collective-permute-start.12 = (bf16[288,512]{1,0:T(8,128)(2,1)S(1)}, bf16[288,512]{1,0:T(8,128)(2,1)S(1)}, u32[]{:S(2)}, u32[]{:S(2)}) collective-permute-start(bf16[288,512]{1,0:T(8,128)(2,1)S(1)} %join.2.refs_6_), channel_id=1, source_target_pairs={{0,16},{1,17},{2,18},{3,19},{4,20},{5,21},{6,22},{7,23},{8,24},{9,... | collective-permute-start | bytes 884744 | tf_op jit(solution)/shard_map/ppermute | solution.py:344
  22.6 2.1 %aggregate.3.refs_0_ = bf16[144,512]{1,0:T(8,128)(2,1)S(1)} custom-call(bf16[144,512]{1,0:T(8,128)(2,1)S(1)} %get-tuple-element.35.refs_0_.refs_1_, bf16[144,512]{1,0:T(8,128)(2,1)S(1)} %collective-permute-done.2.refs_1_, bf16[144,512]{1,0:T(8,128)(2,1)S(1)} %collective-permute-done.3.refs_2_, ...), custom_call_target="tpu_custom_call" | custom-call | flops 6300000256 | tf_op jit(solution)/shard_map/aggregate/pallas_call | solution.py:45
  24.8 2.6 %window.1.refs_0_ = bf16[288,512]{1,0:T(8,128)(2,1)S(1)} custom-call(bf16[144,512]{1,0:T(8,128)(2,1)S(1)} %aggregate.3.refs_0_, bf16[144,512]{1,0:T(8,128)(2,1)S(1)} %collective-permute-done.5.refs_1_, bf16[512,512]{1,0:T(8,128)(2,1)S(1)} %copy-done.7, f32[1,512]{1,0:T(1,128)S(1)} %bitcast.12, bf16[512,1536]{1,0:T(8,128)(2,1)S(1)} %copy-done.3, ...), custom_call_target="tpu_custom_call" | custom-call | flops 8999999488 | tf_op jit(solution)/shard_map/window/pallas_call | solution.py:45
  28.0 1.5 %collective-permute-start.8 = (bf16[288,512]{1,0:T(8,128)(2,1)S(1)}, bf16[288,512]{1,0:T(8,128)(2,1)S(1)}, u32[]{:S(2)}, u32[]{:S(2)}) collective-permute-start(bf16[288,512]{1,0:T(8,128)(2,1)S(1)} %window.1.refs_0_), channel_id=1, source_target_pairs={{0,16},{1,17},{2,18},{3,19},{4,20},{5,21},{6,22},{7,23},{8,24},{9,... | collective-permute-start | bytes 884744 | tf_op jit(solution)/shard_map/ppermute | solution.py:344
  29.5 2.4 %grad.3 = (f32[256,1024]{1,0:T(8,128)S(1)}, f32[256,1024]{1,0:T(8,128)S(1)}) custom-call(bf16[288,512]{1,0:T(8,128)(2,1)S(1)} %window.1.refs_0_, bf16[288,512]{1,0:T(8,128)(2,1)S(1)} %get-tuple-element.47.refs_1_.refs_2_, bf16[144,512]{1,0:T(8,128)(2,1)S(1)} %collective-permute-done.6.refs_0_.refs_2_, f32[1,512]{1,0:T(1,128)S(1)} %bitcast.6, ...), custom_call_target="tpu_custom_call" | custom-call | flops 6600000000 | tf_op jit(solution)/shard_map/grad/pallas_call | solution.py:45
  31.9 6.4 %collective-permute-start.13 = (bf16[288,512]{1,0:T(8,128)(2,1)S(1)}, bf16[288,512]{1,0:T(8,128)(2,1)S(1)}, u32[]{:S(2)}, u32[]{:S(2)}) collective-permute-start(bf16[288,512]{1,0:T(8,128)(2,1)S(1)} %copy.19.refs_4_), channel_id=1, source_target_pairs={{0,6},{1,1},{2,0},{3,3},{4,2},{5,5},{6,4},{7,7},{8,14},{9,9},{10,8... | collective-permute-start | bytes 884744 | tf_op jit(solution)/shard_map/ppermute | solution.py:344
  38.3 2.2 %mlp.2 = (bf16[144,512]{1,0:T(8,128)(2,1)S(1)}, bf16[144,512]{1,0:T(8,128)(2,1)S(1)}) custom-call(bf16[288,512]{1,0:T(8,128)(2,1)S(1)} %window.1.refs_0_, f32[1,512]{1,0:T(1,128)S(1)} %bitcast.7, bf16[512,2048]{1,0:T(8,128)(2,1)S(1)} %copy-done, bf16[2048,512]{1,0:T(8,128)(2,1)S(1)} %copy-done.1, bf16[288,512]{1,0:T(8,128)(2,1)S(1)} %copy.19.refs_4_), custom_call_target="tpu_custom_call" | custom-call | flops 6000000000 | tf_op jit(solution)/shard_map/mlp/pallas_call | solution.py:45
  41.2 2.2 %mlp.3 = (bf16[144,512]{1,0:T(8,128)(2,1)S(1)}, bf16[144,512]{1,0:T(8,128)(2,1)S(1)}) custom-call(bf16[288,512]{1,0:T(8,128)(2,1)S(1)} %collective-permute-done.8.refs_0_, f32[1,512]{1,0:T(1,128)S(1)} %bitcast.8, bf16[512,2048]{1,0:T(8,128)(2,1)S(1)} %copy-done, bf16[2048,512]{1,0:T(8,128)(2,1)S(1)} %copy-done.1, ...), custom_call_target="tpu_custom_call" | custom-call | flops 8999999488 | tf_op jit(solution)/shard_map/mlp/pallas_call | solution.py:45
  43.4 2.1 %collective-permute-start.15 = (bf16[288,512]{1,0:T(8,128)(2,1)S(1)}, bf16[288,512]{1,0:T(8,128)(2,1)S(1)}, u32[]{:S(2)}, u32[]{:S(2)}) collective-permute-start(bf16[288,512]{1,0:T(8,128)(2,1)S(1)} %join.3), channel_id=1, source_target_pairs={{0,1},{1,2},{2,3},{3,4},{4,5},{5,6},{6,7},{7,0},{8,9},{9,10},{10,1... | collective-permute-start | bytes 884744 | tf_op jit(solution)/shard_map/ppermute | solution.py:344
  45.4 3.5 %grad.4 = (f32[256,1024]{1,0:T(8,128)S(1)}, f32[256,1024]{1,0:T(8,128)S(1)}) custom-call(bf16[288,512]{1,0:T(8,128)(2,1)S(1)} %collective-permute-done.8.refs_0_, bf16[288,512]{1,0:T(8,128)(2,1)S(1)} %collective-permute-done.10.refs_5_.refs_1_, bf16[288,512]{1,0:T(8,128)(2,1)S(1)} %get-tuple-element.47.refs_1_.refs_2_, ...), custom_call_target="tpu_custom_call" | custom-call | flops 150000000 | tf_op jit(solution)/shard_map/grad/pallas_call | solution.py:45
  49.0 2.7 %grad.5 = (bf16[256,1024]{1,0:T(8,128)(2,1)S(1)}, f32[256,1024]{1,0:T(8,128)S(1)}) custom-call(bf16[144,512]{1,0:T(8,128)(2,1)S(1)} %collective-permute-done.9.refs_0_, bf16[144,512]{1,0:T(8,128)(2,1)S(1)} %collective-permute-done.11.refs_1_, bf16[288,512]{1,0:T(8,128)(2,1)S(1)} %collective-permute-done.12.refs_6_.refs_3_.refs_2_, ...), custom_call_target="tpu_custom_call" | custom-call | flops 7800000000 | tf_op jit(solution)/shard_map/grad/pallas_call | solution.py:45
  51.8 1.1 %collective-permute-done.15.refs_2_ = bf16[288,512]{1,0:T(8,128)(2,1)S(1)} collective-permute-done((bf16[288,512]{1,0:T(8,128)(2,1)S(1)}, bf16[288,512]{1,0:T(8,128)(2,1)S(1)}, u32[]{:S(2)}, u32[]{:S(2)}) %collective-permute-start.15) | collective-permute-done | bytes 294944 | tf_op jit(solution)/shard_map/ppermute | solution.py:344
  52.9 0.8 %collective-permute-done.14.recv = bf16[256,1024]{1,0:T(8,128)(2,1)S(1)} collective-permute-done((bf16[256,1024]{1,0:T(8,128)(2,1)S(1)}, bf16[256,1024]{1,0:T(8,128)(2,1)S(1)}, u32[]{:S(2)}, u32[]{:S(2)}) %collective-permute-start.14) | collective-permute-done | bytes 524320 | tf_op jit(solution)/shard_map/ppermute | solution.py:344
  54.1 3.6 %collective-permute-start.17 = (bf16[256,256]{1,0:T(8,128)(2,1)S(1)}, bf16[256,256]{1,0:T(8,128)(2,1)S(1)}, u32[]{:S(2)}, u32[]{:S(2)}) collective-permute-start(bf16[256,256]{1,0:T(8,128)(2,1)S(1)} %get-tuple-element.61), channel_id=1, source_target_pairs={{0,6},{1,7},{2,4},{3,5},{4,2},{5,3},{6,0},{7,1},{8,14},{9,15},{10,... | collective-permute-start | bytes 393224 | tf_op jit(solution)/shard_map/ppermute | solution.py:344
  57.7 0.8 %collective-permute-start.19 = (bf16[256,256]{1,0:T(8,128)(2,1)S(1)}, bf16[256,256]{1,0:T(8,128)(2,1)S(1)}, u32[]{:S(2)}, u32[]{:S(2)}) collective-permute-start(bf16[256,256]{1,0:T(8,128)(2,1)S(1)} %get-tuple-element.63), channel_id=1, source_target_pairs={{0,2},{1,3},{2,0},{3,1},{4,6},{5,7},{6,4},{7,5},{8,10},{9,11},{10,... | collective-permute-start | bytes 393224 | tf_op jit(solution)/shard_map/ppermute | solution.py:344
  58.5 1.6 %unpack.1 = (bf16[4,12,24,512]{3,2,1,0:T(8,128)(2,1)}, f32[8,128]{1,0:T(8,128)S(1)}) custom-call(bf16[576,512]{1,0:T(8,128)(2,1)S(1)} %get-tuple-element.58.own, bf16[576,512]{1,0:T(8,128)(2,1)S(1)} %collective-permute-done.16.core), custom_call_target="tpu_custom_call" | custom-call | flops 4800000000 | tf_op jit(solution)/shard_map/unpack/pallas_call | solution.py:45
  60.1 2.2 %collective-permute-done.17.refs_1_ = bf16[256,256]{1,0:T(8,128)(2,1)S(1)} collective-permute-done((bf16[256,256]{1,0:T(8,128)(2,1)S(1)}, bf16[256,256]{1,0:T(8,128)(2,1)S(1)}, u32[]{:S(2)}, u32[]{:S(2)}) %collective-permute-start.17) | collective-permute-done | bytes 131104 | tf_op jit(solution)/shard_map/ppermute | solution.py:344
  62.3 5.0 %collective-permute-done.18.refs_2_ = bf16[256,256]{1,0:T(8,128)(2,1)S(1)} collective-permute-done((bf16[256,256]{1,0:T(8,128)(2,1)S(1)}, bf16[256,256]{1,0:T(8,128)(2,1)S(1)}, u32[]{:S(2)}, u32[]{:S(2)}) %collective-permute-start.18) | collective-permute-done | bytes 131104 | tf_op jit(solution)/shard_map/ppermute | solution.py:344
  (60 shorter events, 5.2 us)
Async XLA Ops:
  3.3 8.8 %collective-permute-start = (bf16[288,512]{1,0:T(8,128)(2,1)S(1)}, bf16[288,512]{1,0:T(8,128)(2,1)S(1)}, u32[]{:S(2)}, u32[]{:S(2)}) collective-permute-start(bf16[288,512]{1,0:T(8,128)(2,1)S(1)} %get-tuple-element.38), channel_id=1, source_target_pairs={{0,8},{1,9},{2,10},{3,11},{4,12},{5,13},{6,14},{7,15},{8,0},{9,1},... | collective-permute-start | bytes 884744 | tf_op jit(solution)/shard_map/ppermute | solution.py:344
  3.8 8.3 %collective-permute-start.1 = (bf16[144,512]{1,0:T(8,128)(2,1)S(1)}, bf16[144,512]{1,0:T(8,128)(2,1)S(1)}, u32[]{:S(2)}, u32[]{:S(2)}) collective-permute-start(bf16[144,512]{1,0:T(8,128)(2,1)S(1)} %get-tuple-element.39), channel_id=1, source_target_pairs={{0,24},{1,25},{2,26},{3,27},{4,28},{5,29},{6,30},{7,31},{8,16},{9,... | collective-permute-start | bytes 442376 | tf_op jit(solution)/shard_map/ppermute | solution.py:344
  6.5 7.6 %collective-permute-start.4 = (bf16[144,512]{1,0:T(8,128)(2,1)S(1)}, bf16[144,512]{1,0:T(8,128)(2,1)S(1)}, u32[]{:S(2)}, u32[]{:S(2)}) collective-permute-start(bf16[144,512]{1,0:T(8,128)(2,1)S(1)} %get-tuple-element.43), channel_id=1, source_target_pairs={{0,16},{1,17},{2,18},{3,19},{4,20},{5,21},{6,22},{7,23},{8,24},{9,... | collective-permute-start | bytes 442376 | tf_op jit(solution)/shard_map/ppermute | solution.py:344
  7.0 7.0 %copy-start.5 = (bf16[512,512]{1,0:T(8,128)(2,1)S(1)}, bf16[512,512]{1,0:T(8,128)(2,1)}, u32[]{:S(2)}) copy-start(bf16[512,512]{1,0:T(8,128)(2,1)} %refs_5_.4) | copy-start | bytes 1572868
  7.0 7.0 %copy-start.6 = (bf16[512,512]{1,0:T(8,128)(2,1)S(1)}, bf16[512,512]{1,0:T(8,128)(2,1)}, u32[]{:S(2)}) copy-start(bf16[512,512]{1,0:T(8,128)(2,1)} %refs_6_.2) | copy-start | bytes 1572868
  7.0 7.0 %copy-start.9 = (bf16[4,512]{1,0:T(4,128)(2,1)S(1)}, bf16[4,512]{1,0:T(4,128)(2,1)}, u32[]{:S(2)}) copy-start(bf16[4,512]{1,0:T(4,128)(2,1)} %refs_4_.3) | copy-start | bytes 12292
  7.1 13.9 %collective-permute-start.6 = (bf16[144,512]{1,0:T(8,128)(2,1)S(1)}, bf16[144,512]{1,0:T(8,128)(2,1)S(1)}, u32[]{:S(2)}, u32[]{:S(2)}) collective-permute-start(bf16[144,512]{1,0:T(8,128)(2,1)S(1)} %get-tuple-element.44), channel_id=1, source_target_pairs={{0,7},{1,0},{2,1},{3,2},{4,3},{5,4},{6,5},{7,6},{8,15},{9,8},{10,9... | collective-permute-start | bytes 442376 | tf_op jit(solution)/shard_map/ppermute | solution.py:344
  12.1 8.8 %collective-permute-start.7 = (bf16[144,512]{1,0:T(8,128)(2,1)S(1)}, bf16[144,512]{1,0:T(8,128)(2,1)S(1)}, u32[]{:S(2)}, u32[]{:S(2)}) collective-permute-start(bf16[144,512]{1,0:T(8,128)(2,1)S(1)} %get-tuple-element.45), channel_id=1, source_target_pairs={{0,1},{1,0},{2,3},{3,2},{4,5},{5,4},{6,7},{7,6},{8,9},{9,8},{10,11... | collective-permute-start | bytes 442376 | tf_op jit(solution)/shard_map/ppermute | solution.py:344
  12.1 10.5 %collective-permute-start.2 = (bf16[144,512]{1,0:T(8,128)(2,1)S(1)}, bf16[144,512]{1,0:T(8,128)(2,1)S(1)}, u32[]{:S(2)}, u32[]{:S(2)}) collective-permute-start(bf16[144,512]{1,0:T(8,128)(2,1)S(1)} %get-tuple-element.40), channel_id=1, source_target_pairs={{0,16},{1,17},{2,18},{3,19},{4,20},{5,21},{6,22},{7,23},{8,24},{9,... | collective-permute-start | bytes 442376 | tf_op jit(solution)/shard_map/ppermute | solution.py:344
  13.7 8.9 %collective-permute-start.3 = (bf16[144,512]{1,0:T(8,128)(2,1)S(1)}, bf16[144,512]{1,0:T(8,128)(2,1)S(1)}, u32[]{:S(2)}, u32[]{:S(2)}) collective-permute-start(bf16[144,512]{1,0:T(8,128)(2,1)S(1)} %get-tuple-element.41), channel_id=1, source_target_pairs={{0,24},{1,25},{2,26},{3,27},{4,28},{5,29},{6,30},{7,31},{8,16},{9,... | collective-permute-start | bytes 442376 | tf_op jit(solution)/shard_map/ppermute | solution.py:344
  16.2 8.6 %collective-permute-start.5 = (bf16[144,512]{1,0:T(8,128)(2,1)S(1)}, bf16[144,512]{1,0:T(8,128)(2,1)S(1)}, u32[]{:S(2)}, u32[]{:S(2)}) collective-permute-start(bf16[144,512]{1,0:T(8,128)(2,1)S(1)} %aggregate.2.refs_7_.refs_2_), channel_id=1, source_target_pairs={{0,7},{1,0},{2,1},{3,2},{4,3},{5,4},{6,5},{7,6},{8,15},{9,8},{10,9... | collective-permute-start | bytes 442376 | tf_op jit(solution)/shard_map/ppermute | solution.py:344
  21.0 8.5 %collective-permute-start.12 = (bf16[288,512]{1,0:T(8,128)(2,1)S(1)}, bf16[288,512]{1,0:T(8,128)(2,1)S(1)}, u32[]{:S(2)}, u32[]{:S(2)}) collective-permute-start(bf16[288,512]{1,0:T(8,128)(2,1)S(1)} %join.2.refs_6_), channel_id=1, source_target_pairs={{0,16},{1,17},{2,18},{3,19},{4,20},{5,21},{6,22},{7,23},{8,24},{9,... | collective-permute-start | bytes 884744 | tf_op jit(solution)/shard_map/ppermute | solution.py:344
  24.8 4.7 %copy-start = (bf16[512,2048]{1,0:T(8,128)(2,1)S(1)}, bf16[512,2048]{1,0:T(8,128)(2,1)}, u32[]{:S(2)}) copy-start(bf16[512,2048]{1,0:T(8,128)(2,1)} %refs_5_.7) | copy-start | bytes 6291460
  27.4 13.0 %collective-permute-start.10 = (bf16[288,512]{1,0:T(8,128)(2,1)S(1)}, bf16[288,512]{1,0:T(8,128)(2,1)S(1)}, u32[]{:S(2)}, u32[]{:S(2)}) collective-permute-start(bf16[288,512]{1,0:T(8,128)(2,1)S(1)} %window.1.refs_0_), channel_id=1, source_target_pairs={{0,1},{1,0},{2,3},{3,2},{4,5},{5,4},{6,7},{7,6},{8,9},{9,8},{10,11... | collective-permute-start | bytes 884744 | tf_op jit(solution)/shard_map/ppermute | solution.py:344
  28.0 13.1 %collective-permute-start.8 = (bf16[288,512]{1,0:T(8,128)(2,1)S(1)}, bf16[288,512]{1,0:T(8,128)(2,1)S(1)}, u32[]{:S(2)}, u32[]{:S(2)}) collective-permute-start(bf16[288,512]{1,0:T(8,128)(2,1)S(1)} %window.1.refs_0_), channel_id=1, source_target_pairs={{0,16},{1,17},{2,18},{3,19},{4,20},{5,21},{6,22},{7,23},{8,24},{9,... | collective-permute-start | bytes 884744 | tf_op jit(solution)/shard_map/ppermute | solution.py:344
  31.9 13.5 %collective-permute-start.13 = (bf16[288,512]{1,0:T(8,128)(2,1)S(1)}, bf16[288,512]{1,0:T(8,128)(2,1)S(1)}, u32[]{:S(2)}, u32[]{:S(2)}) collective-permute-start(bf16[288,512]{1,0:T(8,128)(2,1)S(1)} %copy.19.refs_4_), channel_id=1, source_target_pairs={{0,6},{1,1},{2,0},{3,3},{4,2},{5,5},{6,4},{7,7},{8,14},{9,9},{10,8... | collective-permute-start | bytes 884744 | tf_op jit(solution)/shard_map/ppermute | solution.py:344
  40.5 8.5 %collective-permute-start.11 = (bf16[144,512]{1,0:T(8,128)(2,1)S(1)}, bf16[144,512]{1,0:T(8,128)(2,1)S(1)}, u32[]{:S(2)}, u32[]{:S(2)}) collective-permute-start(bf16[144,512]{1,0:T(8,128)(2,1)S(1)} %slice.9), channel_id=1, source_target_pairs={{0,16},{1,17},{2,18},{3,19},{4,20},{5,21},{6,22},{7,23},{8,24},{9,... | collective-permute-start | bytes 442376 | tf_op jit(solution)/shard_map/ppermute | solution.py:344
  41.1 7.9 %collective-permute-start.9 = (bf16[144,512]{1,0:T(8,128)(2,1)S(1)}, bf16[144,512]{1,0:T(8,128)(2,1)S(1)}, u32[]{:S(2)}, u32[]{:S(2)}) collective-permute-start(bf16[144,512]{1,0:T(8,128)(2,1)S(1)} %slice.8), channel_id=1, source_target_pairs={{0,1},{1,0},{2,3},{3,2},{4,5},{5,4},{6,7},{7,6},{8,9},{9,8},{10,11... | collective-permute-start | bytes 442376 | tf_op jit(solution)/shard_map/ppermute | solution.py:344
  43.4 9.5 %collective-permute-start.15 = (bf16[288,512]{1,0:T(8,128)(2,1)S(1)}, bf16[288,512]{1,0:T(8,128)(2,1)S(1)}, u32[]{:S(2)}, u32[]{:S(2)}) collective-permute-start(bf16[288,512]{1,0:T(8,128)(2,1)S(1)} %join.3), channel_id=1, source_target_pairs={{0,1},{1,2},{2,3},{3,4},{4,5},{5,6},{6,7},{7,0},{8,9},{9,10},{10,1... | collective-permute-start | bytes 884744 | tf_op jit(solution)/shard_map/ppermute | solution.py:344
  51.7 2.0 %collective-permute-start.14 = (bf16[256,1024]{1,0:T(8,128)(2,1)S(1)}, bf16[256,1024]{1,0:T(8,128)(2,1)S(1)}, u32[]{:S(2)}, u32[]{:S(2)}) collective-permute-start(bf16[256,1024]{1,0:T(8,128)(2,1)S(1)} %get-tuple-element.55.refs_3_), channel_id=1, source_target_pairs={{0,8},{1,9},{2,10},{3,11},{4,12},{5,13},{6,14},{7,15},{8,0},{9,1},... | collective-permute-start | bytes 1572872 | tf_op jit(solution)/shard_map/ppermute | solution.py:344
  53.9 4.6 %collective-permute-start.16 = (bf16[576,512]{1,0:T(8,128)(2,1)S(1)}, bf16[576,512]{1,0:T(8,128)(2,1)S(1)}, u32[]{:S(2)}, u32[]{:S(2)}) collective-permute-start(bf16[576,512]{1,0:T(8,128)(2,1)S(1)} %get-tuple-element.58.own), channel_id=1, source_target_pairs={{0,8},{1,9},{2,10},{3,11},{4,12},{5,13},{6,14},{7,15},{8,0},{9,1},... | collective-permute-start | bytes 1769480 | tf_op jit(solution)/shard_map/ppermute | solution.py:344
  54.1 8.2 %collective-permute-start.17 = (bf16[256,256]{1,0:T(8,128)(2,1)S(1)}, bf16[256,256]{1,0:T(8,128)(2,1)S(1)}, u32[]{:S(2)}, u32[]{:S(2)}) collective-permute-start(bf16[256,256]{1,0:T(8,128)(2,1)S(1)} %get-tuple-element.61), channel_id=1, source_target_pairs={{0,6},{1,7},{2,4},{3,5},{4,2},{5,3},{6,0},{7,1},{8,14},{9,15},{10,... | collective-permute-start | bytes 393224 | tf_op jit(solution)/shard_map/ppermute | solution.py:344
  57.7 9.6 %collective-permute-start.18 = (bf16[256,256]{1,0:T(8,128)(2,1)S(1)}, bf16[256,256]{1,0:T(8,128)(2,1)S(1)}, u32[]{:S(2)}, u32[]{:S(2)}) collective-permute-start(bf16[256,256]{1,0:T(8,128)(2,1)S(1)} %get-tuple-element.62), channel_id=1, source_target_pairs={{0,4},{1,5},{2,6},{3,7},{4,0},{5,1},{6,2},{7,3},{8,12},{9,13},{10,... | collective-permute-start | bytes 393224 | tf_op jit(solution)/shard_map/ppermute | solution.py:344
  57.7 9.6 %collective-permute-start.19 = (bf16[256,256]{1,0:T(8,128)(2,1)S(1)}, bf16[256,256]{1,0:T(8,128)(2,1)S(1)}, u32[]{:S(2)}, u32[]{:S(2)}) collective-permute-start(bf16[256,256]{1,0:T(8,128)(2,1)S(1)} %get-tuple-element.63), channel_id=1, source_target_pairs={{0,2},{1,3},{2,0},{3,1},{4,6},{5,7},{6,4},{7,5},{8,10},{9,11},{10,... | collective-permute-start | bytes 393224 | tf_op jit(solution)/shard_map/ppermute | solution.py:344
  (7 other events, 28.2 us)

commit v5 on v4

--- a/solution.py
+++ b/solution.py
@@ -431,7 +431,7 @@
     )[0]
     beside = exchanged(resid, 2, same)
     across = exchanged(resid, 0, peer)
-    far = [exchanged(beside[:rows], 0, peer), exchanged(across[rows:], 2, same)]
+    far = exchanged(across, 2, same)
 
     gain_mlp = gain_mlp[None]
     up_part, down_part = w_up, w_down
@@ -458,8 +458,8 @@
     weights = (gain_mlp, up_part, down_part)
     own_at, middle_at, far_at = (
         ((0, 0), (1, 0)),
-        ((0, 1), (1, 0), (2, 0), (3, 0)),
-        ((0, 1), (1, 1)),
+        ((0, 1), (1, 0), (2, 0)),
+        ((0, 0), (1, 1), (0, 1)),
     )
     so_far = call(
         functools.partial(grad_body, 1, own_at, False, False, part),
@@ -474,7 +474,7 @@
         copy_body, (cot_west,), [((window, width), BF16)], vmem=8, after=so_far[0]
     )[0]
     cot_peer_w = exchanged(cot_west, 0, next_pair)
-    own_out, own_w = mlp(resid, cot_west, 2.0)
+    own_out, own_w = mlp(resid, cot_west, 0.05)
     beside_out, beside_w = mlp(beside, (own_w, across), 3.0)
     out_w = exchanged(
         call(join_body, (own_w, beside_w), [((window, width), BF16)], vmem=8)[0], 0, east
@@ -482,22 +482,22 @@
     so_far = call(
         functools.partial(grad_body, 2, middle_at, True, False, part),
         (
-            *(beside, across),
-            *(cot_east, cot_beside, cot_peer_e, cot_peer_w),
+            *(beside, across[:rows]),
+            *(cot_east, cot_beside, cot_peer_e),
             *weights,
             *so_far,
         ),
         sums,
-        scratch(4),
+        scratch(3),
         vmem=24,
         after=beside_out,
         us=ACROSS_US,
     )
     send, keep = call(
         functools.partial(grad_body, 2, far_at, True, True, part),
-        (*far, cot_beside, cot_peer_w, *weights, *so_far),
+        (across[rows:], far, cot_peer_w, cot_beside, *weights, *so_far),
         [((2 * quarter, hidden // 2), BF16), ((2 * quarter, hidden // 2), F32)],
-        [pltpu.VMEM((2 * quarter, hidden // 2), F32)] * 2 + scratch(2),
+        [pltpu.VMEM((2 * quarter, hidden // 2), F32)] * 2 + scratch(3),
         vmem=24,
         us=2.6,
     )

time: 68.3 us -> 67.1 us (0.982)
  starting transfers between devices: 32 us -> 29.8 us
  waiting for transfers between devices: 9.41 us -> 10.7 us
    ppermute x20 -> x19, starting transfers between devices: 32 us -> 29.8 us  [exchanged(): return lax.ppermute(block, ('lev', 'tile'), route)]
    ppermute x20 -> x19, waiting for transfers between devices: 9.41 us -> 10.7 us  [exchanged(): return lax.ppermute(block, ('lev', 'tile'), route)]
  transfers between devices with their start and end apart: 20 -> 19, of which waited for: 5 -> 5; matrix products, arithmetic and copies ran while one was open for 0% -> 0% of each run, Pallas kernels for 32% -> 32%
where the time goes in v5:
time: 67.1 us; the launch traced here: 66.9 us
  starting transfers between devices  29.8 us (44%)
  Pallas kernels  23.2 us (35%)
  waiting for transfers between devices  10.7 us (16%)
  other arithmetic  2.11 us (3%)
  between operations  0.96 us (1%)
    ppermute x19, starting transfers between devices, exchanged(): return lax.ppermute(block, ('lev', 'tile'), route)  29.8 us
    pallas_call x18, Pallas kernels, call(): pl.pallas_call(body, out_shape=[jax.ShapeDtypeStruct(shape, dtype) for sh...  23.2 us
    ppermute x19, waiting for transfers between devices, exchanged(): return lax.ppermute(block, ('lev', 'tile'), route)  10.7 us
    transpose x1, other arithmetic, per_device(): marked = marked.transpose(0, 2, 1, 3)  1.45 us
  transfers between devices with their start and end apart: 19, of which 5 were waited for; matrix products, arithmetic and copies ran while one was open for 0% of the time, Pallas kernels for 32%

profile of v5, /device:TPU:0, one launch (start us, length us, event | category | flops | bytes accessed | tf_op | source)
XLA Modules:
  0.0 66.9 jit_solution(4382898626977815067)
XLA Ops:
  1.3 1.4 %select_bitcast_fusion.lev_ref = bf16[4,12,24,512]{3,2,1,0:T(8,128)(2,1)S(1)} fusion(bf16[4,24,12,512]{3,1,2,0:T(8,128)(2,1)} %param.13, pred[4]{0:T(512)(128)(4,1)S(1)} %broadcast_compare_fusion), kind=kLoop, calls=%fused_computation | loop fusion | flops 589824 | bytes 2359300 | tf_op jit(solution)/shard_map/transpose | solution.py:380
  3.8 2.6 %collective-permute-start.1 = (bf16[144,512]{1,0:T(8,128)(2,1)S(1)}, bf16[144,512]{1,0:T(8,128)(2,1)S(1)}, u32[]{:S(2)}, u32[]{:S(2)}) collective-permute-start(bf16[144,512]{1,0:T(8,128)(2,1)S(1)} %get-tuple-element.39), channel_id=1, source_target_pairs={{0,24},{1,25},{2,26},{3,27},{4,28},{5,29},{6,30},{7,31},{8,16},{9,... | collective-permute-start | bytes 442376 | tf_op jit(solution)/shard_map/ppermute | solution.py:344
  7.1 5.0 %collective-permute-start.6 = (bf16[144,512]{1,0:T(8,128)(2,1)S(1)}, bf16[144,512]{1,0:T(8,128)(2,1)S(1)}, u32[]{:S(2)}, u32[]{:S(2)}) collective-permute-start(bf16[144,512]{1,0:T(8,128)(2,1)S(1)} %get-tuple-element.44), channel_id=1, source_target_pairs={{0,7},{1,0},{2,1},{3,2},{4,3},{5,4},{6,5},{7,6},{8,15},{9,8},{10,9... | collective-permute-start | bytes 442376 | tf_op jit(solution)/shard_map/ppermute | solution.py:344
  12.1 1.6 %collective-permute-start.2 = (bf16[144,512]{1,0:T(8,128)(2,1)S(1)}, bf16[144,512]{1,0:T(8,128)(2,1)S(1)}, u32[]{:S(2)}, u32[]{:S(2)}) collective-permute-start(bf16[144,512]{1,0:T(8,128)(2,1)S(1)} %get-tuple-element.40), channel_id=1, source_target_pairs={{0,16},{1,17},{2,18},{3,19},{4,20},{5,21},{6,22},{7,23},{8,24},{9,... | collective-permute-start | bytes 442376 | tf_op jit(solution)/shard_map/ppermute | solution.py:344
  14.0 2.1 %aggregate.2.refs_7_.refs_2_ = bf16[144,512]{1,0:T(8,128)(2,1)S(1)} custom-call(bf16[144,512]{1,0:T(8,128)(2,1)S(1)} %get-tuple-element.42.own, bf16[144,512]{1,0:T(8,128)(2,1)S(1)} %collective-permute-done.4.beside, bf16[144,512]{1,0:T(8,128)(2,1)S(1)} %collective-permute-done.1.refs_3_.far, bf16[288,512]{1,0:T(8,128)(2,1)S(1)} %collective-permute-done.refs_2_.core.refs_3_, ...), custom_call_target="tpu_custom_call" | custom-call | flops 6300000256 | tf_op jit(solution)/shard_map/aggregate/pallas_call | solution.py:45
  16.2 4.8 %collective-permute-start.5 = (bf16[144,512]{1,0:T(8,128)(2,1)S(1)}, bf16[144,512]{1,0:T(8,128)(2,1)S(1)}, u32[]{:S(2)}, u32[]{:S(2)}) collective-permute-start(bf16[144,512]{1,0:T(8,128)(2,1)S(1)} %aggregate.2.refs_7_.refs_2_), channel_id=1, source_target_pairs={{0,7},{1,0},{2,1},{3,2},{4,3},{5,4},{6,5},{7,6},{8,15},{9,8},{10,9... | collective-permute-start | bytes 442376 | tf_op jit(solution)/shard_map/ppermute | solution.py:344
  21.0 1.6 %collective-permute-start.10 = (bf16[288,512]{1,0:T(8,128)(2,1)S(1)}, bf16[288,512]{1,0:T(8,128)(2,1)S(1)}, u32[]{:S(2)}, u32[]{:S(2)}) collective-permute-start(bf16[288,512]{1,0:T(8,128)(2,1)S(1)} %join.2.refs_6_), channel_id=1, source_target_pairs={{0,16},{1,17},{2,18},{3,19},{4,20},{5,21},{6,22},{7,23},{8,24},{9,... | collective-permute-start | bytes 884744 | tf_op jit(solution)/shard_map/ppermute | solution.py:344
  22.6 2.1 %aggregate.3.refs_0_ = bf16[144,512]{1,0:T(8,128)(2,1)S(1)} custom-call(bf16[144,512]{1,0:T(8,128)(2,1)S(1)} %get-tuple-element.35.refs_0_.refs_1_, bf16[144,512]{1,0:T(8,128)(2,1)S(1)} %collective-permute-done.2.refs_1_, bf16[144,512]{1,0:T(8,128)(2,1)S(1)} %collective-permute-done.3.refs_2_, ...), custom_call_target="tpu_custom_call" | custom-call | flops 6300000256 | tf_op jit(solution)/shard_map/aggregate/pallas_call | solution.py:45
  24.8 2.6 %window.1.refs_0_ = bf16[288,512]{1,0:T(8,128)(2,1)S(1)} custom-call(bf16[144,512]{1,0:T(8,128)(2,1)S(1)} %aggregate.3.refs_0_, bf16[144,512]{1,0:T(8,128)(2,1)S(1)} %collective-permute-done.5.refs_1_, bf16[512,512]{1,0:T(8,128)(2,1)S(1)} %copy-done.7, f32[1,512]{1,0:T(1,128)S(1)} %bitcast.12, bf16[512,1536]{1,0:T(8,128)(2,1)S(1)} %copy-done.3, ...), custom_call_target="tpu_custom_call" | custom-call | flops 8999999488 | tf_op jit(solution)/shard_map/window/pallas_call | solution.py:45
  28.0 1.5 %collective-permute-start.8 = (bf16[288,512]{1,0:T(8,128)(2,1)S(1)}, bf16[288,512]{1,0:T(8,128)(2,1)S(1)}, u32[]{:S(2)}, u32[]{:S(2)}) collective-permute-start(bf16[288,512]{1,0:T(8,128)(2,1)S(1)} %window.1.refs_0_), channel_id=1, source_target_pairs={{0,1},{1,0},{2,3},{3,2},{4,5},{5,4},{6,7},{7,6},{8,9},{9,8},{10,11... | collective-permute-start | bytes 884744 | tf_op jit(solution)/shard_map/ppermute | solution.py:344
  29.5 2.4 %grad.3 = (f32[256,1024]{1,0:T(8,128)S(1)}, f32[256,1024]{1,0:T(8,128)S(1)}) custom-call(bf16[288,512]{1,0:T(8,128)(2,1)S(1)} %window.1.refs_0_, bf16[288,512]{1,0:T(8,128)(2,1)S(1)} %get-tuple-element.47.refs_1_.refs_2_, bf16[144,512]{1,0:T(8,128)(2,1)S(1)} %collective-permute-done.6.refs_0_.refs_2_, f32[1,512]{1,0:T(1,128)S(1)} %bitcast.6, ...), custom_call_target="tpu_custom_call" | custom-call | flops 6600000000 | tf_op jit(solution)/shard_map/grad/pallas_call | solution.py:45
  31.9 6.4 %collective-permute-start.11 = (bf16[288,512]{1,0:T(8,128)(2,1)S(1)}, bf16[288,512]{1,0:T(8,128)(2,1)S(1)}, u32[]{:S(2)}, u32[]{:S(2)}) collective-permute-start(bf16[288,512]{1,0:T(8,128)(2,1)S(1)} %copy.19.refs_4_), channel_id=1, source_target_pairs={{0,6},{1,1},{2,0},{3,3},{4,2},{5,5},{6,4},{7,7},{8,14},{9,9},{10,8... | collective-permute-start | bytes 884744 | tf_op jit(solution)/shard_map/ppermute | solution.py:344
  38.3 2.2 %mlp.2 = (bf16[144,512]{1,0:T(8,128)(2,1)S(1)}, bf16[144,512]{1,0:T(8,128)(2,1)S(1)}) custom-call(bf16[288,512]{1,0:T(8,128)(2,1)S(1)} %window.1.refs_0_, f32[1,512]{1,0:T(1,128)S(1)} %bitcast.7, bf16[512,2048]{1,0:T(8,128)(2,1)S(1)} %copy-done, bf16[2048,512]{1,0:T(8,128)(2,1)S(1)} %copy-done.1, bf16[288,512]{1,0:T(8,128)(2,1)S(1)} %copy.19.refs_4_), custom_call_target="tpu_custom_call" | custom-call | flops 150000000 | tf_op jit(solution)/shard_map/mlp/pallas_call | solution.py:45
  41.1 2.2 %mlp.3 = (bf16[144,512]{1,0:T(8,128)(2,1)S(1)}, bf16[144,512]{1,0:T(8,128)(2,1)S(1)}) custom-call(bf16[288,512]{1,0:T(8,128)(2,1)S(1)} %collective-permute-done.12.refs_0_, f32[1,512]{1,0:T(1,128)S(1)} %bitcast.8, bf16[512,2048]{1,0:T(8,128)(2,1)S(1)} %copy-done, bf16[2048,512]{1,0:T(8,128)(2,1)S(1)} %copy-done.1, ...), custom_call_target="tpu_custom_call" | custom-call | flops 8999999488 | tf_op jit(solution)/shard_map/mlp/pallas_call | solution.py:45
  43.3 2.8 %grad.4 = (f32[256,1024]{1,0:T(8,128)S(1)}, f32[256,1024]{1,0:T(8,128)S(1)}) custom-call(bf16[288,512]{1,0:T(8,128)(2,1)S(1)} %collective-permute-done.12.refs_0_, bf16[144,512]{1,0:T(8,128)(2,1)S(1)} %get-tuple-element.67.refs_1_, bf16[288,512]{1,0:T(8,128)(2,1)S(1)} %get-tuple-element.47.refs_1_.refs_2_, ...), custom_call_target="tpu_custom_call" | custom-call | flops 150000000 | tf_op jit(solution)/shard_map/grad/pallas_call | solution.py:45
  46.2 1.1 %collective-permute-done.9.refs_1_ = bf16[288,512]{1,0:T(8,128)(2,1)S(1)} collective-permute-done((bf16[288,512]{1,0:T(8,128)(2,1)S(1)}, bf16[288,512]{1,0:T(8,128)(2,1)S(1)}, u32[]{:S(2)}, u32[]{:S(2)}) %collective-permute-start.9) | collective-permute-done | bytes 294944 | tf_op jit(solution)/shard_map/ppermute | solution.py:344
  47.3 3.1 %grad.5 = (bf16[256,1024]{1,0:T(8,128)(2,1)S(1)}, f32[256,1024]{1,0:T(8,128)S(1)}) custom-call(bf16[144,512]{1,0:T(8,128)(2,1)S(1)} %get-tuple-element.68.refs_0_, bf16[288,512]{1,0:T(8,128)(2,1)S(1)} %collective-permute-done.9.refs_1_, bf16[288,512]{1,0:T(8,128)(2,1)S(1)} %collective-permute-done.11.refs_2_, ...), custom_call_target="tpu_custom_call" | custom-call | flops 7800000000 | tf_op jit(solution)/shard_map/grad/pallas_call | solution.py:45
  50.5 2.3 %collective-permute-done.14.refs_2_ = bf16[288,512]{1,0:T(8,128)(2,1)S(1)} collective-permute-done((bf16[288,512]{1,0:T(8,128)(2,1)S(1)}, bf16[288,512]{1,0:T(8,128)(2,1)S(1)}, u32[]{:S(2)}, u32[]{:S(2)}) %collective-permute-start.14) | collective-permute-done | bytes 294944 | tf_op jit(solution)/shard_map/ppermute | solution.py:344
  53.2 0.8 %collective-permute-start.17 = (bf16[256,256]{1,0:T(8,128)(2,1)S(1)}, bf16[256,256]{1,0:T(8,128)(2,1)S(1)}, u32[]{:S(2)}, u32[]{:S(2)}) collective-permute-start(bf16[256,256]{1,0:T(8,128)(2,1)S(1)} %get-tuple-element.62), channel_id=1, source_target_pairs={{0,4},{1,5},{2,6},{3,7},{4,0},{5,1},{6,2},{7,3},{8,12},{9,13},{10,... | collective-permute-start | bytes 393224 | tf_op jit(solution)/shard_map/ppermute | solution.py:344
  54.0 3.6 %collective-permute-start.18 = (bf16[256,256]{1,0:T(8,128)(2,1)S(1)}, bf16[256,256]{1,0:T(8,128)(2,1)S(1)}, u32[]{:S(2)}, u32[]{:S(2)}) collective-permute-start(bf16[256,256]{1,0:T(8,128)(2,1)S(1)} %get-tuple-element.63), channel_id=1, source_target_pairs={{0,2},{1,3},{2,0},{3,1},{4,6},{5,7},{6,4},{7,5},{8,10},{9,11},{10,... | collective-permute-start | bytes 393224 | tf_op jit(solution)/shard_map/ppermute | solution.py:344
  57.6 1.6 %unpack.1 = (bf16[4,12,24,512]{3,2,1,0:T(8,128)(2,1)}, f32[8,128]{1,0:T(8,128)S(1)}) custom-call(bf16[576,512]{1,0:T(8,128)(2,1)S(1)} %get-tuple-element.58.own, bf16[576,512]{1,0:T(8,128)(2,1)S(1)} %collective-permute-done.15.core), custom_call_target="tpu_custom_call" | custom-call | flops 4800000000 | tf_op jit(solution)/shard_map/unpack/pallas_call | solution.py:45
  59.2 2.3 %collective-permute-done.16.refs_1_ = bf16[256,256]{1,0:T(8,128)(2,1)S(1)} collective-permute-done((bf16[256,256]{1,0:T(8,128)(2,1)S(1)}, bf16[256,256]{1,0:T(8,128)(2,1)S(1)}, u32[]{:S(2)}, u32[]{:S(2)}) %collective-permute-start.16) | collective-permute-done | bytes 131104 | tf_op jit(solution)/shard_map/ppermute | solution.py:344
  61.4 4.7 %collective-permute-done.17.refs_2_ = bf16[256,256]{1,0:T(8,128)(2,1)S(1)} collective-permute-done((bf16[256,256]{1,0:T(8,128)(2,1)S(1)}, bf16[256,256]{1,0:T(8,128)(2,1)S(1)}, u32[]{:S(2)}, u32[]{:S(2)}) %collective-permute-start.17) | collective-permute-done | bytes 131104 | tf_op jit(solution)/shard_map/ppermute | solution.py:344
  66.2 0.7 %total.1 = (f32[128,256]{1,0:T(8,128)}, f32[128,256]{1,0:T(8,128)}) custom-call(f32[256,256]{1,0:T(8,128)S(1)} %get-tuple-element.60.refs_0_, bf16[256,256]{1,0:T(8,128)(2,1)S(1)} %collective-permute-done.16.refs_1_, bf16[256,256]{1,0:T(8,128)(2,1)S(1)} %collective-permute-done.17.refs_2_, bf16[256,256]{1,0:T(8,128)(2,1)S(1)} %collective-permute-done.18.refs_3_, ...), custom_call_target="tpu_custom_call" | custom-call | flops 2100000000 | tf_op jit(solution)/shard_map/total/pallas_call | solution.py:45
  (57 shorter events, 4.5 us)
Async XLA Ops:
  3.3 8.8 %collective-permute-start = (bf16[288,512]{1,0:T(8,128)(2,1)S(1)}, bf16[288,512]{1,0:T(8,128)(2,1)S(1)}, u32[]{:S(2)}, u32[]{:S(2)}) collective-permute-start(bf16[288,512]{1,0:T(8,128)(2,1)S(1)} %get-tuple-element.38), channel_id=1, source_target_pairs={{0,8},{1,9},{2,10},{3,11},{4,12},{5,13},{6,14},{7,15},{8,0},{9,1},... | collective-permute-start | bytes 884744 | tf_op jit(solution)/shard_map/ppermute | solution.py:344
  3.8 8.3 %collective-permute-start.1 = (bf16[144,512]{1,0:T(8,128)(2,1)S(1)}, bf16[144,512]{1,0:T(8,128)(2,1)S(1)}, u32[]{:S(2)}, u32[]{:S(2)}) collective-permute-start(bf16[144,512]{1,0:T(8,128)(2,1)S(1)} %get-tuple-element.39), channel_id=1, source_target_pairs={{0,24},{1,25},{2,26},{3,27},{4,28},{5,29},{6,30},{7,31},{8,16},{9,... | collective-permute-start | bytes 442376 | tf_op jit(solution)/shard_map/ppermute | solution.py:344
  6.5 7.6 %collective-permute-start.4 = (bf16[144,512]{1,0:T(8,128)(2,1)S(1)}, bf16[144,512]{1,0:T(8,128)(2,1)S(1)}, u32[]{:S(2)}, u32[]{:S(2)}) collective-permute-start(bf16[144,512]{1,0:T(8,128)(2,1)S(1)} %get-tuple-element.43), channel_id=1, source_target_pairs={{0,16},{1,17},{2,18},{3,19},{4,20},{5,21},{6,22},{7,23},{8,24},{9,... | collective-permute-start | bytes 442376 | tf_op jit(solution)/shard_map/ppermute | solution.py:344
  7.0 7.0 %copy-start.5 = (bf16[512,512]{1,0:T(8,128)(2,1)S(1)}, bf16[512,512]{1,0:T(8,128)(2,1)}, u32[]{:S(2)}) copy-start(bf16[512,512]{1,0:T(8,128)(2,1)} %refs_5_.4) | copy-start | bytes 1572868
  7.0 7.0 %copy-start.6 = (bf16[512,512]{1,0:T(8,128)(2,1)S(1)}, bf16[512,512]{1,0:T(8,128)(2,1)}, u32[]{:S(2)}) copy-start(bf16[512,512]{1,0:T(8,128)(2,1)} %refs_6_.3) | copy-start | bytes 1572868
  7.0 7.0 %copy-start.9 = (bf16[4,512]{1,0:T(4,128)(2,1)S(1)}, bf16[4,512]{1,0:T(4,128)(2,1)}, u32[]{:S(2)}) copy-start(bf16[4,512]{1,0:T(4,128)(2,1)} %refs_4_.3) | copy-start | bytes 12292
  7.1 13.9 %collective-permute-start.6 = (bf16[144,512]{1,0:T(8,128)(2,1)S(1)}, bf16[144,512]{1,0:T(8,128)(2,1)S(1)}, u32[]{:S(2)}, u32[]{:S(2)}) collective-permute-start(bf16[144,512]{1,0:T(8,128)(2,1)S(1)} %get-tuple-element.44), channel_id=1, source_target_pairs={{0,7},{1,0},{2,1},{3,2},{4,3},{5,4},{6,5},{7,6},{8,15},{9,8},{10,9... | collective-permute-start | bytes 442376 | tf_op jit(solution)/shard_map/ppermute | solution.py:344
  12.1 8.8 %collective-permute-start.7 = (bf16[144,512]{1,0:T(8,128)(2,1)S(1)}, bf16[144,512]{1,0:T(8,128)(2,1)S(1)}, u32[]{:S(2)}, u32[]{:S(2)}) collective-permute-start(bf16[144,512]{1,0:T(8,128)(2,1)S(1)} %get-tuple-element.45), channel_id=1, source_target_pairs={{0,1},{1,0},{2,3},{3,2},{4,5},{5,4},{6,7},{7,6},{8,9},{9,8},{10,11... | collective-permute-start | bytes 442376 | tf_op jit(solution)/shard_map/ppermute | solution.py:344
  12.1 10.5 %collective-permute-start.2 = (bf16[144,512]{1,0:T(8,128)(2,1)S(1)}, bf16[144,512]{1,0:T(8,128)(2,1)S(1)}, u32[]{:S(2)}, u32[]{:S(2)}) collective-permute-start(bf16[144,512]{1,0:T(8,128)(2,1)S(1)} %get-tuple-element.40), channel_id=1, source_target_pairs={{0,16},{1,17},{2,18},{3,19},{4,20},{5,21},{6,22},{7,23},{8,24},{9,... | collective-permute-start | bytes 442376 | tf_op jit(solution)/shard_map/ppermute | solution.py:344
  13.7 8.9 %collective-permute-start.3 = (bf16[144,512]{1,0:T(8,128)(2,1)S(1)}, bf16[144,512]{1,0:T(8,128)(2,1)S(1)}, u32[]{:S(2)}, u32[]{:S(2)}) collective-permute-start(bf16[144,512]{1,0:T(8,128)(2,1)S(1)} %get-tuple-element.41), channel_id=1, source_target_pairs={{0,24},{1,25},{2,26},{3,27},{4,28},{5,29},{6,30},{7,31},{8,16},{9,... | collective-permute-start | bytes 442376 | tf_op jit(solution)/shard_map/ppermute | solution.py:344
  16.2 8.6 %collective-permute-start.5 = (bf16[144,512]{1,0:T(8,128)(2,1)S(1)}, bf16[144,512]{1,0:T(8,128)(2,1)S(1)}, u32[]{:S(2)}, u32[]{:S(2)}) collective-permute-start(bf16[144,512]{1,0:T(8,128)(2,1)S(1)} %aggregate.2.refs_7_.refs_2_), channel_id=1, source_target_pairs={{0,7},{1,0},{2,1},{3,2},{4,3},{5,4},{6,5},{7,6},{8,15},{9,8},{10,9... | collective-permute-start | bytes 442376 | tf_op jit(solution)/shard_map/ppermute | solution.py:344
  21.0 8.5 %collective-permute-start.10 = (bf16[288,512]{1,0:T(8,128)(2,1)S(1)}, bf16[288,512]{1,0:T(8,128)(2,1)S(1)}, u32[]{:S(2)}, u32[]{:S(2)}) collective-permute-start(bf16[288,512]{1,0:T(8,128)(2,1)S(1)} %join.2.refs_6_), channel_id=1, source_target_pairs={{0,16},{1,17},{2,18},{3,19},{4,20},{5,21},{6,22},{7,23},{8,24},{9,... | collective-permute-start | bytes 884744 | tf_op jit(solution)/shard_map/ppermute | solution.py:344
  24.8 4.7 %copy-start = (bf16[512,2048]{1,0:T(8,128)(2,1)S(1)}, bf16[512,2048]{1,0:T(8,128)(2,1)}, u32[]{:S(2)}) copy-start(bf16[512,2048]{1,0:T(8,128)(2,1)} %refs_5_.7) | copy-start | bytes 6291460
  24.8 4.7 %copy-start.1 = (bf16[2048,512]{1,0:T(8,128)(2,1)S(1)}, bf16[2048,512]{1,0:T(8,128)(2,1)}, u32[]{:S(2)}) copy-start(bf16[2048,512]{1,0:T(8,128)(2,1)} %refs_6_.5) | copy-start | bytes 6291460
  27.4 13.6 %collective-permute-start.12 = (bf16[288,512]{1,0:T(8,128)(2,1)S(1)}, bf16[288,512]{1,0:T(8,128)(2,1)S(1)}, u32[]{:S(2)}, u32[]{:S(2)}) collective-permute-start(bf16[288,512]{1,0:T(8,128)(2,1)S(1)} %window.1.refs_0_), channel_id=1, source_target_pairs={{0,16},{1,17},{2,18},{3,19},{4,20},{5,21},{6,22},{7,23},{8,24},{9,... | collective-permute-start | bytes 884744 | tf_op jit(solution)/shard_map/ppermute | solution.py:344
  28.0 12.5 %collective-permute-start.8 = (bf16[288,512]{1,0:T(8,128)(2,1)S(1)}, bf16[288,512]{1,0:T(8,128)(2,1)S(1)}, u32[]{:S(2)}, u32[]{:S(2)}) collective-permute-start(bf16[288,512]{1,0:T(8,128)(2,1)S(1)} %window.1.refs_0_), channel_id=1, source_target_pairs={{0,1},{1,0},{2,3},{3,2},{4,5},{5,4},{6,7},{7,6},{8,9},{9,8},{10,11... | collective-permute-start | bytes 884744 | tf_op jit(solution)/shard_map/ppermute | solution.py:344
  31.9 14.3 %collective-permute-start.11 = (bf16[288,512]{1,0:T(8,128)(2,1)S(1)}, bf16[288,512]{1,0:T(8,128)(2,1)S(1)}, u32[]{:S(2)}, u32[]{:S(2)}) collective-permute-start(bf16[288,512]{1,0:T(8,128)(2,1)S(1)} %copy.19.refs_4_), channel_id=1, source_target_pairs={{0,6},{1,1},{2,0},{3,3},{4,2},{5,5},{6,4},{7,7},{8,14},{9,9},{10,8... | collective-permute-start | bytes 884744 | tf_op jit(solution)/shard_map/ppermute | solution.py:344
  40.5 6.8 %collective-permute-start.9 = (bf16[288,512]{1,0:T(8,128)(2,1)S(1)}, bf16[288,512]{1,0:T(8,128)(2,1)S(1)}, u32[]{:S(2)}, u32[]{:S(2)}) collective-permute-start(bf16[288,512]{1,0:T(8,128)(2,1)S(1)} %collective-permute-done.8.refs_5_), channel_id=1, source_target_pairs={{0,16},{1,17},{2,18},{3,19},{4,20},{5,21},{6,22},{7,23},{8,24},{9,... | collective-permute-start | bytes 884744 | tf_op jit(solution)/shard_map/ppermute | solution.py:344
  43.3 9.5 %collective-permute-start.14 = (bf16[288,512]{1,0:T(8,128)(2,1)S(1)}, bf16[288,512]{1,0:T(8,128)(2,1)S(1)}, u32[]{:S(2)}, u32[]{:S(2)}) collective-permute-start(bf16[288,512]{1,0:T(8,128)(2,1)S(1)} %join.3), channel_id=1, source_target_pairs={{0,1},{1,2},{2,3},{3,4},{4,5},{5,6},{6,7},{7,0},{8,9},{9,10},{10,1... | collective-permute-start | bytes 884744 | tf_op jit(solution)/shard_map/ppermute | solution.py:344
  50.4 2.4 %collective-permute-start.13 = (bf16[256,1024]{1,0:T(8,128)(2,1)S(1)}, bf16[256,1024]{1,0:T(8,128)(2,1)S(1)}, u32[]{:S(2)}, u32[]{:S(2)}) collective-permute-start(bf16[256,1024]{1,0:T(8,128)(2,1)S(1)} %get-tuple-element.55.refs_3_), channel_id=1, source_target_pairs={{0,8},{1,9},{2,10},{3,11},{4,12},{5,13},{6,14},{7,15},{8,0},{9,1},... | collective-permute-start | bytes 1572872 | tf_op jit(solution)/shard_map/ppermute | solution.py:344
  53.0 4.5 %collective-permute-start.15 = (bf16[576,512]{1,0:T(8,128)(2,1)S(1)}, bf16[576,512]{1,0:T(8,128)(2,1)S(1)}, u32[]{:S(2)}, u32[]{:S(2)}) collective-permute-start(bf16[576,512]{1,0:T(8,128)(2,1)S(1)} %get-tuple-element.58.own), channel_id=1, source_target_pairs={{0,8},{1,9},{2,10},{3,11},{4,12},{5,13},{6,14},{7,15},{8,0},{9,1},... | collective-permute-start | bytes 1769480 | tf_op jit(solution)/shard_map/ppermute | solution.py:344
  53.1 8.3 %collective-permute-start.16 = (bf16[256,256]{1,0:T(8,128)(2,1)S(1)}, bf16[256,256]{1,0:T(8,128)(2,1)S(1)}, u32[]{:S(2)}, u32[]{:S(2)}) collective-permute-start(bf16[256,256]{1,0:T(8,128)(2,1)S(1)} %get-tuple-element.61), channel_id=1, source_target_pairs={{0,6},{1,7},{2,4},{3,5},{4,2},{5,3},{6,0},{7,1},{8,14},{9,15},{10,... | collective-permute-start | bytes 393224 | tf_op jit(solution)/shard_map/ppermute | solution.py:344
  53.2 13.0 %collective-permute-start.17 = (bf16[256,256]{1,0:T(8,128)(2,1)S(1)}, bf16[256,256]{1,0:T(8,128)(2,1)S(1)}, u32[]{:S(2)}, u32[]{:S(2)}) collective-permute-start(bf16[256,256]{1,0:T(8,128)(2,1)S(1)} %get-tuple-element.62), channel_id=1, source_target_pairs={{0,4},{1,5},{2,6},{3,7},{4,0},{5,1},{6,2},{7,3},{8,12},{9,13},{10,... | collective-permute-start | bytes 393224 | tf_op jit(solution)/shard_map/ppermute | solution.py:344
  54.0 12.2 %collective-permute-start.18 = (bf16[256,256]{1,0:T(8,128)(2,1)S(1)}, bf16[256,256]{1,0:T(8,128)(2,1)S(1)}, u32[]{:S(2)}, u32[]{:S(2)}) collective-permute-start(bf16[256,256]{1,0:T(8,128)(2,1)S(1)} %get-tuple-element.63), channel_id=1, source_target_pairs={{0,2},{1,3},{2,0},{3,1},{4,6},{5,7},{6,4},{7,5},{8,10},{9,11},{10,... | collective-permute-start | bytes 393224 | tf_op jit(solution)/shard_map/ppermute | solution.py:344
  (6 other events, 23.5 us)
